TPU v7x, 128 devices: a whole 4x4x4 slice. The times are simulated.
128 devices in a mesh: ctx: 128 (over z, y, x, core).
Axes of the slice: x: 4, y: 4, z: 4, core: 2. Of those that a mesh axis runs over, the one named last changes fastest.
Arguments:
- queries: bfloat16 [32768, 4096], P('ctx'), may hold values from -8 to 8
- keys: bfloat16 [32768, 1024], P('ctx'), may hold values from -8 to 8
- values: bfloat16 [32768, 1024], P('ctx'), may hold values from -6 to 6
- cotangent: bfloat16 [32768, 4096], P('ctx'), may hold values from -6 to 6
- selected: int32 [128, 16], P('ctx'), may hold values from -1 to 62, as said below
Outputs:
- attended: bfloat16 [32768, 4096], P('ctx')
- grad_queries: bfloat16 [32768, 4096], P('ctx')
- grad_keys: bfloat16 [32768, 1024], P('ctx')
- grad_values: bfloat16 [32768, 1024], P('ctx')
Inputs may be any that keep to these rules, and one draw needn't show every extreme that they name: `selected`: rows d and e are equal when d // 2 == e // 2. A row of query block b = d // 2 holds min(b, 16) live entries, each naming an earlier key block, and -1 elsewhere; its live entries name different blocks; every block b >= 1 names block b - 1, and the last block names block 0.
All inputs are finite; a program needn't handle non-finite values.
Results may differ from a plain program's by a relative error of at most 0.014.
Values may be sent and summed in bfloat16 or wider, within the bound.
No kernel may reach another device: no remote copies, remote signals or barrier semaphores. Data moves between devices by JAX's collectives and lax.ppermute only.
A program may use at most 192 MiB of HBM per device.

v0:
```python
import jax
import jax.numpy as jnp
from jax import lax
from jax.sharding import PartitionSpec as P

HD = 128
QH = 32
KVH = 8
BLOCK = 512


def shifted(block, axis, distance):
    devices = range(lax.axis_size(axis))
    route = [(i - distance, i) for i in devices if i - distance in devices]
    return lax.ppermute(block, axis, route)


def scores_for(query_head, key_rows, valid):
    score = jnp.einsum(
        "rgd,ld->grl", query_head, key_rows, preferred_element_type=jnp.float32
    ) * HD ** (-0.5)
    return jnp.where(valid[None], score, -1e30)


def forward_head(items):
    query_head, key_rows, value_rows, valid = items
    score = scores_for(query_head, key_rows, valid)
    top = jnp.max(score, axis=2, keepdims=True)
    raised = jnp.exp(score - top)
    total = jnp.sum(raised, axis=2, keepdims=True)
    weight = (raised / total).astype(jnp.bfloat16)
    attended = jnp.einsum(
        "grl,lc->rgc", weight, value_rows, preferred_element_type=jnp.float32
    ).astype(jnp.bfloat16)
    return (attended, top, total)


def backward_head(items):
    query_head, key_rows, value_rows, valid, cot_head, top, total = items
    scale = HD ** (-0.5)
    score = scores_for(query_head, key_rows, valid)
    weight = jnp.exp(score - top) / total
    weight_b = weight.astype(jnp.bfloat16)
    dweight = jnp.einsum("rgc,lc->grl", cot_head, value_rows, preferred_element_type=jnp.float32)
    delta = jnp.sum(weight * dweight, axis=2, keepdims=True)
    dscore = (weight * (dweight - delta)).astype(jnp.bfloat16)
    grad_query = (
        jnp.einsum("grl,ld->rgd", dscore, key_rows, preferred_element_type=jnp.float32) * scale
    ).astype(jnp.bfloat16)
    grad_key = (
        jnp.einsum("grl,rgd->ld", dscore, query_head, preferred_element_type=jnp.float32) * scale
    )
    grad_value = jnp.einsum("grl,rgc->lc", weight_b, cot_head, preferred_element_type=jnp.float32)
    return (grad_query, jnp.concatenate([grad_key, grad_value], axis=1))


def earlier_rows(packed, distance):
    return shifted(packed, "ctx", distance)


def later_grads(term, distance):
    return shifted(term, "ctx", -distance)


def per_device(queries, keys, values, cotangent, selected):
    local_rows = queries.shape[0]
    devices = lax.axis_size("ctx")
    device = lax.axis_index("ctx")
    pieces = BLOCK // local_rows
    group = QH // KVH
    width = 2 * KVH
    span = 2 * pieces * local_rows
    table = lax.all_gather(selected, "ctx", axis=0, tiled=True)
    my_block = device // pieces
    my_piece = device % pieces
    packed = jnp.concatenate(
        [keys.reshape(local_rows, KVH, HD), values.reshape(local_rows, KVH, HD)], axis=2
    )
    asked = jnp.sum((table == my_block).reshape(devices, KVH, 2), axis=2).astype(jnp.bfloat16)
    chosen = selected[0]
    live = chosen >= 0
    source = jnp.maximum(chosen, 0)[:, None] * pieces + jnp.arange(pieces, dtype=jnp.int32)[None, :]
    outgoing = jnp.einsum("ph,rhc->prc", asked, packed, preferred_element_type=jnp.float32).astype(
        jnp.bfloat16
    )
    fetched = lax.all_to_all(outgoing, "ctx", split_axis=0, concat_axis=0, tiled=True)
    picked = fetched[source.reshape(-1)].reshape(KVH, span, 2 * HD)
    near = [packed] + [earlier_rows(packed, 1)]
    near_rows = jnp.transpose(jnp.stack(near, axis=0), (2, 0, 1, 3)).reshape(
        KVH, pieces * local_rows, 2 * HD
    )
    query_pos = my_piece * local_rows + jnp.arange(local_rows, dtype=jnp.int32)
    slot_piece = my_piece - jnp.arange(pieces, dtype=jnp.int32)
    slot_pos = (
        slot_piece[:, None] * local_rows + jnp.arange(local_rows, dtype=jnp.int32)[None, :]
    ).reshape(-1)
    slot_live = jnp.repeat(slot_piece >= 0, local_rows)
    near_valid = (slot_pos[None, :] <= query_pos[:, None]) & slot_live[None, :]
    far_valid = jnp.repeat(live.reshape(KVH, 2), span // 2, axis=1)
    valid = jnp.concatenate(
        [
            jnp.broadcast_to(near_valid[None], (KVH, local_rows, pieces * local_rows)),
            jnp.broadcast_to(far_valid[:, None, :], (KVH, local_rows, span)),
        ],
        axis=2,
    )
    query_heads = jnp.transpose(queries.reshape(local_rows, KVH, group, HD), (1, 0, 2, 3))
    cot_heads = jnp.transpose(cotangent.reshape(local_rows, KVH, group, HD), (1, 0, 2, 3))
    all_rows = jnp.concatenate([near_rows, picked], axis=1)
    attended_heads, top, total = lax.map(
        forward_head, (query_heads, all_rows[..., :HD], all_rows[..., HD:], valid)
    )
    grad_query_heads, grad_rows = lax.map(
        backward_head,
        (query_heads, all_rows[..., :HD], all_rows[..., HD:], valid, cot_heads, top, total),
    )
    near_grad = grad_rows[:, : pieces * local_rows].reshape(KVH, pieces, local_rows, 2 * HD)
    own_total = near_grad[:, 0]
    own_total = own_total + later_grads(near_grad[:, 1].astype(jnp.bfloat16), 1).astype(jnp.float32)
    far_grad = (
        grad_rows[:, pieces * local_rows :]
        .astype(jnp.bfloat16)
        .reshape(width * pieces, local_rows, 2 * HD)
    )
    target = jnp.where(jnp.repeat(live, pieces), source.reshape(-1), devices)
    outgoing_grads = (
        jnp.zeros((devices, local_rows, 2 * HD), jnp.bfloat16).at[target].set(far_grad, mode="drop")
    )
    returned = lax.all_to_all(outgoing_grads, "ctx", split_axis=0, concat_axis=0, tiled=True)
    gathered_total = jnp.einsum("ph,prc->rhc", asked, returned, preferred_element_type=jnp.float32)
    grad_all = jnp.transpose(own_total, (1, 0, 2)) + gathered_total
    attended = jnp.transpose(attended_heads, (1, 0, 2, 3)).reshape(local_rows, QH * HD)
    grad_queries = jnp.transpose(grad_query_heads, (1, 0, 2, 3)).reshape(local_rows, QH * HD)
    grad_keys = grad_all[..., :HD].reshape(local_rows, KVH * HD).astype(jnp.bfloat16)
    grad_values = grad_all[..., HD:].reshape(local_rows, KVH * HD).astype(jnp.bfloat16)
    return (attended, grad_queries, grad_keys, grad_values)


def solution(mesh):
    in_specs = (P("ctx", None), P("ctx", None), P("ctx", None), P("ctx", None), P("ctx", None))
    out_specs = (P("ctx", None), P("ctx", None), P("ctx", None), P("ctx", None))
    return jax.shard_map(
        per_device, mesh=mesh, in_specs=in_specs, out_specs=out_specs, check_vma=False
    )
```

profile of v0, /device:TPU:84, one launch (start us, length us, event | category | flops | bytes accessed | tf_op | source)
XLA Modules:
  0.0 817.4 jit_solution(61188168045279181)
XLA Ops:
  3.0 29.8 %all-gather = s32[128,1,16]{2,1,0:T(1,128)S(1)} all-gather(s32[1,1,16]{2,1,0:T(1,128)} %bitcast.253), channel_id=1, replica_groups=mesh['ctx'=128] {'ctx'}, dimensions={0}, use_global_device_ids=true | all-gather | bytes 8256 | tf_op jit(solution)/shard_map/all_gather | solution.py:73
  33.1 8.2 %convolution_convert_fusion = bf16[128,256,256]{2,0,1:T(8,128)(2,1)} fusion(bf16[256,8,256]{2,1,0:T(8,128)(2,1)S(1)} %constant_dynamic-update-slice_fusion, s32[128,8]{0,1:T(8,128)S(1)} %reduce_sum.27), kind=kOutput, calls=%fused_computation.71 | convolution fusion | flops 142607360 | bytes 17829888 | tf_op jit(solution)/shard_map/ph,rhc->prc/dot_general | solution.py:83
  41.3 16.2 %copy.52 = bf16[128,256,256]{2,1,0:T(8,128)(2,1)} copy(bf16[128,256,256]{2,0,1:T(8,128)(2,1)} %convolution_convert_fusion) | data formatting | bytes 33554432 | tf_op jit(solution)/shard_map/convert_element_type | solution.py:83
  57.5 10.2 %all-to-all-start = ((bf16[128,256,256]{2,1,0:T(8,128)(2,1)}), bf16[128,256,256]{2,1,0:T(8,128)(2,1)}, u32[]{:S(2)}, u32[]{:S(2)}) async-start(bf16[128,256,256]{2,1,0:T(8,128)(2,1)} %copy.52), calls=%async_computation | async-start | bytes 33554432 | tf_op jit(solution)/shard_map/all_to_all | solution.py:86
  67.8 2.2 collective-permute-start
  71.6 3.3 copy.55
  74.9 2.4 copy.57
  77.3 4.1 copy.59
  81.4 2.2 broadcast_in_dim.88
  83.9 4.4 pad_add_fusion
  88.3 169.2 %collective-permute-done = bf16[256,8,256]{2,1,0:T(8,128)(2,1)} collective-permute-done((bf16[256,8,256]{2,1,0:T(8,128)(2,1)S(1)}, bf16[256,8,256]{2,1,0:T(8,128)(2,1)}, u32[]{:S(2)}, u32[]{:S(2)}) %collective-permute-start) | collective-permute-done | bytes 1048608 | tf_op jit(solution)/shard_map/ppermute | solution.py:15
  260.6 48.1 %all-to-all-done = bf16[128,256,256]{2,1,0:T(8,128)(2,1)} async-done(((bf16[128,256,256]{2,1,0:T(8,128)(2,1)}), bf16[128,256,256]{2,1,0:T(8,128)(2,1)}, u32[]{:S(2)}, u32[]{:S(2)}) %all-to-all-start) | async-done | bytes 16777248 | tf_op jit(solution)/shard_map/all_to_all | solution.py:86
  308.8 8.5 %gather_fusion = bf16[32,256,256]{2,1,0:T(8,128)(2,1)} fusion(bf16[128,256,256]{2,1,0:T(8,128)(2,1)} %all-to-all-done, s32[1024]{0:T(1024)S(1)} %pad_clamp_fusion), kind=kCustom, calls=%fused_computation | custom fusion | bytes 8388736 | tf_op jit(solution)/shard_map/gather | solution.py:87
  317.3 4.2 pad_maximum_fusion
  323.1 65.7 %while.26 = (s32[]{:T(128)}, bf16[8,256,4,128]{1,3,2,0:T(8,128)(2,1)}, f32[8,4,256,1]{2,1,3,0:T(4,128)S(1)}, f32[8,4,256,1]{2,1,3,0:T(4,128)S(1)}, bf16[8,1536,1...) while((s32[]{:T(128)}, ...), condition=%wide.region_4.5_spmd, body=%wide.region_1.4_spmd.sunk | while | flops 824309760 | bytes 22190188 | solution.py:110
  327.6 3.6 fusion.97
  335.8 3.6 fusion.97
  340.6 2.1 fusion.95
  344.0 3.6 fusion.97
  348.8 2.1 fusion.95
  352.2 3.6 fusion.97
  357.0 2.1 fusion.95
  360.5 3.6 fusion.97
  368.7 3.6 fusion.97
  376.9 3.6 fusion.97
  385.1 3.6 fusion.97
  390.3 115.2 %while.27 = (s32[]{:T(128)}, bf16[8,256,4,128]{1,3,2,0:T(8,128)(2,1)}, f32[8,1536,256]{1,2,0:T(8,128)}, bf16[8,1536,128]{2,1,0:T(8,128)(2,1)S(1)}, pred[8,256,15...) while((s32[]{:T(128)}, ...), condition=%wide.region_7.8_spmd, body=%wide.region_5.7_spmd.sunk | while | flops 2029845504 | bytes 55610504 | solution.py:113
  393.5 3.1 fusion.107
  399.2 2.1 fusion.110
  401.3 2.1 fusion.111
  407.8 3.1 fusion.107
  413.5 2.1 fusion.110
  415.7 2.1 fusion.111
  422.2 3.1 fusion.107
  427.9 2.1 fusion.110
  430.0 2.1 fusion.111
  436.6 3.1 fusion.107
  442.3 2.1 fusion.110
  444.4 2.1 fusion.111
  451.0 3.1 fusion.107
  456.7 2.1 fusion.110
  458.8 2.1 fusion.111
  465.4 3.1 fusion.107
  471.1 2.1 fusion.110
  473.2 2.1 fusion.111
  479.8 3.1 fusion.107
  485.5 2.1 fusion.110
  487.6 2.1 fusion.111
  494.3 3.1 fusion.107
  499.9 2.1 fusion.110
  502.1 2.1 fusion.111
  505.4 10.0 %copy.64 = bf16[8,1536,256]{2,1,0:T(8,128)(2,1)} copy(f32[8,1536,256]{1,2,0:T(8,128)} %get-tuple-element.105) | data formatting | bytes 18874368 | tf_op jit(solution)/shard_map/while | solution.py:113
  515.4 4.5 slice.66
  519.9 5.9 broadcast_in_dim.90
  525.8 11.4 %scatter_fusion = bf16[128,256,256]{2,1,0:T(8,128)(2,1)} fusion(bf16[128,256,256]{2,1,0:T(8,128)(2,1)} %broadcast_in_dim.90, s32[32]{0:T(128)S(1)} %copy-done.3, bf16[32,256,256]{2,1,0:T(8,128)(2,1)} %bitcast.235), kind=kCustom, calls=%fused_computation.1 | custom fusion | bytes 12583040 | tf_op jit(solution)/shard_map/scatter | solution.py:127
  537.2 22.7 %all-to-all-start.1 = ((bf16[128,256,256]{2,1,0:T(8,128)(2,1)}), bf16[128,256,256]{2,1,0:T(8,128)(2,1)}, u32[]{:S(2)}, u32[]{:S(2)}) async-start(bf16[128,256,256]{2,1,0:T(8,128)(2,1)} %scatter_fusion), calls=%async_computation.1 | async-start | bytes 33554432 | tf_op jit(solution)/shard_map/all_to_all | solution.py:129
  559.9 4.6 slice.32
  564.4 5.6 copy.63
  571.7 2.2 collective-permute-start.1
  574.0 3.1 copy.74
  577.1 4.1 copy.75
  581.2 191.9 %collective-permute-done.1 = bf16[8,256,256]{2,0,1:T(8,128)(2,1)} collective-permute-done((bf16[8,256,256]{2,0,1:T(8,128)(2,1)S(1)}, bf16[8,256,256]{2,0,1:T(8,128)(2,1)}, u32[]{:S(2)}, u32[]{:S(2)}) %collective-permute-start.1) | collective-permute-done | bytes 1048608 | tf_op jit(solution)/shard_map/ppermute | solution.py:15
  773.1 27.4 %all-to-all-done.1 = bf16[128,256,256]{2,1,0:T(8,128)(2,1)} async-done(((bf16[128,256,256]{2,1,0:T(8,128)(2,1)}), bf16[128,256,256]{2,1,0:T(8,128)(2,1)}, u32[]{:S(2)}, u32[]{:S(2)}) %all-to-all-start.1) | async-done | bytes 16777248 | tf_op jit(solution)/shard_map/all_to_all | solution.py:129
  800.5 15.7 %fusion.59 = bf16[256,8,256]{2,1,0:T(8,128)(2,1)S(1)} fusion(f32[8,2,256,256]{3,0,2,1:T(8,128)} %bitcast.242, bf16[8,256,256]{2,0,1:T(8,128)(2,1)} %collective-permute-done.1, bf16[128,256,256]{2,1,0:T(8,128)(2,1)} %all-to-all-done.1, s32[128,8]{0,1:T(8,128)S(1)} %copy-done.2), kind=kOutput, calls=%fused_computation.82 | convolution fusion | flops 136315904 | bytes 20975616 | tf_op jit(solution)/shard_map/ph,prc->rhc/dot_general | solution.py:130
  (124 shorter events, 99.7 us)
Async XLA Ops:
  33.0 8.4 %copy-start.1 = (s32[128,8]{0,1:T(8,128)}, s32[128,8]{0,1:T(8,128)S(1)}, u32[]{:S(2)}) copy-start(s32[128,8]{0,1:T(8,128)S(1)} %reduce_sum.27) | copy-start | bytes 12292
  57.5 12.5 %copy-start.4 = (s32[1,16]{1,0:T(1,128)S(1)}, s32[1,16]{1,0:T(1,128)}, u32[]{:S(2)}) copy-start(s32[1,16]{1,0:T(1,128)} %param.13) | copy-start | bytes 196
  57.5 251.2 %all-to-all-start = ((bf16[128,256,256]{2,1,0:T(8,128)(2,1)}), bf16[128,256,256]{2,1,0:T(8,128)(2,1)}, u32[]{:S(2)}, u32[]{:S(2)}) async-start(bf16[128,256,256]{2,1,0:T(8,128)(2,1)} %copy.52), calls=%async_computation | async-start | bytes 33554432 | tf_op jit(solution)/shard_map/all_to_all | solution.py:86
  67.8 189.7 %collective-permute-start = (bf16[256,8,256]{2,1,0:T(8,128)(2,1)S(1)}, bf16[256,8,256]{2,1,0:T(8,128)(2,1)}, u32[]{:S(2)}, u32[]{:S(2)}) collective-permute-start(bf16[256,8,256]{2,1,0:T(8,128)(2,1)S(1)} %constant_dynamic-update-slice_fusion), channel_id=1, source_target_pairs={{0,1},{1,2},{2,3},{3,4},{4,5},{5,6},{6,7},{7,8},{8,9},{9,10},{10,1... | collective-permute-start | bytes 3145736 | tf_op jit(solution)/shard_map/ppermute | solution.py:15
  519.9 5.9 copy-start.3
  537.2 263.3 %all-to-all-start.1 = ((bf16[128,256,256]{2,1,0:T(8,128)(2,1)}), bf16[128,256,256]{2,1,0:T(8,128)(2,1)}, u32[]{:S(2)}, u32[]{:S(2)}) async-start(bf16[128,256,256]{2,1,0:T(8,128)(2,1)} %scatter_fusion), calls=%async_computation.1 | async-start | bytes 33554432 | tf_op jit(solution)/shard_map/all_to_all | solution.py:129
  564.4 9.6 %copy-start = (bf16[8,256,4,128]{1,3,2,0:T(8,128)(2,1)S(1)}, bf16[8,256,4,128]{1,3,2,0:T(8,128)(2,1)}, u32[]{:S(2)}) copy-start(bf16[8,256,4,128]{1,3,2,0:T(8,128)(2,1)} %get-tuple-element.101) | copy-start | bytes 6291460
  571.7 201.3 %collective-permute-start.1 = (bf16[8,256,256]{2,0,1:T(8,128)(2,1)S(1)}, bf16[8,256,256]{2,0,1:T(8,128)(2,1)}, u32[]{:S(2)}, u32[]{:S(2)}) collective-permute-start(bf16[8,256,256]{2,0,1:T(8,128)(2,1)S(1)} %fusion.62), channel_id=1, source_target_pairs={{1,0},{2,1},{3,2},{4,3},{5,4},{6,5},{7,6},{8,7},{9,8},{10,9},{11,1... | collective-permute-start | bytes 3145736 | tf_op jit(solution)/shard_map/ppermute | solution.py:15
  574.0 226.5 %copy-start.2 = (s32[128,8]{0,1:T(8,128)S(1)}, s32[128,8]{0,1:T(8,128)}, u32[]{:S(2)}) copy-start(s32[128,8]{0,1:T(8,128)} %copy-done.1) | copy-start | bytes 12292
where the time goes:
time: 821 us; the launch traced here: 817 us
  waiting for transfers between devices  437 us (53%)
  matrix products  156 us (19%)
  local copies, waits for them, and re-layouts  115 us (14%)
  other arithmetic  41.5 us (5%)
  starting transfers between devices  37.3 us (5%)
  blocking collectives  29.8 us (4%)
    ppermute x2, waiting for transfers between devices, shifted(): return lax.ppermute(block, axis, route)  361 us
    all_to_all x1, waiting for transfers between devices, per_device(): lax.all_to_all(outgoing, 'ctx', split_axis=0, concat_axis=0, tiled=True)  48.1 us
    dot_general x16, matrix products, scores_for(): jnp.einsum('rgd,ld->grl', query_head, key_rows, preferred_element_type=jn...  41.7 us
    all_gather x1, blocking collectives, per_device(): table = lax.all_gather(selected, 'ctx', axis=0, tiled=True)  29.8 us
    dot_general x8, matrix products, forward_head(): jnp.einsum('grl,lc->rgc', weight, value_rows, preferred_element_type=jnp....  29.2 us
    all_to_all x1, waiting for transfers between devices, per_device(): lax.all_to_all(outgoing_grads, 'ctx', split_axis=0, concat_axis=0, tiled=...  27.4 us
    all_to_all x1, starting transfers between devices, per_device(): lax.all_to_all(outgoing_grads, 'ctx', split_axis=0, concat_axis=0, tiled=...  22.7 us
    broadcast_in_dim x16, local copies, waits for them, and re-layouts, scores_for(): return jnp.where(valid[None], score, -1e+30)  18.1 us
  transfers between devices with their start and end apart: 4, of which 4 were waited for; matrix products, arithmetic and copies ran while one was open for 5% of the time, Pallas kernels for 0%

commit v1 on v0

v1 whole, which is shorter than its diff:
```python
import math

import jax
import jax.numpy as jnp
from jax import lax
from jax.experimental import pallas as pl
from jax.experimental.pallas import tpu as pltpu
from jax.sharding import PartitionSpec as P

HD = 128
QH = 32
KVH = 8
BLOCK = 512
ROWS = 256
BLOCKS = 64
HALF = KVH // 2
GROUP = QH // KVH
FAR = 2 * BLOCK
SCALE = HD ** -0.5
SCALE_LOG2 = SCALE * math.log2(math.e)
NN = (((1,), (0,)), ((), ()))
NT = (((1,), (1,)), ((), ()))
TN = (((0,), (0,)), ((), ()))
f32 = jnp.float32
bf16 = jnp.bfloat16

PAIR = [(i, i ^ 1) for i in range(2 * BLOCKS)]
SAME_HALF = [list(range(k, 2 * BLOCKS, 2)) for k in (0, 1)]


def dot(a, b, dims):
    return lax.dot_general(a, b, dims, preferred_element_type=f32)


def pick_kernel(table, shares, out):
    step = pl.program_id(0)
    count = out.shape[0]
    for i in range(count):
        row = (step * count + i) * 2 * HALF
        for h in range(HALF):
            first = jnp.maximum(table[row + 2 * h], 0)
            second = jnp.maximum(table[row + 2 * h + 1], 0)
            for kv in range(2):
                tile = kv * HALF + h
                both = jnp.concatenate(
                    [shares[first, tile].astype(f32), shares[second, tile].astype(f32)], axis=0
                )
                out[i, h, kv] = both.astype(bf16)


def pick(table, shares):
    count = 8
    return pl.pallas_call(
        pick_kernel,
        grid_spec=pltpu.PrefetchScalarGridSpec(
            num_scalar_prefetch=1,
            grid=(BLOCKS // count,),
            in_specs=[pl.BlockSpec(shares.shape, lambda i, t: (0, 0, 0, 0))],
            out_specs=pl.BlockSpec((count, HALF, 2, 16, HD), lambda i, t: (i, 0, 0, 0, 0)),
        ),
        out_shape=jax.ShapeDtypeStruct((BLOCKS, HALF, 2, 16, HD), bf16),
        compiler_params=pltpu.CompilerParams(vmem_limit_bytes=32 * 2**20),
        name="pick",
    )(table, shares)


def add_kernel(table, terms, out, total):
    step = pl.program_id(0)
    count = terms.shape[0]

    @pl.when(step == 0)
    def _():
        total[...] = jnp.zeros_like(total)

    for i in range(count):
        row = (step * count + i) * 2 * HALF
        places = []
        sums = []
        for h in range(HALF):
            for e in range(2):
                block = table[row + 2 * h + e]
                slot = jnp.where(block < 0, BLOCKS, block)
                for kv in range(2):
                    places.append((slot, kv * HALF + h))
                    term = terms[i, h, kv].astype(f32)[8 * e : 8 * e + 8]
                    sums.append(total[slot, kv * HALF + h] + term)
        for place, value in zip(places, sums):
            total[place] = value

    @pl.when(step == pl.num_programs(0) - 1)
    def _():
        out[...] = total[:BLOCKS].astype(bf16)


def add_terms(table, terms):
    count = 8
    return pl.pallas_call(
        add_kernel,
        grid_spec=pltpu.PrefetchScalarGridSpec(
            num_scalar_prefetch=1,
            grid=(BLOCKS // count,),
            in_specs=[pl.BlockSpec((count, HALF, 2, 16, HD), lambda i, t: (i, 0, 0, 0, 0))],
            out_specs=pl.BlockSpec((BLOCKS, 2 * HALF, 8, HD), lambda i, t: (0, 0, 0, 0)),
            scratch_shapes=[pltpu.VMEM((BLOCKS + 1, 2 * HALF, 8, HD), f32)],
        ),
        out_shape=jax.ShapeDtypeStruct((BLOCKS, 2 * HALF, 8, HD), bf16),
        compiler_params=pltpu.CompilerParams(vmem_limit_bytes=32 * 2**20),
        name="add_terms",
    )(table, terms)


def attention_kernel(
    chosen, queries, cot, keys, values, far, att, grad_q, grad_k, grad_v, grad_far, K, V, sum_k, sum_v
):
    h = pl.program_id(0)
    g = pl.program_id(1)

    @pl.when(g == 0)
    def _():
        K[:ROWS] = keys[ROWS:]
        K[ROWS:BLOCK] = keys[:ROWS]
        K[BLOCK:] = far[:, 0, 0].reshape(FAR, HD)
        V[:ROWS] = values[ROWS:]
        V[ROWS:BLOCK] = values[:ROWS]
        V[BLOCK:] = far[:, 0, 1].reshape(FAR, HD)
        sum_k[...] = jnp.zeros_like(sum_k)
        sum_v[...] = jnp.zeros_like(sum_v)

    causal = lax.broadcasted_iota(jnp.int32, (ROWS, ROWS), 0) >= lax.broadcasted_iota(
        jnp.int32, (ROWS, ROWS), 1
    )
    first = chosen[2 * h]
    second = chosen[2 * h + 1]

    def run(masked):
        for piece in (0, 1):
            low = ROWS * (1 - piece)
            width = BLOCK + FAR - low
            rows = slice(ROWS * piece, ROWS * piece + ROWS)
            q = queries[rows]
            k = K[low:]
            v = V[low:]
            score = dot(q, k, NT)
            diagonal = jnp.where(causal, score[:, :ROWS], -1e30)
            rest = score[:, ROWS:]
            if masked:
                col = lax.broadcasted_iota(jnp.int32, (1, width - ROWS), 1) - (width - ROWS - FAR)
                entry = jnp.where(jnp.bitwise_and(col, 8) == 0, first, second)
                rest = rest + jnp.where((col >= 0) & (entry < 0), -1e30, 0.0)
            score = jnp.concatenate([diagonal, rest], axis=1)
            top = jnp.max(score, axis=1, keepdims=True)
            raised = jnp.exp2(score * SCALE_LOG2 - top * SCALE_LOG2)
            over = 1.0 / jnp.sum(raised, axis=1, keepdims=True)
            raised_b = raised.astype(bf16)
            out = dot(raised_b, v, NN) * over
            att[rows] = out.astype(bf16)
            cot_over = (cot[rows].astype(f32) * over).astype(bf16)
            delta = jnp.sum(cot_over.astype(f32) * out, axis=1, keepdims=True)
            dweight = dot(cot_over, v, NT)
            dscore = (raised * (dweight - delta)).astype(bf16)
            grad_q[rows] = (dot(dscore, k, NN) * SCALE).astype(bf16)
            sum_v[:, low:] += dot(cot_over, raised_b, TN)
            sum_k[:, low:] += dot(q, dscore, TN)

    alive = jnp.minimum(first, second) >= 0

    @pl.when(alive)
    def _():
        run(False)

    @pl.when(jnp.logical_not(alive))
    def _():
        run(True)

    @pl.when(g == pl.num_programs(1) - 1)
    def _():
        all_k = sum_k[...].T * SCALE
        all_v = sum_v[...].T
        grad_k[:ROWS] = all_k[ROWS:BLOCK]
        grad_k[ROWS:] = all_k[:ROWS]
        grad_v[:ROWS] = all_v[ROWS:BLOCK]
        grad_v[ROWS:] = all_v[:ROWS]
        grad_far[:, 0, 0] = all_k[BLOCK:].astype(bf16).reshape(BLOCKS, 16, HD)
        grad_far[:, 0, 1] = all_v[BLOCK:].astype(bf16).reshape(BLOCKS, 16, HD)


def attention(chosen, queries, cot, keys, values, far):
    per_query = pl.BlockSpec((BLOCK, HD), lambda h, g, c: (0, GROUP * h + g))
    per_key = pl.BlockSpec((BLOCK, HD), lambda h, g, c: (0, h))
    gated = pl.BlockSpec((BLOCKS, 1, 2, 16, HD), lambda h, g, c: (0, h, 0, 0, 0))
    return pl.pallas_call(
        attention_kernel,
        grid_spec=pltpu.PrefetchScalarGridSpec(
            num_scalar_prefetch=1,
            grid=(HALF, GROUP),
            in_specs=[per_query, per_query, per_key, per_key, gated],
            out_specs=[per_query, per_query, per_key, per_key, gated],
            scratch_shapes=[
                pltpu.VMEM((BLOCK + FAR, HD), bf16),
                pltpu.VMEM((BLOCK + FAR, HD), bf16),
                pltpu.VMEM((HD, BLOCK + FAR), f32),
                pltpu.VMEM((HD, BLOCK + FAR), f32),
            ],
        ),
        out_shape=[
            jax.ShapeDtypeStruct(queries.shape, bf16),
            jax.ShapeDtypeStruct(queries.shape, bf16),
            jax.ShapeDtypeStruct(keys.shape, f32),
            jax.ShapeDtypeStruct(keys.shape, f32),
            jax.ShapeDtypeStruct(far.shape, bf16),
        ],
        compiler_params=pltpu.CompilerParams(vmem_limit_bytes=48 * 2**20),
        name="attention",
    )(chosen, queries, cot, keys, values, far)


def spread(x):
    return lax.all_to_all(x, "ctx", 0, 0, axis_index_groups=SAME_HALF, tiled=True)


def halves(x, core):
    width = x.shape[1] // 2
    left, right = x[:, :width], x[:, width:]
    return jnp.where(core == 0, left, right), jnp.where(core == 0, right, left)


def swap(x):
    return lax.ppermute(x, "ctx", PAIR)


def in_order(mine, other, core, axis):
    return jnp.where(
        core == 0,
        jnp.concatenate([mine, other], axis=axis),
        jnp.concatenate([other, mine], axis=axis),
    )


def to_block(x, core):
    mine, other = halves(x, core)
    return in_order(mine, swap(other), core, 0)


def from_block(x, core):
    top, bottom = x[:ROWS], x[ROWS:]
    mine = jnp.where(core == 0, top, bottom)
    other = jnp.where(core == 0, bottom, top)
    return in_order(mine, swap(other), core, 1)


def per_device(queries, keys, values, cotangent, selected):
    core = lax.axis_index("ctx") % 2
    my_keys, other_keys = halves(keys, core)
    my_values, other_values = halves(values, core)
    near = in_order(
        jnp.concatenate([my_keys, my_values], axis=1),
        swap(jnp.concatenate([other_keys, other_values], axis=1)),
        core,
        0,
    )
    shares = jnp.transpose(near.reshape(BLOCKS, 8, 2 * HALF, HD), (0, 2, 1, 3))
    row = jnp.pad(selected.astype(bf16), ((0, 7), (0, HD - selected.shape[1])))
    shares = jnp.concatenate(
        [shares, jnp.broadcast_to(row[None, None], (BLOCKS, 1, 8, HD))], axis=1
    )
    shares = spread(shares)
    table = shares[:, 2 * HALF, 0, : 2 * KVH].astype(jnp.int32)
    table = jnp.where(core == 0, table[:, :KVH], table[:, KVH:]).reshape(-1)
    chosen = jnp.where(core == 0, selected[0, :KVH], selected[0, KVH:])
    far = spread(pick(table, shares))
    block_queries = to_block(queries, core)
    block_cot = to_block(cotangent, core)
    attended, grad_q, grad_k, grad_v, grad_far = attention(
        chosen, block_queries, block_cot, near[:, : HALF * HD], near[:, HALF * HD :], far
    )
    summed = spread(add_terms(table, spread(grad_far)))
    summed = jnp.transpose(summed, (0, 2, 1, 3)).reshape(BLOCK, 2 * HALF * HD).astype(f32)
    grad_k = (grad_k + summed[:, : HALF * HD]).astype(bf16)
    grad_v = (grad_v + summed[:, HALF * HD :]).astype(bf16)
    return (
        from_block(attended, core),
        from_block(grad_q, core),
        from_block(grad_k, core),
        from_block(grad_v, core),
    )


def solution(mesh):
    specs = (P("ctx", None),) * 5
    return jax.shard_map(
        per_device, mesh=mesh, in_specs=specs, out_specs=specs[:4], check_vma=False
    )
```

time: 821 us -> 198 us (0.24)
  the two profiles are of different devices: /device:TPU:84 before, /device:TPU:1 now
where the time goes in v1:
time: 198 us; the launch traced here: 197 us
  Pallas kernels  58.2 us (29%)
  waiting for transfers between devices  48.4 us (24%)
  starting transfers between devices  32.7 us (17%)
  blocking collectives  30.4 us (15%)
  other arithmetic  24.2 us (12%)
  local copies, waits for them, and re-layouts  2.52 us (1%)
    pallas_call x1, Pallas kernels, attention(): pl.pallas_call(attention_kernel, grid_spec=pltpu.PrefetchScalarGridSpec(n...  51.6 us
    all_to_all x3, waiting for transfers between devices, spread(): lax.all_to_all(x, 'ctx', 0, 0, axis_index_groups=SAME_HALF, tiled=True)  46.3 us
    all_to_all x1, blocking collectives, spread(): lax.all_to_all(x, 'ctx', 0, 0, axis_index_groups=SAME_HALF, tiled=True)  30.4 us
    all_to_all x3, starting transfers between devices, spread(): lax.all_to_all(x, 'ctx', 0, 0, axis_index_groups=SAME_HALF, tiled=True)  17.4 us
    ppermute x7, starting transfers between devices, swap(): return lax.ppermute(x, 'ctx', PAIR)  15.2 us
    select_n x7, other arithmetic, in_order(): jnp.where(core == 0, jnp.concatenate([mine, other], axis=axis), jnp.conca...  14.4 us
    select_n x4, other arithmetic, from_block(): mine = jnp.where(core == 0, top, bottom)  5.8 us
  transfers between devices with their start and end apart: 10, of which 5 were waited for; matrix products, arithmetic and copies ran while one was open for 11% of the time, Pallas kernels for 1%

profile of v1, /device:TPU:1, one launch (start us, length us, event | category | flops | bytes accessed | tf_op | source)
XLA Modules:
  0.0 197.2 jit_solution(15890742182465535939)
XLA Ops:
  0.6 0.0 copy-start.6
  0.7 1.3 broadcast_select_fusion.14
  1.9 0.1 pad_maximum_fusion.1
  2.0 1.5 collective-permute-start.2
  3.5 0.0 copy-done.6
  3.5 1.5 collective-permute-done.2
  5.0 0.4 maximum_select_fusion.4
  5.5 0.1 pad_maximum_fusion
  5.6 30.4 %all_to_all.20.shares = bf16[64,9,8,128]{3,2,1,0:T(8,128)(2,1)S(1)} all-to-all(bf16[64,9,8,128]{3,2,1,0:T(8,128)(2,1)S(1)} %pad_maximum_fusion), channel_id=1, replica_groups={{0,2,4,6,8,10,12,14,16,18,20,22,24,26,28,30,32,34,36,38,40,42,44,46,48,..., dimensions={0} | all-to-all | bytes 2359296 | tf_op jit(solution)/shard_map/all_to_all | solution.py:218
  36.1 0.1 slice_select_fusion
  36.1 0.1 reshape.26.table
  36.2 3.9 %pick.1 = bf16[64,4,2,16,128]{4,3,2,1,0:T(8,128)(2,1)} custom-call(s32[512]{0:T(512)S(1)} %reshape.26.table, bf16[64,9,8,128]{3,2,1,0:T(8,128)(2,1)S(1)} %all_to_all.20.shares), custom_call_target="tpu_custom_call" | custom-call | tf_op jit(solution)/shard_map/pick/pallas_call | solution.py:53
  40.1 0.0 copy-start.4
  40.1 5.7 %all-to-all-start.1 = ((bf16[64,4,2,16,128]{4,3,2,1,0:T(8,128)(2,1)}), bf16[64,4,2,16,128]{4,3,2,1,0:T(8,128)(2,1)}, u32[]{:S(2)}, u32[]{:S(2)}) async-start(bf16[64,4,2,16,128]{4,3,2,1,0:T(8,128)(2,1)} %pick.1), calls=%async_computation.1 | async-start | bytes 4194304 | tf_op jit(solution)/shard_map/all_to_all | solution.py:218
  45.8 0.0 copy-done.4
  45.9 0.0 copy-start.5
  45.9 0.1 broadcast_select_fusion.7
  46.0 1.9 collective-permute-start
  47.9 0.0 copy-done.5
  47.9 0.1 broadcast_select_fusion.5
  48.1 1.4 collective-permute-start.1
  49.5 0.1 fusion.2.chosen
  49.6 0.1 fusion.3
  49.6 0.6 collective-permute-done
  50.2 2.4 %maximum_select_fusion.queries = bf16[512,2048]{1,0:T(8,128)(2,1)} fusion(bf16[256,2048]{1,0:T(8,128)(2,1)S(1)} %collective-permute-done, bf16[256,2048]{1,0:T(8,128)(2,1)S(1)} %get-tuple-element.22, pred[]{:T(512)S(6)} %eq.4), kind=kLoop, calls=%fused_computation | loop fusion | flops 9437184 | bytes 4194305 | tf_op jit(solution)/shard_map/jit(_where)/select_n | solution.py:232
  52.6 0.0 collective-permute-done.1
  52.6 2.4 %maximum_select_fusion.1.cot = bf16[512,2048]{1,0:T(8,128)(2,1)} fusion(bf16[256,2048]{1,0:T(8,128)(2,1)S(1)} %collective-permute-done.1, bf16[256,2048]{1,0:T(8,128)(2,1)S(1)} %get-tuple-element.20, pred[]{:T(512)S(6)} %eq.4), kind=kLoop, calls=%fused_computation.1 | loop fusion | flops 9437184 | bytes 4194305 | tf_op jit(solution)/shard_map/jit(_where)/select_n | solution.py:232
  55.0 18.6 %all-to-all-done.1.far = bf16[64,4,2,16,128]{4,3,2,1,0:T(8,128)(2,1)} async-done(((bf16[64,4,2,16,128]{4,3,2,1,0:T(8,128)(2,1)}), bf16[64,4,2,16,128]{4,3,2,1,0:T(8,128)(2,1)}, u32[]{:S(2)}, u32[]{:S(2)}) %all-to-all-start.1) | async-done | bytes 2097184 | tf_op jit(solution)/shard_map/all_to_all | solution.py:218
  73.6 51.6 %attention.1 = (bf16[512,2048]{1,0:T(8,128)(2,1)S(1)}, bf16[512,2048]{1,0:T(8,128)(2,1)}, f32[512,512]{1,0:T(8,128)S(1)}, f32[512,512]{1,0:T(8,128)S(1)}, bf16[64,4,2,16,128]{4,3,2,1,0:T(8,128)(2,1)}) custom-call(s32[8]{0:T(128)S(1)} %fusion.2.chosen, bf16[512,2048]{1,0:T(8,128)(2,1)} %maximum_select_fusion.queries, ...), custom_call_target="tpu_custom_call" | custom-call | tf_op jit(solution)/shard_map/attention/pallas_call | solution.py:191
  125.2 0.0 copy-start
  125.2 1.3 copy-done
  126.5 0.0 copy-start.1
  126.5 1.0 copy-done.1
  127.5 6.2 %all-to-all-start.2 = ((bf16[64,4,2,16,128]{4,3,2,1,0:T(8,128)(2,1)}), bf16[64,4,2,16,128]{4,3,2,1,0:T(8,128)(2,1)S(1)}, u32[]{:S(2)}, u32[]{:S(2)}) async-start(bf16[64,4,2,16,128]{4,3,2,1,0:T(8,128)(2,1)} %get-tuple-element.12), calls=%async_computation.2 | async-start | bytes 4194304 | tf_op jit(solution)/shard_map/all_to_all | solution.py:218
  133.7 3.0 %broadcast_select_fusion.3 = (bf16[256,2048]{1,0:T(8,128)(2,1)}, bf16[256,2048]{1,0:T(8,128)(2,1)}) fusion(pred[]{:T(512)S(6)} %eq.4, bf16[512,2048]{1,0:T(8,128)(2,1)} %copy-done), kind=kLoop, calls=%fused_computation.14 | loop fusion | flops 1048576 | bytes 4194305 | tf_op jit(solution)/shard_map/jit(_where)/select_n | solution.py:246
  136.7 2.4 %collective-permute-start.3 = (bf16[256,2048]{1,0:T(8,128)(2,1)}, bf16[256,2048]{1,0:T(8,128)(2,1)}, u32[]{:S(2)}, u32[]{:S(2)}) collective-permute-start(bf16[256,2048]{1,0:T(8,128)(2,1)} %get-tuple-element.19), channel_id=1, source_target_pairs={{0,1},{1,0},{2,3},{3,2},{4,5},{5,4},{6,7},{7,6},{8,9},{9,8},{10,11... | collective-permute-start | bytes 3145736 | tf_op jit(solution)/shard_map/ppermute | solution.py:228
  139.1 22.3 %all-to-all-done.2.terms = bf16[64,4,2,16,128]{4,3,2,1,0:T(8,128)(2,1)S(1)} async-done(((bf16[64,4,2,16,128]{4,3,2,1,0:T(8,128)(2,1)}), bf16[64,4,2,16,128]{4,3,2,1,0:T(8,128)(2,1)S(1)}, u32[]{:S(2)}, u32[]{:S(2)}) %all-to-all-start.2) | async-done | bytes 2097184 | tf_op jit(solution)/shard_map/all_to_all | solution.py:218
  161.3 2.7 %add_terms.1 = bf16[64,8,8,128]{3,2,1,0:T(8,128)(2,1)} custom-call(s32[512]{0:T(512)S(1)} %reshape.26.table, bf16[64,4,2,16,128]{4,3,2,1,0:T(8,128)(2,1)S(1)} %all-to-all-done.2.terms), custom_call_target="tpu_custom_call" | custom-call | tf_op jit(solution)/shard_map/add_terms/pallas_call | solution.py:97
  164.1 5.5 %all-to-all-start.3 = ((bf16[64,8,8,128]{3,2,1,0:T(8,128)(2,1)}), bf16[64,8,8,128]{3,2,1,0:T(8,128)(2,1)}, u32[]{:S(2)}, u32[]{:S(2)}) async-start(bf16[64,8,8,128]{3,2,1,0:T(8,128)(2,1)} %add_terms.1), calls=%async_computation.3 | async-start | bytes 2097152 | tf_op jit(solution)/shard_map/all_to_all | solution.py:218
  169.6 0.0 copy-start.3
  169.6 2.7 %broadcast_select_fusion.1 = (bf16[256,2048]{1,0:T(8,128)(2,1)S(1)}, bf16[256,2048]{1,0:T(8,128)(2,1)}) fusion(pred[]{:T(512)S(6)} %eq.4, bf16[512,2048]{1,0:T(8,128)(2,1)} %get-tuple-element.10), kind=kLoop, calls=%fused_computation.12 | loop fusion | flops 1048576 | bytes 4194305 | tf_op jit(solution)/shard_map/jit(_where)/select_n | solution.py:246
  172.4 3.5 %collective-permute-start.4 = (bf16[256,2048]{1,0:T(8,128)(2,1)}, bf16[256,2048]{1,0:T(8,128)(2,1)}, u32[]{:S(2)}, u32[]{:S(2)}) collective-permute-start(bf16[256,2048]{1,0:T(8,128)(2,1)} %get-tuple-element.17), channel_id=1, source_target_pairs={{0,1},{1,0},{2,3},{3,2},{4,5},{5,4},{6,7},{7,6},{8,9},{9,8},{10,11... | collective-permute-start | bytes 3145736 | tf_op jit(solution)/shard_map/ppermute | solution.py:228
  175.9 0.0 collective-permute-done.3
  175.9 0.0 copy-done.3
  175.9 3.7 %maximum_select_fusion.2 = bf16[256,4096]{1,0:T(8,128)(2,1)} fusion(bf16[256,2048]{1,0:T(8,128)(2,1)} %collective-permute-done.3, bf16[256,2048]{1,0:T(8,128)(2,1)S(1)} %copy-done.3, pred[]{:T(512)S(6)} %eq.4), kind=kLoop, calls=%fused_computation.2 | loop fusion | flops 9437184 | bytes 4194305 | tf_op jit(solution)/shard_map/jit(_where)/select_n | solution.py:232
  179.6 0.0 copy-start.2
  179.6 5.4 %all-to-all-done.3 = bf16[64,8,8,128]{3,2,1,0:T(8,128)(2,1)} async-done(((bf16[64,8,8,128]{3,2,1,0:T(8,128)(2,1)}), bf16[64,8,8,128]{3,2,1,0:T(8,128)(2,1)}, u32[]{:S(2)}, u32[]{:S(2)}) %all-to-all-start.3) | async-done | bytes 1048608 | tf_op jit(solution)/shard_map/all_to_all | solution.py:218
  185.0 1.5 convert_bitcast_fusion
  186.4 0.0 copy-done.2
  186.4 0.6 fusion
  187.1 4.4 %collective-permute-start.6 = (bf16[256,512]{1,0:T(8,128)(2,1)S(1)}, bf16[256,512]{1,0:T(8,128)(2,1)S(1)}, u32[]{:S(2)}, u32[]{:S(2)}) collective-permute-start(bf16[256,512]{1,0:T(8,128)(2,1)S(1)} %get-tuple-element.27), channel_id=1, source_target_pairs={{0,1},{1,0},{2,3},{3,2},{4,5},{5,4},{6,7},{7,6},{8,9},{9,8},{10,11... | collective-permute-start | bytes 786440 | tf_op jit(solution)/shard_map/ppermute | solution.py:228
  191.5 0.1 collective-permute-start.5
  191.6 0.0 collective-permute-done.4
  191.6 3.7 %maximum_select_fusion.3 = bf16[256,4096]{1,0:T(8,128)(2,1)} fusion(bf16[256,2048]{1,0:T(8,128)(2,1)} %collective-permute-done.4, bf16[256,2048]{1,0:T(8,128)(2,1)S(1)} %get-tuple-element.16, pred[]{:T(512)S(6)} %eq.4), kind=kLoop, calls=%fused_computation.3 | loop fusion | flops 9437184 | bytes 4194305 | tf_op jit(solution)/shard_map/jit(_where)/select_n | solution.py:232
  195.3 0.0 collective-permute-done.6
  195.3 0.9 maximum_select_fusion.6
  196.2 0.0 collective-permute-done.5
  196.2 0.9 maximum_select_fusion.5
  (6 shorter events, 0.1 us)
Async XLA Ops:
  0.6 2.9 %copy-start.6 = (s32[1,16]{1,0:T(1,128)S(1)}, s32[1,16]{1,0:T(1,128)}, u32[]{:S(2)}) copy-start(s32[1,16]{1,0:T(1,128)} %param.9) | copy-start | bytes 196
  2.0 3.0 %collective-permute-start.2 = (bf16[256,1024]{1,0:T(8,128)(2,1)S(1)}, bf16[256,1024]{1,0:T(8,128)(2,1)S(1)}, u32[]{:S(2)}, u32[]{:S(2)}) collective-permute-start(bf16[256,1024]{1,0:T(8,128)(2,1)S(1)} %pad_maximum_fusion.1), channel_id=1, source_target_pairs={{0,1},{1,0},{2,3},{3,2},{4,5},{5,4},{6,7},{7,6},{8,9},{9,8},{10,11... | collective-permute-start | bytes 1572872 | tf_op jit(solution)/shard_map/ppermute | solution.py:228
  40.1 5.7 %copy-start.4 = (bf16[256,4096]{1,0:T(8,128)(2,1)S(1)}, bf16[256,4096]{1,0:T(8,128)(2,1)}, u32[]{:S(2)}) copy-start(bf16[256,4096]{1,0:T(8,128)(2,1)} %param.5) | copy-start | bytes 6291460
  40.1 33.5 %all-to-all-start.1 = ((bf16[64,4,2,16,128]{4,3,2,1,0:T(8,128)(2,1)}), bf16[64,4,2,16,128]{4,3,2,1,0:T(8,128)(2,1)}, u32[]{:S(2)}, u32[]{:S(2)}) async-start(bf16[64,4,2,16,128]{4,3,2,1,0:T(8,128)(2,1)} %pick.1), calls=%async_computation.1 | async-start | bytes 4194304 | tf_op jit(solution)/shard_map/all_to_all | solution.py:218
  45.9 2.1 %copy-start.5 = (bf16[256,4096]{1,0:T(8,128)(2,1)S(1)}, bf16[256,4096]{1,0:T(8,128)(2,1)}, u32[]{:S(2)}) copy-start(bf16[256,4096]{1,0:T(8,128)(2,1)} %param.8) | copy-start | bytes 6291460
  46.0 4.2 %collective-permute-start = (bf16[256,2048]{1,0:T(8,128)(2,1)S(1)}, bf16[256,2048]{1,0:T(8,128)(2,1)S(1)}, u32[]{:S(2)}, u32[]{:S(2)}) collective-permute-start(bf16[256,2048]{1,0:T(8,128)(2,1)S(1)} %get-tuple-element.23), channel_id=1, source_target_pairs={{0,1},{1,0},{2,3},{3,2},{4,5},{5,4},{6,7},{7,6},{8,9},{9,8},{10,11... | collective-permute-start | bytes 3145736 | tf_op jit(solution)/shard_map/ppermute | solution.py:228
  48.1 4.5 %collective-permute-start.1 = (bf16[256,2048]{1,0:T(8,128)(2,1)S(1)}, bf16[256,2048]{1,0:T(8,128)(2,1)S(1)}, u32[]{:S(2)}, u32[]{:S(2)}) collective-permute-start(bf16[256,2048]{1,0:T(8,128)(2,1)S(1)} %get-tuple-element.21), channel_id=1, source_target_pairs={{0,1},{1,0},{2,3},{3,2},{4,5},{5,4},{6,7},{7,6},{8,9},{9,8},{10,11... | collective-permute-start | bytes 3145736 | tf_op jit(solution)/shard_map/ppermute | solution.py:228
  125.2 1.3 copy-start
  126.5 1.0 copy-start.1
  127.5 33.9 %all-to-all-start.2 = ((bf16[64,4,2,16,128]{4,3,2,1,0:T(8,128)(2,1)}), bf16[64,4,2,16,128]{4,3,2,1,0:T(8,128)(2,1)S(1)}, u32[]{:S(2)}, u32[]{:S(2)}) async-start(bf16[64,4,2,16,128]{4,3,2,1,0:T(8,128)(2,1)} %get-tuple-element.12), calls=%async_computation.2 | async-start | bytes 4194304 | tf_op jit(solution)/shard_map/all_to_all | solution.py:218
  136.7 39.2 %collective-permute-start.3 = (bf16[256,2048]{1,0:T(8,128)(2,1)}, bf16[256,2048]{1,0:T(8,128)(2,1)}, u32[]{:S(2)}, u32[]{:S(2)}) collective-permute-start(bf16[256,2048]{1,0:T(8,128)(2,1)} %get-tuple-element.19), channel_id=1, source_target_pairs={{0,1},{1,0},{2,3},{3,2},{4,5},{5,4},{6,7},{7,6},{8,9},{9,8},{10,11... | collective-permute-start | bytes 3145736 | tf_op jit(solution)/shard_map/ppermute | solution.py:228
  164.1 20.9 %all-to-all-start.3 = ((bf16[64,8,8,128]{3,2,1,0:T(8,128)(2,1)}), bf16[64,8,8,128]{3,2,1,0:T(8,128)(2,1)}, u32[]{:S(2)}, u32[]{:S(2)}) async-start(bf16[64,8,8,128]{3,2,1,0:T(8,128)(2,1)} %add_terms.1), calls=%async_computation.3 | async-start | bytes 2097152 | tf_op jit(solution)/shard_map/all_to_all | solution.py:218
  169.6 6.3 %copy-start.3 = (bf16[256,2048]{1,0:T(8,128)(2,1)S(1)}, bf16[256,2048]{1,0:T(8,128)(2,1)}, u32[]{:S(2)}) copy-start(bf16[256,2048]{1,0:T(8,128)(2,1)} %get-tuple-element.18) | copy-start | bytes 3145732
  172.4 19.3 %collective-permute-start.4 = (bf16[256,2048]{1,0:T(8,128)(2,1)}, bf16[256,2048]{1,0:T(8,128)(2,1)}, u32[]{:S(2)}, u32[]{:S(2)}) collective-permute-start(bf16[256,2048]{1,0:T(8,128)(2,1)} %get-tuple-element.17), channel_id=1, source_target_pairs={{0,1},{1,0},{2,3},{3,2},{4,5},{5,4},{6,7},{7,6},{8,9},{9,8},{10,11... | collective-permute-start | bytes 3145736 | tf_op jit(solution)/shard_map/ppermute | solution.py:228
  179.6 6.9 %copy-start.2 = (f32[512,512]{1,0:T(8,128)S(1)}, f32[512,512]{1,0:T(8,128)}, u32[]{:S(2)}) copy-start(f32[512,512]{1,0:T(8,128)} %copy-done.1) | copy-start | bytes 3145732
  187.1 8.2 %collective-permute-start.6 = (bf16[256,512]{1,0:T(8,128)(2,1)S(1)}, bf16[256,512]{1,0:T(8,128)(2,1)S(1)}, u32[]{:S(2)}, u32[]{:S(2)}) collective-permute-start(bf16[256,512]{1,0:T(8,128)(2,1)S(1)} %get-tuple-element.27), channel_id=1, source_target_pairs={{0,1},{1,0},{2,3},{3,2},{4,5},{5,4},{6,7},{7,6},{8,9},{9,8},{10,11... | collective-permute-start | bytes 786440 | tf_op jit(solution)/shard_map/ppermute | solution.py:228
  191.5 4.7 %collective-permute-start.5 = (bf16[256,512]{1,0:T(8,128)(2,1)S(1)}, bf16[256,512]{1,0:T(8,128)(2,1)S(1)}, u32[]{:S(2)}, u32[]{:S(2)}) collective-permute-start(bf16[256,512]{1,0:T(8,128)(2,1)S(1)} %get-tuple-element.29), channel_id=1, source_target_pairs={{0,1},{1,0},{2,3},{3,2},{4,5},{5,4},{6,7},{7,6},{8,9},{9,8},{10,11... | collective-permute-start | bytes 786440 | tf_op jit(solution)/shard_map/ppermute | solution.py:228

commit v2 on v1

v2 whole, which is shorter than its diff:
```python
import math

import jax
import jax.numpy as jnp
from jax import lax
from jax.experimental import pallas as pl
from jax.experimental.pallas import tpu as pltpu
from jax.sharding import PartitionSpec as P

HD = 128
QH = 32
KVH = 8
BLOCK = 512
ROWS = 256
BLOCKS = 64
HALF = KVH // 2
GROUP = QH // KVH
FAR = 2 * BLOCK
SCALE = HD ** -0.5
SCALE_LOG2 = SCALE * math.log2(math.e)
NN = (((1,), (0,)), ((), ()))
NT = (((1,), (1,)), ((), ()))
TN = (((0,), (0,)), ((), ()))
f32 = jnp.float32
bf16 = jnp.bfloat16
LIMIT = 2.0**40

PAIR = [(i, i ^ 1) for i in range(2 * BLOCKS)]
SAME_HALF = [list(range(k, 2 * BLOCKS, 2)) for k in (0, 1)]


def pick_kernel(table, shares, out):
    step = pl.program_id(0)
    count, heads = out.shape[:2]

    def one(i, carry):
        row = (step * count + i) * 2 * heads
        for h in range(heads):
            first = jnp.maximum(table[row + 2 * h], 0)
            second = jnp.maximum(table[row + 2 * h + 1], 0)
            for kv in range(2):
                tile = kv * HALF + h
                both = jnp.concatenate(
                    [shares[first, tile].astype(f32), shares[second, tile].astype(f32)], axis=0
                )
                out[i, h, kv] = both.astype(bf16)
        return carry

    lax.fori_loop(0, count, one, 0, unroll=8)


def pick(table, shares):
    count = 32
    return pl.pallas_call(
        pick_kernel,
        grid_spec=pltpu.PrefetchScalarGridSpec(
            num_scalar_prefetch=1,
            grid=(BLOCKS // count,),
            in_specs=[pl.BlockSpec(shares.shape, lambda i, t: (0, 0, 0, 0))],
            out_specs=pl.BlockSpec((count, HALF, 2, 16, HD), lambda i, t: (i, 0, 0, 0, 0)),
        ),
        out_shape=jax.ShapeDtypeStruct((BLOCKS, HALF, 2, 16, HD), bf16),
        compiler_params=pltpu.CompilerParams(vmem_limit_bytes=60 * 2**20),
        name="pick",
    )(table, shares)


def add_kernel(table, terms, out, total):
    step = pl.program_id(0)
    count, heads = terms.shape[:2]

    @pl.when(step == 0)
    def _():
        total[...] = jnp.zeros_like(total)

    def one(i, carry):
        row = (step * count + i) * 2 * heads
        places = []
        sums = []
        for h in range(heads):
            for e in range(2):
                block = table[row + 2 * h + e]
                slot = jnp.where(block < 0, BLOCKS, block)
                for kv in range(2):
                    place = (slot, kv * heads + h)
                    term = terms[i, h, kv].astype(f32)[8 * e : 8 * e + 8]
                    places.append(place)
                    sums.append(total[place] + term)
        for place, value in zip(places, sums):
            total[place] = value
        return carry

    lax.fori_loop(0, count, one, 0, unroll=8)

    @pl.when(step == pl.num_programs(0) - 1)
    def _():
        out[...] = total[:BLOCKS].astype(bf16)


def add_terms(table, terms):
    count = 16
    tiles = 2 * terms.shape[1]
    whole = lambda i, t: (0, 0, 0, 0)
    return pl.pallas_call(
        add_kernel,
        grid_spec=pltpu.PrefetchScalarGridSpec(
            num_scalar_prefetch=1,
            grid=(BLOCKS // count,),
            in_specs=[pl.BlockSpec((count,) + terms.shape[1:], lambda i, t: (i, 0, 0, 0, 0))],
            out_specs=pl.BlockSpec((BLOCKS, tiles, 8, HD), whole),
            scratch_shapes=[pltpu.VMEM((BLOCKS + 1, tiles, 8, HD), f32)],
        ),
        out_shape=jax.ShapeDtypeStruct((BLOCKS, tiles, 8, HD), bf16),
        compiler_params=pltpu.CompilerParams(vmem_limit_bytes=60 * 2**20),
        name="add_terms",
    )(table, terms)


def finish_kernel(core, mine, other, near_mine, near_other, grad_k, grad_v):
    rows = grad_k.shape[0]
    for side, far, near in ((core[0], mine, near_mine), (1 - core[0], other, near_other)):
        tile = 0
        for out in (grad_k, grad_v):
            for h in range(HALF):
                term = far[:, tile].reshape(rows, HD).astype(f32)
                place = pl.ds(pl.multiple_of((side * HALF + h) * HD, HD), HD)
                out[:, place] = (near[:, HD * tile : HD * tile + HD] + term).astype(bf16)
                tile += 1


def finish(core, mine, other, near):
    steps = 4
    tiles = mine.shape[1]
    chunk = ROWS // 8 // steps
    near_mine, near_other = near
    far = pl.BlockSpec((chunk, tiles, 8, HD), lambda i, c: (i, 0, 0, 0))
    far_mine = pl.BlockSpec((chunk, tiles, 8, HD), lambda i, c: (i + steps * c[0], 0, 0, 0))
    rows = pl.BlockSpec((ROWS // steps, KVH * HD), lambda i, c: (i, 0))
    rows_mine = pl.BlockSpec((ROWS // steps, KVH * HD), lambda i, c: (i + steps * c[0], 0))
    return pl.pallas_call(
        finish_kernel,
        grid_spec=pltpu.PrefetchScalarGridSpec(
            num_scalar_prefetch=1,
            grid=(steps,),
            in_specs=[far_mine, far, rows_mine, rows],
            out_specs=[rows, rows],
        ),
        out_shape=[jax.ShapeDtypeStruct((ROWS, KVH * HD), bf16)] * 2,
        compiler_params=pltpu.CompilerParams(vmem_limit_bytes=12 * 2**20),
        name="finish",
    )(core.reshape(1), mine, other, near_mine, near_other)


def dot(a, b, dims):
    return lax.dot_general(a, b, dims, preferred_element_type=f32)


def cost(heads, keys, products):
    pairs = heads * GROUP * BLOCK * keys
    return pl.CostEstimate(
        flops=products * 4 * pairs * HD, transcendentals=pairs, bytes_accessed=heads * 5 * 2**20
    )


def lanes(values):
    each = HD // len(values)
    lane = lax.broadcasted_iota(jnp.int32, (ROWS, HD), 1)
    out = jnp.broadcast_to(values[-1], (ROWS, HD))
    for i in range(len(values) - 2, -1, -1):
        out = jnp.where(lane < (i + 1) * each, values[i], out)
    return out


def near_scores(q, keys_t, piece):
    score = dot(q, keys_t, NN) * SCALE_LOG2
    shape = (ROWS, ROWS)
    causal = lax.broadcasted_iota(jnp.int32, shape, 0) >= lax.broadcasted_iota(jnp.int32, shape, 1)
    diagonal = jnp.where(causal, score[:, ROWS * piece :], -1e30)
    return jnp.concatenate([score[:, :ROWS], diagonal], axis=1) if piece else diagonal


def near_forward_kernel(queries, keys, values, out, lse, keys_t):
    keys_t[...] = keys[...].T
    for piece in (0, 1):
        rows = slice(ROWS * piece, ROWS * piece + ROWS)
        width = ROWS * piece + ROWS
        found = []
        for g in range(GROUP):
            cols = slice(HD * g, HD * g + HD)
            score = near_scores(queries[rows, cols], keys_t[:, :width], piece)
            top = jnp.max(score, axis=1, keepdims=True)
            raised = jnp.exp2(score - top)
            total = jnp.sum(raised, axis=1, keepdims=True)
            out[rows, cols] = dot(raised.astype(bf16), values[:width], NN) * (1.0 / total)
            found.append(top + jnp.log2(total))
        lse[rows] = lanes(found)


def near_forward(queries, near):
    wide = pl.BlockSpec((BLOCK, GROUP * HD), lambda h: (0, h))
    key = pl.BlockSpec((BLOCK, HD), lambda h: (0, h))
    value = pl.BlockSpec((BLOCK, HD), lambda h: (0, HALF + h))
    return pl.pallas_call(
        near_forward_kernel,
        grid=(HALF,),
        in_specs=[wide, key, value],
        out_specs=[wide, key],
        out_shape=[
            jax.ShapeDtypeStruct(queries.shape, f32),
            jax.ShapeDtypeStruct((BLOCK, HALF * HD), f32),
        ],
        scratch_shapes=[pltpu.VMEM((HD, BLOCK), bf16)],
        compiler_params=pltpu.CompilerParams(vmem_limit_bytes=60 * 2**20),
        cost_estimate=cost(HALF, BLOCK * 3 // 4, 2),
        name="near_forward",
    )(queries, near, near)


def far_kernel(
    chosen, queries, cot, near_out, near_lse, far, att, grad_q, stats, grad_far, keys_t, values_t, sum_k, sum_v
):
    h = pl.program_id(0)
    first = chosen[2 * h]
    second = chosen[2 * h + 1]
    keys_t[...] = far[:, 0, 0].reshape(FAR, HD).T
    values_t[...] = far[:, 0, 1].reshape(FAR, HD).T

    def one(rows, cols, l0, masked, general):
        k = far[:, 0, 0].reshape(FAR, HD)
        v = far[:, 0, 1].reshape(FAR, HD)
        q = queries[rows, cols]
        score = dot(q, keys_t[...], NN) * SCALE_LOG2
        if masked:
            col = lax.broadcasted_iota(jnp.int32, (1, FAR), 1)
            entry = jnp.where(jnp.bitwise_and(col, 8) == 0, first, second)
            score = score + jnp.where(entry < 0, -1e30, 0.0)
        top = jnp.maximum(jnp.max(score, axis=1, keepdims=True), l0) if general else l0
        raised = jnp.exp2(score - top)
        near = jnp.exp2(l0 - top) if general else 1.0
        total = jnp.sum(raised, axis=1, keepdims=True) + near
        over = 1.0 / total
        raised_b = raised.astype(bf16)
        out = (dot(raised_b, v, NN) + near * near_out[rows, cols]) * over
        att[rows, cols] = out.astype(bf16)
        cot_over = (cot[rows, cols].astype(f32) * over).astype(bf16)
        delta = jnp.sum(cot_over.astype(f32) * out, axis=1, keepdims=True)
        dscore = (raised * (dot(cot_over, values_t[...], NN) - delta)).astype(bf16)
        grad_q[rows, cols] = dot(dscore, k, NN)
        sum_v[...] += dot(cot_over, raised_b, TN)
        sum_k[...] += dot(q, dscore, TN)
        return total, top + jnp.log2(total), delta * total

    def run(masked, general):
        sum_k[...] = jnp.zeros_like(sum_k)
        sum_v[...] = jnp.zeros_like(sum_v)

        def half(piece, worst):
            rows = pl.ds(pl.multiple_of(ROWS * piece, ROWS), ROWS)
            found = []
            for g in range(GROUP):
                cols = slice(HD * g, HD * g + HD)
                l0 = near_lse[rows, 32 * g : 32 * g + 1]
                total, lse, delta = one(rows, cols, l0, masked, general)
                worst = jnp.maximum(worst, total)
                found += [lse, delta]
            stats[rows, :] = lanes(found)
            return worst

        return jnp.max(lax.fori_loop(0, 2, half, jnp.zeros((ROWS, 1), f32)))

    worst = run(True, False)

    @pl.when(jnp.logical_not(worst <= LIMIT))
    def _():
        run(True, True)

    grad_far[:, 0, 0] = (sum_k[...].T * SCALE).astype(bf16).reshape(BLOCKS, 16, HD)
    grad_far[:, 0, 1] = sum_v[...].T.astype(bf16).reshape(BLOCKS, 16, HD)


def far_attention(chosen, queries, cot, near_out, near_lse, far):
    heads = far.shape[1]
    wide = pl.BlockSpec((BLOCK, GROUP * HD), lambda h, c: (0, h))
    lse = pl.BlockSpec((BLOCK, HD), lambda h, c: (0, h))
    out_wide = pl.BlockSpec((BLOCK, GROUP * HD), lambda h, c: (0, h))
    out_lse = pl.BlockSpec((BLOCK, HD), lambda h, c: (0, h))
    gated = pl.BlockSpec((BLOCKS, 1, 2, 16, HD), lambda h, c: (0, h, 0, 0, 0))
    return pl.pallas_call(
        far_kernel,
        grid_spec=pltpu.PrefetchScalarGridSpec(
            num_scalar_prefetch=1,
            grid=(heads,),
            in_specs=[wide, wide, wide, lse, gated],
            out_specs=[out_wide, out_wide, out_lse, gated],
            scratch_shapes=[pltpu.VMEM((HD, FAR), bf16)] * 2 + [pltpu.VMEM((HD, FAR), f32)] * 2,
        ),
        out_shape=[
            jax.ShapeDtypeStruct((BLOCK, heads * GROUP * HD), bf16),
            jax.ShapeDtypeStruct((BLOCK, heads * GROUP * HD), f32),
            jax.ShapeDtypeStruct((BLOCK, heads * HD), f32),
            jax.ShapeDtypeStruct(far.shape, bf16),
        ],
        compiler_params=pltpu.CompilerParams(vmem_limit_bytes=60 * 2**20),
        cost_estimate=cost(heads, FAR, 6),
        name="far_attention",
    )(chosen, queries, cot, near_out, near_lse, far)


def near_backward_kernel(queries, cot, keys, values, stats, far_q, grad_q, grad_k, grad_v, keys_t, values_t, sum_k, sum_v):
    keys_t[...] = keys[...].T
    values_t[...] = values[...].T
    sum_k[...] = jnp.zeros_like(sum_k)
    sum_v[...] = jnp.zeros_like(sum_v)
    for piece in (0, 1):
        rows = slice(ROWS * piece, ROWS * piece + ROWS)
        width = ROWS * piece + ROWS
        for g in range(GROUP):
            cols = slice(HD * g, HD * g + HD)
            q = queries[rows, cols]
            c = cot[rows, cols]
            weight = jnp.exp2(near_scores(q, keys_t[:, :width], piece) - stats[rows, 32 * g : 32 * g + 1])
            dweight = dot(c, values_t[:, :width], NN)
            dscore = (weight * (dweight - stats[rows, 32 * g + 16 : 32 * g + 17])).astype(bf16)
            grad_q[rows, cols] = ((far_q[rows, cols] + dot(dscore, keys[:width], NN)) * SCALE).astype(bf16)
            sum_v[:, :width] += dot(c, weight.astype(bf16), TN)
            sum_k[:, :width] += dot(q, dscore, TN)
    grad_k[...] = sum_k[...].T * SCALE
    grad_v[...] = sum_v[...].T


def near_backward(queries, cot, near, stats, far_q):
    heads = stats.shape[1] // HD
    wide = pl.BlockSpec((BLOCK, GROUP * HD), lambda h: (0, h))
    key = pl.BlockSpec((BLOCK, HD), lambda h: (0, h))
    value = pl.BlockSpec((BLOCK, HD), lambda h: (0, HALF + h))
    out_wide = pl.BlockSpec((BLOCK, GROUP * HD), lambda h: (0, h))
    narrow = pl.BlockSpec((BLOCK, HD), lambda h: (0, h))
    return pl.pallas_call(
        near_backward_kernel,
        grid=(heads,),
        in_specs=[wide, wide, key, value, narrow, out_wide],
        out_specs=[out_wide, narrow, narrow],
        out_shape=[jax.ShapeDtypeStruct(far_q.shape, bf16)]
        + [jax.ShapeDtypeStruct((BLOCK, heads * HD), f32)] * 2,
        scratch_shapes=[pltpu.VMEM((HD, BLOCK), bf16)] * 2 + [pltpu.VMEM((HD, BLOCK), f32)] * 2,
        compiler_params=pltpu.CompilerParams(vmem_limit_bytes=60 * 2**20),
        cost_estimate=cost(heads, BLOCK * 3 // 4, 5),
        name="near_backward",
    )(queries, cot, near, near, stats, far_q)


def spread(x):
    return lax.all_to_all(x, "ctx", 0, 0, axis_index_groups=SAME_HALF, tiled=True)


def halves(x, core):
    width = x.shape[1] // 2
    left, right = x[:, :width], x[:, width:]
    return jnp.where(core == 0, left, right), jnp.where(core == 0, right, left)


def swap(x):
    return lax.ppermute(x, "ctx", PAIR)


def in_order(mine, other, core, axis):
    return jnp.where(
        core == 0,
        jnp.concatenate([mine, other], axis=axis),
        jnp.concatenate([other, mine], axis=axis),
    )


def to_block(x, core):
    mine, other = halves(x, core)
    return in_order(mine, swap(other), core, 0)


def others_rows(x, core):
    half = x.shape[0] // 2
    return lax.dynamic_slice_in_dim(x, (1 - core) * half, half, 0)


def my_rows(x, core):
    half = x.shape[0] // 2
    return lax.dynamic_slice_in_dim(x, core * half, half, 0)


def per_device(queries, keys, values, cotangent, selected):
    core = lax.axis_index("ctx") % 2
    my_keys, other_keys = halves(keys, core)
    my_values, other_values = halves(values, core)
    near = in_order(
        jnp.concatenate([my_keys, my_values], axis=1),
        swap(jnp.concatenate([other_keys, other_values], axis=1)),
        core,
        0,
    )
    tiles = jnp.transpose(near.reshape(BLOCKS, 8, 2 * HALF, HD), (0, 2, 1, 3))
    row = jnp.pad(selected.astype(bf16), ((0, 7), (0, HD - selected.shape[1])))
    row = jnp.broadcast_to(row[None, None], (BLOCKS, 1, 8, HD))
    tiles = jnp.concatenate([tiles, row], axis=1)
    shares = spread(tiles)
    block_queries = to_block(queries, core)
    block_cot = to_block(cotangent, core)
    near_out, near_lse = near_forward(block_queries, near)
    shares, near_out, near_lse, block_cot = lax.optimization_barrier(
        (shares, near_out, near_lse, block_cot)
    )
    shares, queries, cotangent = lax.optimization_barrier((shares, queries, cotangent))
    table = shares[:, -1, 0, : 2 * KVH].astype(jnp.int32)
    table = jnp.where(core == 0, table[:, :KVH], table[:, KVH:]).reshape(-1)
    chosen = jnp.where(core == 0, selected[0, :KVH], selected[0, KVH:])
    far = spread(pick(table, shares))
    block_queries = to_block(queries, core)
    block_cot = to_block(cotangent, core)
    near_out, near_lse = near_forward(block_queries, near)
    far, near_out, near_lse, block_cot = lax.optimization_barrier(
        (far, near_out, near_lse, block_cot)
    )
    attended, far_q, stats, grad_far = far_attention(
        chosen, block_queries, block_cot, near_out, near_lse, far
    )
    back = spread(grad_far)
    grad_q, grad_k, grad_v = near_backward(block_queries, block_cot, near, stats, far_q)
    attended, grad_q = lax.optimization_barrier((attended, grad_q))
    near_grad = jnp.concatenate([grad_k, grad_v], axis=1)
    near_other = swap(others_rows(near_grad, core))
    other_attended = swap(others_rows(attended, core))
    other_q = swap(others_rows(grad_q, core))
    back, near_grad, near_other, attended, grad_q, other_attended, other_q = lax.optimization_barrier(
        (back, near_grad, near_other, attended, grad_q, other_attended, other_q)
    )
    summed = spread(add_terms(table, back))
    attended = in_order(my_rows(attended, core), other_attended, core, 1)
    grad_q = in_order(my_rows(grad_q, core), other_q, core, 1)
    summed, attended, grad_q = lax.optimization_barrier((summed, attended, grad_q))
    other = swap(others_rows(summed, core))
    grad_k, grad_v = finish(core, summed, other, (near_grad, near_other))
    return attended, grad_q, grad_k, grad_v


def solution(mesh):
    specs = (P("ctx", None),) * 5
    return jax.shard_map(
        per_device, mesh=mesh, in_specs=specs, out_specs=specs[:4], check_vma=False
    )
```

time: 198 us -> 223 us (1.13)
  starting transfers between devices: 32.7 us -> 66.4 us
  waiting for transfers between devices: 48.4 us -> 31.3 us
  Pallas kernels: 58.2 us -> 65.7 us
  local copies, waits for them, and re-layouts: 2.52 us -> 8.7 us
  other arithmetic: 24.2 us -> 18.5 us
    all_to_all x3, starting transfers between devices: 17.4 us -> 58.5 us  [spread(): lax.all_to_all(x, 'ctx', 0, 0, axis_index_groups=SAME_HALF, tiled=True)]
    all_to_all x3, waiting for transfers between devices: 46.3 us -> 25.6 us  [spread(): lax.all_to_all(x, 'ctx', 0, 0, axis_index_groups=SAME_HALF, tiled=True)]
    ppermute x7, starting transfers between devices: 15.2 us -> 7.92 us  [swap(): return lax.ppermute(x, 'ctx', PAIR)]
    dynamic_slice x0 -> x6, local copies, waits for them, and re-layouts: none -> 6.15 us  [the longest x4 4.61 us: others_rows(): return lax.dynamic_slice_in_dim(x, (1 - core) * half, half, 0)]
    select_n x4 -> x0, other arithmetic: 5.8 us -> none  [from_block(): mine = jnp.where(core == 0, top, bottom)]
    pallas_call x1 -> x4, Pallas kernels: 51.6 us -> 57.1 us  [the longest x1 32 us: far_attention(): pl.pallas_call(far_kernel, grid_spec=pltpu.PrefetchScalarGridSpec(num_sca...]
    select_n x3 -> x4, other arithmetic: 1.54 us -> 6.02 us  [halves(): jnp.where(core == 0, left, right)]
    ppermute x7, waiting for transfers between devices: 2.1 us -> 5.73 us  [swap(): return lax.ppermute(x, 'ctx', PAIR)]
  transfers between devices with their start and end apart: 10 -> 10, of which waited for: 5 -> 7; matrix products, arithmetic and copies ran while one was open for 11% -> 10% of each run, Pallas kernels for 1% -> 12%
where the time goes in v2:
time: 223 us; the launch traced here: 222 us
  starting transfers between devices  66.4 us (30%)
  Pallas kernels  65.7 us (29%)
  waiting for transfers between devices  31.3 us (14%)
  blocking collectives  30.7 us (14%)
  other arithmetic  18.5 us (8%)
  local copies, waits for them, and re-layouts  8.7 us (4%)
    all_to_all x3, starting transfers between devices, spread(): lax.all_to_all(x, 'ctx', 0, 0, axis_index_groups=SAME_HALF, tiled=True)  58.5 us
    pallas_call x1, Pallas kernels, far_attention(): pl.pallas_call(far_kernel, grid_spec=pltpu.PrefetchScalarGridSpec(num_sca...  32 us
    all_to_all x1, blocking collectives, spread(): lax.all_to_all(x, 'ctx', 0, 0, axis_index_groups=SAME_HALF, tiled=True)  30.7 us
    all_to_all x3, waiting for transfers between devices, spread(): lax.all_to_all(x, 'ctx', 0, 0, axis_index_groups=SAME_HALF, tiled=True)  25.6 us
    pallas_call x1, Pallas kernels, near_backward(): pl.pallas_call(near_backward_kernel, grid=(heads,), in_specs=[wide, wide,...  13.3 us
    select_n x4, other arithmetic, in_order(): jnp.where(core == 0, jnp.concatenate([mine, other], axis=axis), jnp.conca...  11.6 us
    pallas_call x1, Pallas kernels, near_forward(): pl.pallas_call(near_forward_kernel, grid=(HALF,), in_specs=[wide, key, va...  10.2 us
    ppermute x7, starting transfers between devices, swap(): return lax.ppermute(x, 'ctx', PAIR)  7.92 us
  transfers between devices with their start and end apart: 10, of which 7 were waited for; matrix products, arithmetic and copies ran while one was open for 10% of the time, Pallas kernels for 12%

profile of v2, /device:TPU:1, one launch (start us, length us, event | category | flops | bytes accessed | tf_op | source)
XLA Modules:
  0.0 222.0 jit_solution(16531368113499495441)
XLA Ops:
  0.6 0.0 copy-start.9
  0.7 1.1 broadcast_select_fusion.7
  1.7 1.1 broadcast_select_fusion.6
  2.8 0.1 pad_maximum_fusion.1
  2.9 1.5 collective-permute-start
  4.4 0.0 copy-done.9
  4.4 1.5 collective-permute-done
  5.9 0.4 maximum_select_fusion.4.keys.values
  6.4 0.0 copy-start.3
  6.4 0.0 copy-start.6
  6.4 0.1 pad_maximum_fusion
  6.5 30.7 %all_to_all.20.shares = bf16[64,9,8,128]{3,2,1,0:T(8,128)(2,1)S(1)} all-to-all(bf16[64,9,8,128]{3,2,1,0:T(8,128)(2,1)S(1)} %pad_maximum_fusion), channel_id=1, replica_groups={{0,2,4,6,8,10,12,14,16,18,20,22,24,26,28,30,32,34,36,38,40,42,44,46,48,..., dimensions={0} | all-to-all | bytes 2359296 | tf_op jit(solution)/shard_map/all_to_all | solution.py:353
  37.2 0.0 copy-done.3
  37.2 0.0 copy-done.6
  37.2 0.0 copy-start.2
  37.2 1.2 broadcast_select_fusion.3
  38.4 1.8 collective-permute-start.1
  40.2 0.0 copy-done.2
  40.3 0.1 slice_select_fusion
  40.4 0.7 reshape.26.table
  41.0 3.9 %pick.1 = bf16[64,4,2,16,128]{4,3,2,1,0:T(8,128)(2,1)} custom-call(s32[512]{0:T(512)} %reshape.26.table, bf16[64,9,8,128]{3,2,1,0:T(8,128)(2,1)} %copy-done.2), custom_call_target="tpu_custom_call" | custom-call | tf_op jit(solution)/shard_map/pick/pallas_call | solution.py:54
  44.9 5.6 %all-to-all-start.1 = ((bf16[64,4,2,16,128]{4,3,2,1,0:T(8,128)(2,1)}), bf16[64,4,2,16,128]{4,3,2,1,0:T(8,128)(2,1)}, u32[]{:S(2)}, u32[]{:S(2)}) async-start(bf16[64,4,2,16,128]{4,3,2,1,0:T(8,128)(2,1)} %pick.1), calls=%async_computation.1 | async-start | bytes 4194304 | tf_op jit(solution)/shard_map/all_to_all | solution.py:353
  50.5 2.7 %broadcast_select_fusion.1 = (bf16[256,2048]{1,0:T(8,128)(2,1)S(1)}, bf16[256,2048]{1,0:T(8,128)(2,1)}) fusion(pred[]{:T(512)S(6)} %eq.4, bf16[256,4096]{1,0:T(8,128)(2,1)} %param.8), kind=kLoop, calls=%fused_computation.7 | loop fusion | flops 1048576 | bytes 4194305 | tf_op jit(solution)/shard_map/jit(_where)/select_n | solution.py:359
  53.2 0.1 collective-permute-start.2
  53.3 0.6 fusion.chosen
  53.9 0.0 collective-permute-done.1
  53.9 2.3 %maximum_select_fusion.queries = bf16[512,2048]{1,0:T(8,128)(2,1)} fusion(bf16[256,2048]{1,0:T(8,128)(2,1)S(1)} %collective-permute-done.1, bf16[256,2048]{1,0:T(8,128)(2,1)S(1)} %get-tuple-element.66, pred[]{:T(512)S(6)} %eq.4), kind=kLoop, calls=%fused_computation | loop fusion | flops 9437184 | bytes 4194305 | tf_op jit(solution)/shard_map/jit(_where)/select_n | solution.py:367
  56.2 0.0 collective-permute-done.2
  56.2 3.8 %maximum_select_fusion.1.cot = bf16[512,2048]{1,0:T(8,128)(2,1)} fusion(bf16[256,2048]{1,0:T(8,128)(2,1)} %collective-permute-done.2, bf16[256,2048]{1,0:T(8,128)(2,1)S(1)} %get-tuple-element.64, pred[]{:T(512)S(6)} %eq.4), kind=kLoop, calls=%fused_computation.1 | loop fusion | flops 9437184 | bytes 4194305 | tf_op jit(solution)/shard_map/jit(_where)/select_n | solution.py:367
  60.0 10.2 %near_forward.2 = (f32[512,2048]{1,0:T(8,128)}, f32[512,512]{1,0:T(8,128)}) custom-call(bf16[512,2048]{1,0:T(8,128)(2,1)} %maximum_select_fusion.queries, bf16[512,1024]{1,0:T(8,128)(2,1)} %copy-done.3, bf16[512,1024]{1,0:T(8,128)(2,1)} %copy-done.3), custom_call_target="tpu_custom_call" | custom-call | flops 3221225472 | bytes 20971520 | tf_op jit(solution)/shard_map/near_forward/pallas_call | solution.py:203
  70.2 9.9 %all-to-all-done.1.far = bf16[64,4,2,16,128]{4,3,2,1,0:T(8,128)(2,1)} async-done(((bf16[64,4,2,16,128]{4,3,2,1,0:T(8,128)(2,1)}), bf16[64,4,2,16,128]{4,3,2,1,0:T(8,128)(2,1)}, u32[]{:S(2)}, u32[]{:S(2)}) %all-to-all-start.1) | async-done | bytes 2097184 | tf_op jit(solution)/shard_map/all_to_all | solution.py:353
  80.0 32.0 %far_attention.1 = (bf16[512,2048]{1,0:T(8,128)(2,1)}, f32[512,2048]{1,0:T(8,128)}, f32[512,512]{1,0:T(8,128)}, bf16[64,4,2,16,128]{4,3,2,1,0:T(8,128)(2,1)}) custom-call(s32[8]{0:T(128)} %fusion.chosen, bf16[512,2048]{1,0:T(8,128)(2,1)} %maximum_select_fusion.queries, bf16[512,2048]{1,0:T(8,128)(2,1)} %maximum_select_fusion.1.cot, ...), custom_call_target="tpu_custom_call" | custom-call | flops 25769803776 | bytes 20971520 | tf_op jit(solution)/shard_map/far_attention/pallas_call | solution.py:288
  112.0 45.5 %all-to-all-start.2 = ((bf16[64,4,2,16,128]{4,3,2,1,0:T(8,128)(2,1)}), bf16[64,4,2,16,128]{4,3,2,1,0:T(8,128)(2,1)}, u32[]{:S(2)}, u32[]{:S(2)}) async-start(bf16[64,4,2,16,128]{4,3,2,1,0:T(8,128)(2,1)} %get-tuple-element.43), calls=%async_computation.2 | async-start | bytes 4194304 | tf_op jit(solution)/shard_map/all_to_all | solution.py:353
  157.5 13.3 %near_backward.1 = (bf16[512,2048]{1,0:T(8,128)(2,1)}, f32[512,512]{1,0:T(8,128)}, f32[512,512]{1,0:T(8,128)}) custom-call(bf16[512,2048]{1,0:T(8,128)(2,1)} %maximum_select_fusion.queries, bf16[512,2048]{1,0:T(8,128)(2,1)} %maximum_select_fusion.1.cot, bf16[512,1024]{1,0:T(8,128)(2,1)} %copy-done.3, bf16[512,1024]{1,0:T(8,128)(2,1)} %copy-done.3, ...), custom_call_target="tpu_custom_call" | custom-call | flops 8053063680 | bytes 20971520 | tf_op jit(solution)/shard_map/near_backward/pallas_call | solution.py:338
  170.8 0.0 copy-start.4
  170.8 0.0 copy-start.8
  170.9 2.5 %constant_dynamic-slice_fusion.3 = bf16[256,2048]{1,0:T(8,128)(2,1)} fusion(bf16[512,2048]{1,0:T(8,128)(2,1)} %get-tuple-element.55, s32[]{:T(128)S(6)} %select_n.145), kind=kLoop, calls=%fused_computation.22 | loop fusion | bytes 2097156 | tf_op jit(solution)/shard_map/dynamic_slice | solution.py:381
  173.3 1.2 collective-permute-start.5
  174.6 0.0 copy-done.4
  174.6 1.0 constant_dynamic-slice_fusion.4
  175.6 0.0 collective-permute-start.4
  175.6 0.0 copy-done.8
  175.6 0.1 constant_dynamic-update-slice_fusion.1
  175.7 0.0 copy-done.7
  175.7 0.1 constant_dynamic-update-slice_fusion.near_mine
  175.8 1.1 constant_dynamic-slice_fusion.5
  176.9 0.5 collective-permute-start.3
  177.4 0.0 collective-permute-done.5
  177.4 1.3 collective-permute-done.4
  178.7 1.4 collective-permute-done.3.near_other
  180.1 5.5 %all-to-all-done.2.terms = bf16[64,4,2,16,128]{4,3,2,1,0:T(8,128)(2,1)} async-done(((bf16[64,4,2,16,128]{4,3,2,1,0:T(8,128)(2,1)}), bf16[64,4,2,16,128]{4,3,2,1,0:T(8,128)(2,1)}, u32[]{:S(2)}, u32[]{:S(2)}) %all-to-all-start.2) | async-done | bytes 2097184 | tf_op jit(solution)/shard_map/all_to_all | solution.py:353
  185.6 4.7 %add_terms.1 = bf16[64,8,8,128]{3,2,1,0:T(8,128)(2,1)} custom-call(s32[512]{0:T(512)} %reshape.26.table, bf16[64,4,2,16,128]{4,3,2,1,0:T(8,128)(2,1)} %all-to-all-done.2.terms), custom_call_target="tpu_custom_call" | custom-call | tf_op jit(solution)/shard_map/add_terms/pallas_call | solution.py:104
  190.3 0.0 copy-done
  190.3 7.4 %all-to-all-start.3 = ((bf16[64,8,8,128]{3,2,1,0:T(8,128)(2,1)}), bf16[64,8,8,128]{3,2,1,0:T(8,128)(2,1)S(1)}, u32[]{:S(2)}, u32[]{:S(2)}) async-start(bf16[64,8,8,128]{3,2,1,0:T(8,128)(2,1)} %add_terms.1), calls=%async_computation.3 | async-start | bytes 2097152 | tf_op jit(solution)/shard_map/all_to_all | solution.py:353
  197.7 0.0 copy-start.5
  197.7 1.5 constant_dynamic-slice_fusion.1
  199.2 0.4 copy-done.5
  199.6 0.1 constant_dynamic-slice_fusion.2
  199.7 5.1 %maximum_select_fusion.2 = (bf16[256,4096]{1,0:T(8,128)(2,1)}, bf16[256,4096]{1,0:T(8,128)(2,1)}) fusion(bf16[256,2048]{1,0:T(8,128)(2,1)} %collective-permute-done.4, bf16[256,2048]{1,0:T(8,128)(2,1)S(1)} %constant_dynamic-slice_fusion.2, pred[]{:T(512)S(6)} %eq.4, bf16[256,2048]{1,0:T(8,128)(2,1)S(1)} %constant_dynamic-slice_fusion.1, ...), kind=kLoop, calls=%fused_computation.2 | loop fusion | flops 18874368 | bytes 8388609 | tf_op jit(solution)/shard_map/jit(_where)/select_n | solution.py:367
  204.7 10.2 %all-to-all-done.3.mine = bf16[64,8,8,128]{3,2,1,0:T(8,128)(2,1)S(1)} async-done(((bf16[64,8,8,128]{3,2,1,0:T(8,128)(2,1)}), bf16[64,8,8,128]{3,2,1,0:T(8,128)(2,1)S(1)}, u32[]{:S(2)}, u32[]{:S(2)}) %all-to-all-start.3) | async-done | bytes 1048608 | tf_op jit(solution)/shard_map/all_to_all | solution.py:353
  215.0 2.7 %collective-permute-start.6 = (bf16[32,8,8,128]{3,2,1,0:T(8,128)(2,1)S(1)}, bf16[32,8,8,128]{3,2,1,0:T(8,128)(2,1)S(1)}, u32[]{:S(2)}, u32[]{:S(2)}) collective-permute-start(bf16[32,8,8,128]{3,2,1,0:T(8,128)(2,1)S(1)} %constant_dynamic-slice_fusion), channel_id=1, source_target_pairs={{0,1},{1,0},{2,3},{3,2},{4,5},{5,4},{6,7},{7,6},{8,9},{9,8},{10,11... | collective-permute-start | bytes 1572872 | tf_op jit(solution)/shard_map/ppermute | solution.py:363
  217.7 1.5 collective-permute-done.6.other
  219.2 1.2 copy-done.1
  220.4 1.6 finish.1
  (8 shorter events, 0.1 us)
Async XLA Ops:
  0.6 3.7 %copy-start.9 = (s32[1,16]{1,0:T(1,128)S(1)}, s32[1,16]{1,0:T(1,128)}, u32[]{:S(2)}) copy-start(s32[1,16]{1,0:T(1,128)} %param.9) | copy-start | bytes 196
  2.9 3.0 %collective-permute-start = (bf16[256,1024]{1,0:T(8,128)(2,1)S(1)}, bf16[256,1024]{1,0:T(8,128)(2,1)S(1)}, u32[]{:S(2)}, u32[]{:S(2)}) collective-permute-start(bf16[256,1024]{1,0:T(8,128)(2,1)S(1)} %pad_maximum_fusion.1), channel_id=1, source_target_pairs={{0,1},{1,0},{2,3},{3,2},{4,5},{5,4},{6,7},{7,6},{8,9},{9,8},{10,11... | collective-permute-start | bytes 1572872 | tf_op jit(solution)/shard_map/ppermute | solution.py:363
  6.4 30.8 %copy-start.3 = (bf16[512,1024]{1,0:T(8,128)(2,1)}, bf16[512,1024]{1,0:T(8,128)(2,1)S(1)}, u32[]{:S(2)}) copy-start(bf16[512,1024]{1,0:T(8,128)(2,1)S(1)} %maximum_select_fusion.4.keys.values) | copy-start | bytes 3145732
  6.4 30.8 %copy-start.6 = (bf16[256,4096]{1,0:T(8,128)(2,1)S(1)}, bf16[256,4096]{1,0:T(8,128)(2,1)}, u32[]{:S(2)}) copy-start(bf16[256,4096]{1,0:T(8,128)(2,1)} %param.5) | copy-start | bytes 6291460
  37.2 3.0 %copy-start.2 = (bf16[64,9,8,128]{3,2,1,0:T(8,128)(2,1)}, bf16[64,9,8,128]{3,2,1,0:T(8,128)(2,1)S(1)}, u32[]{:S(2)}) copy-start(bf16[64,9,8,128]{3,2,1,0:T(8,128)(2,1)S(1)} %all_to_all.20.shares) | copy-start | bytes 3538948
  38.4 15.5 %collective-permute-start.1 = (bf16[256,2048]{1,0:T(8,128)(2,1)}, bf16[256,2048]{1,0:T(8,128)(2,1)S(1)}, u32[]{:S(2)}, u32[]{:S(2)}) collective-permute-start(bf16[256,2048]{1,0:T(8,128)(2,1)} %get-tuple-element.67), channel_id=1, source_target_pairs={{0,1},{1,0},{2,3},{3,2},{4,5},{5,4},{6,7},{7,6},{8,9},{9,8},{10,11... | collective-permute-start | bytes 3145736 | tf_op jit(solution)/shard_map/ppermute | solution.py:363
  44.9 35.1 %all-to-all-start.1 = ((bf16[64,4,2,16,128]{4,3,2,1,0:T(8,128)(2,1)}), bf16[64,4,2,16,128]{4,3,2,1,0:T(8,128)(2,1)}, u32[]{:S(2)}, u32[]{:S(2)}) async-start(bf16[64,4,2,16,128]{4,3,2,1,0:T(8,128)(2,1)} %pick.1), calls=%async_computation.1 | async-start | bytes 4194304 | tf_op jit(solution)/shard_map/all_to_all | solution.py:353
  53.2 3.1 %collective-permute-start.2 = (bf16[256,2048]{1,0:T(8,128)(2,1)}, bf16[256,2048]{1,0:T(8,128)(2,1)}, u32[]{:S(2)}, u32[]{:S(2)}) collective-permute-start(bf16[256,2048]{1,0:T(8,128)(2,1)} %get-tuple-element.65), channel_id=1, source_target_pairs={{0,1},{1,0},{2,3},{3,2},{4,5},{5,4},{6,7},{7,6},{8,9},{9,8},{10,11... | collective-permute-start | bytes 3145736 | tf_op jit(solution)/shard_map/ppermute | solution.py:363
  112.0 73.5 %all-to-all-start.2 = ((bf16[64,4,2,16,128]{4,3,2,1,0:T(8,128)(2,1)}), bf16[64,4,2,16,128]{4,3,2,1,0:T(8,128)(2,1)}, u32[]{:S(2)}, u32[]{:S(2)}) async-start(bf16[64,4,2,16,128]{4,3,2,1,0:T(8,128)(2,1)} %get-tuple-element.43), calls=%async_computation.2 | async-start | bytes 4194304 | tf_op jit(solution)/shard_map/all_to_all | solution.py:353
  170.8 3.7 %copy-start.4 = (bf16[512,2048]{1,0:T(8,128)(2,1)S(1)}, bf16[512,2048]{1,0:T(8,128)(2,1)}, u32[]{:S(2)}) copy-start(bf16[512,2048]{1,0:T(8,128)(2,1)} %get-tuple-element.53) | copy-start | bytes 6291460
  170.8 4.8 %copy-start.8 = (f32[512,512]{1,0:T(8,128)S(1)}, f32[512,512]{1,0:T(8,128)}, u32[]{:S(2)}) copy-start(f32[512,512]{1,0:T(8,128)} %get-tuple-element.46) | copy-start | bytes 3145732
  173.3 2.4 %copy-start.7 = (f32[512,512]{1,0:T(8,128)S(1)}, f32[512,512]{1,0:T(8,128)}, u32[]{:S(2)}) copy-start(f32[512,512]{1,0:T(8,128)} %get-tuple-element.47) | copy-start | bytes 3145732
  173.3 4.1 %collective-permute-start.5 = (bf16[256,2048]{1,0:T(8,128)(2,1)}, bf16[256,2048]{1,0:T(8,128)(2,1)}, u32[]{:S(2)}, u32[]{:S(2)}) collective-permute-start(bf16[256,2048]{1,0:T(8,128)(2,1)} %constant_dynamic-slice_fusion.3), channel_id=1, source_target_pairs={{0,1},{1,0},{2,3},{3,2},{4,5},{5,4},{6,7},{7,6},{8,9},{9,8},{10,11... | collective-permute-start | bytes 3145736 | tf_op jit(solution)/shard_map/ppermute | solution.py:363
  175.6 3.1 %collective-permute-start.4 = (bf16[256,2048]{1,0:T(8,128)(2,1)}, bf16[256,2048]{1,0:T(8,128)(2,1)}, u32[]{:S(2)}, u32[]{:S(2)}) collective-permute-start(bf16[256,2048]{1,0:T(8,128)(2,1)} %constant_dynamic-slice_fusion.4), channel_id=1, source_target_pairs={{0,1},{1,0},{2,3},{3,2},{4,5},{5,4},{6,7},{7,6},{8,9},{9,8},{10,11... | collective-permute-start | bytes 3145736 | tf_op jit(solution)/shard_map/ppermute | solution.py:363
  176.9 3.2 %collective-permute-start.3 = (f32[256,1024]{1,0:T(8,128)}, f32[256,1024]{1,0:T(8,128)S(1)}, u32[]{:S(2)}, u32[]{:S(2)}) collective-permute-start(f32[256,1024]{1,0:T(8,128)} %constant_dynamic-slice_fusion.5), channel_id=1, source_target_pairs={{0,1},{1,0},{2,3},{3,2},{4,5},{5,4},{6,7},{7,6},{8,9},{9,8},{10,11... | collective-permute-start | bytes 3145736 | tf_op jit(solution)/shard_map/ppermute | solution.py:363
  180.1 10.2 %copy-start = (f32[256,1024]{1,0:T(8,128)}, f32[256,1024]{1,0:T(8,128)S(1)}, u32[]{:S(2)}) copy-start(f32[256,1024]{1,0:T(8,128)S(1)} %collective-permute-done.3.near_other) | copy-start | bytes 3145732
  190.3 24.6 %all-to-all-start.3 = ((bf16[64,8,8,128]{3,2,1,0:T(8,128)(2,1)}), bf16[64,8,8,128]{3,2,1,0:T(8,128)(2,1)S(1)}, u32[]{:S(2)}, u32[]{:S(2)}) async-start(bf16[64,8,8,128]{3,2,1,0:T(8,128)(2,1)} %add_terms.1), calls=%async_computation.3 | async-start | bytes 2097152 | tf_op jit(solution)/shard_map/all_to_all | solution.py:353
  197.7 1.9 copy-start.5
  215.0 4.2 %collective-permute-start.6 = (bf16[32,8,8,128]{3,2,1,0:T(8,128)(2,1)S(1)}, bf16[32,8,8,128]{3,2,1,0:T(8,128)(2,1)S(1)}, u32[]{:S(2)}, u32[]{:S(2)}) collective-permute-start(bf16[32,8,8,128]{3,2,1,0:T(8,128)(2,1)S(1)} %constant_dynamic-slice_fusion), channel_id=1, source_target_pairs={{0,1},{1,0},{2,3},{3,2},{4,5},{5,4},{6,7},{7,6},{8,9},{9,8},{10,11... | collective-permute-start | bytes 1572872 | tf_op jit(solution)/shard_map/ppermute | solution.py:363
  219.2 1.2 copy-start.1

commit v3 on v2

v3 whole, which is shorter than its diff:
```python
import math

import jax
import jax.numpy as jnp
from jax import lax
from jax.experimental import pallas as pl
from jax.experimental.pallas import tpu as pltpu
from jax.sharding import PartitionSpec as P

HD = 128
QH = 32
KVH = 8
BLOCK = 512
ROWS = 256
BLOCKS = 64
HALF = KVH // 2
GROUP = QH // KVH
FAR = 2 * BLOCK
SCALE = HD ** -0.5
SCALE_LOG2 = SCALE * math.log2(math.e)
NN = (((1,), (0,)), ((), ()))
NT = (((1,), (1,)), ((), ()))
TN = (((0,), (0,)), ((), ()))
f32 = jnp.float32
bf16 = jnp.bfloat16
LIMIT = 2.0**40

PAIR = [(i, i ^ 1) for i in range(2 * BLOCKS)]
SAME_HALF = [list(range(k, 2 * BLOCKS, 2)) for k in (0, 1)]


def pick_kernel(table, shares, out):
    step = pl.program_id(0)
    count, heads = out.shape[:2]

    def one(i, carry):
        row = (step * count + i) * 2 * heads
        for h in range(heads):
            first = jnp.maximum(table[row + 2 * h], 0)
            second = jnp.maximum(table[row + 2 * h + 1], 0)
            for kv in range(2):
                tile = kv * HALF + h
                out[i, h, kv, :8] = shares[first, tile]
                out[i, h, kv, 8:] = shares[second, tile]
        return carry

    lax.fori_loop(0, count, one, 0, unroll=8)


def pick(table, shares):
    count = 32
    return pl.pallas_call(
        pick_kernel,
        grid_spec=pltpu.PrefetchScalarGridSpec(
            num_scalar_prefetch=1,
            grid=(BLOCKS // count,),
            in_specs=[pl.BlockSpec(shares.shape, lambda i, t: (0, 0, 0, 0))],
            out_specs=pl.BlockSpec((count, HALF, 2, 16, HD), lambda i, t: (i, 0, 0, 0, 0)),
        ),
        out_shape=jax.ShapeDtypeStruct((BLOCKS, HALF, 2, 16, HD), bf16),
        compiler_params=pltpu.CompilerParams(vmem_limit_bytes=16 * 2**20),
        name="pick",
    )(table, shares)


def add_kernel(table, terms, out, total):
    step = pl.program_id(0)
    count, heads = terms.shape[:2]

    @pl.when(step == 0)
    def _():
        total[...] = jnp.zeros_like(total)

    def one(i, carry):
        row = (step * count + i) * 2 * heads
        places = []
        sums = []
        for h in range(heads):
            for e in range(2):
                block = table[row + 2 * h + e]
                slot = jnp.where(block < 0, BLOCKS, block)
                for kv in range(2):
                    place = (slot, kv * heads + h)
                    term = terms[i, h, kv].astype(f32)[8 * e : 8 * e + 8]
                    places.append(place)
                    sums.append(total[place] + term)
        for place, value in zip(places, sums):
            total[place] = value
        return carry

    lax.fori_loop(0, count, one, 0, unroll=8)

    @pl.when(step == pl.num_programs(0) - 1)
    def _():
        out[...] = total[:BLOCKS].astype(bf16)


def add_terms(table, terms):
    count = 16
    tiles = 2 * terms.shape[1]
    whole = lambda i, t: (0, 0, 0, 0)
    return pl.pallas_call(
        add_kernel,
        grid_spec=pltpu.PrefetchScalarGridSpec(
            num_scalar_prefetch=1,
            grid=(BLOCKS // count,),
            in_specs=[pl.BlockSpec((count,) + terms.shape[1:], lambda i, t: (i, 0, 0, 0, 0))],
            out_specs=pl.BlockSpec((BLOCKS, tiles, 8, HD), whole),
            scratch_shapes=[pltpu.VMEM((BLOCKS + 1, tiles, 8, HD), f32)],
        ),
        out_shape=jax.ShapeDtypeStruct((BLOCKS, tiles, 8, HD), bf16),
        compiler_params=pltpu.CompilerParams(vmem_limit_bytes=16 * 2**20),
        name="add_terms",
    )(table, terms)


def finish_kernel(core, mine, other, near_k, near_v, near_other, grad_k, grad_v):
    rows = grad_k.shape[0]
    for side, far in ((core[0], mine), (1 - core[0], other)):
        for kv, (out, near) in enumerate(((grad_k, near_k), (grad_v, near_v))):
            for h in range(HALF):
                tile = kv * HALF + h
                term = far[:, tile].reshape(rows, HD).astype(f32)
                if far is mine:
                    term += near[:, HD * h : HD * h + HD]
                else:
                    term += near_other[:, HD * tile : HD * tile + HD].astype(f32)
                place = pl.ds(pl.multiple_of((side * HALF + h) * HD, HD), HD)
                out[:, place] = term.astype(bf16)


def finish(core, mine, other, near_k, near_v, near_other):
    steps = 4
    tiles = mine.shape[1]
    chunk = ROWS // 8 // steps
    far = pl.BlockSpec((chunk, tiles, 8, HD), lambda i, c: (i, 0, 0, 0))
    far_mine = pl.BlockSpec((chunk, tiles, 8, HD), lambda i, c: (i + steps * c[0], 0, 0, 0))
    rows = pl.BlockSpec((ROWS // steps, KVH * HD), lambda i, c: (i, 0))
    rows_mine = pl.BlockSpec((ROWS // steps, HALF * HD), lambda i, c: (i + steps * c[0], 0))
    return pl.pallas_call(
        finish_kernel,
        grid_spec=pltpu.PrefetchScalarGridSpec(
            num_scalar_prefetch=1,
            grid=(steps,),
            in_specs=[far_mine, far, rows_mine, rows_mine, rows],
            out_specs=[rows, rows],
        ),
        out_shape=[jax.ShapeDtypeStruct((ROWS, KVH * HD), bf16)] * 2,
        compiler_params=pltpu.CompilerParams(vmem_limit_bytes=12 * 2**20),
        name="finish",
    )(core.reshape(1), mine, other, near_k, near_v, near_other)


def dot(a, b, dims):
    return lax.dot_general(a, b, dims, preferred_element_type=f32)


def cost(heads, keys, products):
    pairs = heads * GROUP * BLOCK * keys
    return pl.CostEstimate(
        flops=products * 4 * pairs * HD, transcendentals=pairs, bytes_accessed=heads * 5 * 2**20
    )


def lanes(values):
    each = HD // len(values)
    lane = lax.broadcasted_iota(jnp.int32, (ROWS, HD), 1)
    out = jnp.broadcast_to(values[-1], (ROWS, HD))
    for i in range(len(values) - 2, -1, -1):
        out = jnp.where(lane < (i + 1) * each, values[i], out)
    return out


def near_scores(q, keys_t, piece):
    score = dot(q, keys_t, NN) * SCALE_LOG2
    shape = (ROWS, ROWS)
    causal = lax.broadcasted_iota(jnp.int32, shape, 0) >= lax.broadcasted_iota(jnp.int32, shape, 1)
    diagonal = jnp.where(causal, score[:, ROWS * piece :], -1e30)
    return jnp.concatenate([score[:, :ROWS], diagonal], axis=1) if piece else diagonal


def near_forward_kernel(queries, cot, keys, values, out_t, lse_t, cot_t, keys_t):
    keys_t[...] = keys[...].T
    cot_t[...] = cot[...].T
    for piece in (0, 1):
        rows = slice(ROWS * piece, ROWS * piece + ROWS)
        width = ROWS * piece + ROWS
        found = []
        for g in range(GROUP):
            cols = slice(HD * g, HD * g + HD)
            score = near_scores(queries[rows, cols], keys_t[:, :width], piece)
            top = jnp.max(score, axis=1, keepdims=True)
            raised = jnp.exp2(score - top)
            total = jnp.sum(raised, axis=1, keepdims=True)
            out = dot(raised.astype(bf16), values[:width], NN) * (1.0 / total)
            out_t[cols, rows] = out.T
            found.append(top + jnp.log2(total))
        lse = lanes(found).T
        for g in range(GROUP):
            lse_t[g : g + 1, rows] = lse[HD // GROUP * g : HD // GROUP * g + 1]


def near_forward(queries, cot, near):
    wide = pl.BlockSpec((BLOCK, GROUP * HD), lambda h: (0, h))
    key = pl.BlockSpec((BLOCK, HD), lambda h: (0, h))
    value = pl.BlockSpec((BLOCK, HD), lambda h: (0, HALF + h))
    tall = pl.BlockSpec((GROUP * HD, BLOCK), lambda h: (h, 0))
    return pl.pallas_call(
        near_forward_kernel,
        grid=(HALF,),
        in_specs=[wide, wide, key, value],
        out_specs=[tall, pl.BlockSpec((8, BLOCK), lambda h: (h, 0)), tall],
        out_shape=[
            jax.ShapeDtypeStruct(queries.shape[::-1], f32),
            jax.ShapeDtypeStruct((HALF * 8, BLOCK), f32),
            jax.ShapeDtypeStruct(queries.shape[::-1], bf16),
        ],
        scratch_shapes=[pltpu.VMEM((HD, BLOCK), bf16)],
        compiler_params=pltpu.CompilerParams(vmem_limit_bytes=60 * 2**20),
        cost_estimate=cost(HALF, BLOCK * 3 // 4, 2),
        name="near_forward",
    )(queries, cot, near, near)


def far_kernel(
    chosen, queries, cot_t, near_t, lse_t, far, att_t, grad_t, stats, grad_far, keys_t, values_t, sum_k, sum_v
):
    h = pl.program_id(0)
    first = chosen[2 * h]
    second = chosen[2 * h + 1]
    keys_t[...] = far[:, 0, 0].reshape(FAR, HD).T
    values_t[...] = far[:, 0, 1].reshape(FAR, HD).T

    def one(g, masked, general):
        k = far[:, 0, 0].reshape(FAR, HD)
        v = far[:, 0, 1].reshape(FAR, HD)
        cols = pl.ds(g * HD if isinstance(g, int) else pl.multiple_of(g * HD, HD), HD)
        q = queries[:, cols]
        l0 = lse_t[pl.ds(g, 1), :]
        score = dot(k, q, NT) * SCALE_LOG2
        if masked:
            row = lax.broadcasted_iota(jnp.int32, score.shape, 0)
            entry = jnp.where(jnp.bitwise_and(row, 8) == 0, first, second)
            score = jnp.where(entry < 0, -1e30, score)
        top = jnp.maximum(jnp.max(score, axis=0, keepdims=True), l0) if general else l0
        raised = jnp.exp2(score - top)
        near = jnp.exp2(l0 - top) if general else 1.0
        total = jnp.sum(raised, axis=0, keepdims=True) + near
        over = 1.0 / total
        raised_b = raised.astype(bf16)
        out = (dot(values_t[...], raised_b, NN) + near * near_t[cols, :]) * over
        att_t[cols, :] = out.astype(bf16)
        cot_over = (cot_t[cols, :].astype(f32) * over).astype(bf16)
        delta = jnp.sum(cot_over.astype(f32) * out, axis=0, keepdims=True)
        dscore = (raised * (dot(v, cot_over, NN) - delta)).astype(bf16)
        grad_t[cols, :] = dot(keys_t[...], dscore, NN)
        sum_v[...] += dot(raised_b, cot_over, NT)
        sum_k[...] += dot(dscore, q, NN)
        stats[pl.ds(g, 1), :] = top + jnp.log2(total)
        stats[pl.ds(GROUP + g, 1), :] = delta * total
        return total

    def run(masked):
        worst = jnp.zeros((1, BLOCK), f32)
        for g in range(GROUP):
            worst = jnp.maximum(worst, one(g, masked, False))
        return jnp.max(worst)

    def clear():
        sum_k[...] = jnp.zeros_like(sum_k)
        sum_v[...] = jnp.zeros_like(sum_v)

    clear()
    alive = jnp.minimum(first, second) >= 0
    worst = lax.cond(alive, lambda: run(False), lambda: run(True))

    @pl.when(jnp.logical_not(worst <= LIMIT))
    def _():
        def again(g, carry):
            one(g, True, True)
            return carry

        clear()
        lax.fori_loop(0, GROUP, again, 0)

    grad_far[:, 0, 0] = (sum_k[...] * SCALE).astype(bf16).reshape(BLOCKS, 16, HD)
    grad_far[:, 0, 1] = sum_v[...].astype(bf16).reshape(BLOCKS, 16, HD)


def far_attention(chosen, queries, cot_t, near_t, lse_t, far):
    wide = pl.BlockSpec((BLOCK, GROUP * HD), lambda h, c: (0, h))
    tall = pl.BlockSpec((GROUP * HD, BLOCK), lambda h, c: (h, 0))
    rows = pl.BlockSpec((8, BLOCK), lambda h, c: (h, 0))
    gated = pl.BlockSpec((BLOCKS, 1, 2, 16, HD), lambda h, c: (0, h, 0, 0, 0))
    return pl.pallas_call(
        far_kernel,
        grid_spec=pltpu.PrefetchScalarGridSpec(
            num_scalar_prefetch=1,
            grid=(HALF,),
            in_specs=[wide, tall, tall, rows, gated],
            out_specs=[tall, tall, rows, gated],
            scratch_shapes=[pltpu.VMEM((HD, FAR), bf16)] * 2 + [pltpu.VMEM((FAR, HD), f32)] * 2,
        ),
        out_shape=[
            jax.ShapeDtypeStruct(cot_t.shape, bf16),
            jax.ShapeDtypeStruct(cot_t.shape, f32),
            jax.ShapeDtypeStruct(lse_t.shape, f32),
            jax.ShapeDtypeStruct(far.shape, bf16),
        ],
        compiler_params=pltpu.CompilerParams(vmem_limit_bytes=60 * 2**20),
        cost_estimate=cost(HALF, FAR, 6),
        name="far_attention",
    )(chosen, queries, cot_t, near_t, lse_t, far)


def near_backward_kernel(
    queries, cot, keys, values, stats, att_t, far_t, att, grad_q, grad_k, grad_v, keys_t, values_t, sum_k, sum_v
):
    keys_t[...] = keys[...].T
    values_t[...] = values[...].T
    att[...] = att_t[...].T
    sum_k[...] = jnp.zeros_like(sum_k)
    sum_v[...] = jnp.zeros_like(sum_v)
    columns = stats[...].T
    for piece in (0, 1):
        rows = slice(ROWS * piece, ROWS * piece + ROWS)
        width = ROWS * piece + ROWS
        for g in range(GROUP):
            cols = slice(HD * g, HD * g + HD)
            q = queries[rows, cols]
            c = cot[rows, cols]
            score = near_scores(q, keys_t[:, :width], piece)
            weight = jnp.exp2(score - columns[rows, g : g + 1])
            dweight = dot(c, values_t[:, :width], NN)
            dscore = (weight * (dweight - columns[rows, GROUP + g : GROUP + g + 1])).astype(bf16)
            grad = far_t[cols, rows].T + dot(dscore, keys[:width], NN)
            grad_q[rows, cols] = (grad * SCALE).astype(bf16)
            sum_v[:, :width] += dot(c, weight.astype(bf16), TN)
            sum_k[:, :width] += dot(q, dscore, TN)
    grad_k[...] = sum_k[...].T * SCALE
    grad_v[...] = sum_v[...].T


def near_backward(queries, cot, near, stats, att_t, far_t):
    wide = pl.BlockSpec((BLOCK, GROUP * HD), lambda h: (0, h))
    tall = pl.BlockSpec((GROUP * HD, BLOCK), lambda h: (h, 0))
    key = pl.BlockSpec((BLOCK, HD), lambda h: (0, h))
    value = pl.BlockSpec((BLOCK, HD), lambda h: (0, HALF + h))
    return pl.pallas_call(
        near_backward_kernel,
        grid=(HALF,),
        in_specs=[wide, wide, key, value, pl.BlockSpec((8, BLOCK), lambda h: (h, 0)), tall, tall],
        out_specs=[wide, wide, key, key],
        out_shape=[jax.ShapeDtypeStruct(queries.shape, bf16)] * 2
        + [jax.ShapeDtypeStruct((BLOCK, HALF * HD), f32)] * 2,
        scratch_shapes=[pltpu.VMEM((HD, BLOCK), bf16)] * 2 + [pltpu.VMEM((HD, BLOCK), f32)] * 2,
        compiler_params=pltpu.CompilerParams(vmem_limit_bytes=58 * 2**20),
        cost_estimate=cost(HALF, BLOCK * 3 // 4, 5),
        name="near_backward",
    )(queries, cot, near, near, stats, att_t, far_t)


def spread(x):
    return lax.all_to_all(x, "ctx", 0, 0, axis_index_groups=SAME_HALF, tiled=True)


def halves(x, core):
    width = x.shape[1] // 2
    mine = lax.dynamic_slice_in_dim(x, core * width, width, 1)
    return mine, lax.dynamic_slice_in_dim(x, (1 - core) * width, width, 1)


def swap(x):
    return lax.ppermute(x, "ctx", PAIR)


def in_order(mine, other, core, axis):
    return jnp.where(
        core == 0,
        jnp.concatenate([mine, other], axis=axis),
        jnp.concatenate([other, mine], axis=axis),
    )


def to_block(x, core):
    mine, other = halves(x, core)
    return in_order(mine, swap(other), core, 0)


def others_rows(x, core):
    half = x.shape[0] // 2
    return lax.dynamic_slice_in_dim(x, (1 - core) * half, half, 0)


def my_rows(x, core):
    half = x.shape[0] // 2
    return lax.dynamic_slice_in_dim(x, core * half, half, 0)


def per_device(queries, keys, values, cotangent, selected):
    core = lax.axis_index("ctx") % 2
    my_keys, other_keys = halves(keys, core)
    my_values, other_values = halves(values, core)
    near = in_order(
        jnp.concatenate([my_keys, my_values], axis=1),
        swap(jnp.concatenate([other_keys, other_values], axis=1)),
        core,
        0,
    )
    tiles = jnp.transpose(near.reshape(BLOCKS, 8, 2 * HALF, HD), (0, 2, 1, 3))
    row = jnp.pad(selected.astype(bf16), ((0, 7), (0, HD - selected.shape[1])))
    row = jnp.broadcast_to(row[None, None], (BLOCKS, 1, 8, HD))
    tiles = jnp.concatenate([tiles, row], axis=1)
    shares = spread(tiles)
    table = shares[:, -1, 0, : 2 * KVH].astype(jnp.int32)
    table = jnp.where(core == 0, table[:, :KVH], table[:, KVH:]).reshape(-1)
    chosen = jnp.where(core == 0, selected[0, :KVH], selected[0, KVH:])
    picked = pick(table, shares)
    picked, queries, cotangent = lax.optimization_barrier((picked, queries, cotangent))
    far = spread(picked)
    block_queries = to_block(queries, core)
    block_cot = to_block(cotangent, core)
    near_t, lse_t, cot_t = near_forward(block_queries, block_cot, near)
    far, near_t, lse_t, cot_t = lax.optimization_barrier((far, near_t, lse_t, cot_t))
    att_t, far_t, stats, grad_far = far_attention(
        chosen, block_queries, cot_t, near_t, lse_t, far
    )
    back = spread(grad_far)
    attended, grad_q, grad_k, grad_v = near_backward(
        block_queries, block_cot, near, stats, att_t, far_t
    )
    near_other = swap(
        jnp.concatenate([others_rows(x, core).astype(bf16) for x in (grad_k, grad_v)], axis=1)
    )
    other_attended = swap(others_rows(attended, core))
    other_q = swap(others_rows(grad_q, core))
    back, grad_k, grad_v, near_other, attended, grad_q, other_attended, other_q = (
        lax.optimization_barrier(
            (back, grad_k, grad_v, near_other, attended, grad_q, other_attended, other_q)
        )
    )
    summed = spread(add_terms(table, back))
    attended = in_order(my_rows(attended, core), other_attended, core, 1)
    grad_q = in_order(my_rows(grad_q, core), other_q, core, 1)
    summed, attended, grad_q = lax.optimization_barrier((summed, attended, grad_q))
    other = swap(others_rows(summed, core))
    grad_k, grad_v = finish(core, summed, other, grad_k, grad_v, near_other)
    return attended, grad_q, grad_k, grad_v


def solution(mesh):
    specs = (P("ctx", None),) * 5
    return jax.shard_map(
        per_device, mesh=mesh, in_specs=specs, out_specs=specs[:4], check_vma=False
    )
```

time: 223 us -> 207 us (0.928)
  blocking collectives: 30.7 us -> 0 us
  waiting for transfers between devices: 31.3 us -> 41.9 us
  local copies, waits for them, and re-layouts: 8.7 us -> 12.1 us
  starting transfers between devices: 66.4 us -> 69.1 us
    all_to_all x1 -> x0, blocking collectives: 30.7 us -> none  [spread(): lax.all_to_all(x, 'ctx', 0, 0, axis_index_groups=SAME_HALF, tiled=True)]
    all_to_all x3 -> x4, waiting for transfers between devices: 25.6 us -> 36.2 us  [spread(): lax.all_to_all(x, 'ctx', 0, 0, axis_index_groups=SAME_HALF, tiled=True)]
    select_n x4 -> x0, other arithmetic: 6.02 us -> none  [halves(): jnp.where(core == 0, left, right)]
    dynamic_slice x0 -> x3, local copies, waits for them, and re-layouts: none -> 5.28 us  [halves(): mine = lax.dynamic_slice_in_dim(x, core * width, width, 1)]
    all_to_all x3 -> x4, starting transfers between devices: 58.5 us -> 62.1 us  [spread(): lax.all_to_all(x, 'ctx', 0, 0, axis_index_groups=SAME_HALF, tiled=True)]
    select_n x4 -> x5, other arithmetic: 11.6 us -> 14.1 us  [in_order(): jnp.where(core == 0, jnp.concatenate([mine, other], axis=axis), jnp.conca...]
    pallas_call x2, Pallas kernels: 23.5 us -> 25.9 us  [the longest x1 13.9 us: near_backward(): pl.pallas_call(near_backward_kernel, grid=(HALF,), in_specs=[wide, wide,...]
    dynamic_slice x4 -> x3, local copies, waits for them, and re-layouts: 4.61 us -> 3.53 us  [others_rows(): return lax.dynamic_slice_in_dim(x, (1 - core) * half, half, 0)]
  transfers between devices with their start and end apart: 10 -> 11, of which waited for: 7 -> 8; matrix products, arithmetic and copies ran while one was open for 10% -> 12% of each run, Pallas kernels for 12% -> 13%
where the time goes in v3:
time: 207 us
  starting transfers between devices  69.1 us (33%)
  Pallas kernels  65.7 us (32%)
  waiting for transfers between devices  41.9 us (20%)
  other arithmetic  16.9 us (8%)
  local copies, waits for them, and re-layouts  12.1 us (6%)
    all_to_all x4, starting transfers between devices, spread(): lax.all_to_all(x, 'ctx', 0, 0, axis_index_groups=SAME_HALF, tiled=True)  62.1 us
    all_to_all x4, waiting for transfers between devices, spread(): lax.all_to_all(x, 'ctx', 0, 0, axis_index_groups=SAME_HALF, tiled=True)  36.2 us
    pallas_call x1, Pallas kernels, far_attention(): pl.pallas_call(far_kernel, grid_spec=pltpu.PrefetchScalarGridSpec(num_sca...  31.1 us
    select_n x5, other arithmetic, in_order(): jnp.where(core == 0, jnp.concatenate([mine, other], axis=axis), jnp.conca...  14.1 us
    pallas_call x1, Pallas kernels, near_backward(): pl.pallas_call(near_backward_kernel, grid=(HALF,), in_specs=[wide, wide,...  13.9 us
    pallas_call x1, Pallas kernels, near_forward(): pl.pallas_call(near_forward_kernel, grid=(HALF,), in_specs=[wide, wide, k...  12 us
    ppermute x7, starting transfers between devices, swap(): return lax.ppermute(x, 'ctx', PAIR)  7.01 us
    ppermute x7, waiting for transfers between devices, swap(): return lax.ppermute(x, 'ctx', PAIR)  5.72 us
  transfers between devices with their start and end apart: 11, of which 8 were waited for; matrix products, arithmetic and copies ran while one was open for 12% of the time, Pallas kernels for 13%

profile of v3, /device:TPU:1, one launch (start us, length us, event | category | flops | bytes accessed | tf_op | source)
XLA Modules:
  0.0 206.6 jit_solution(17858158095284244743)
XLA Ops:
  0.6 0.0 copy-start.6
  0.7 1.3 constant_dynamic-slice_fusion.11
  1.9 0.1 pad_maximum_fusion.1
  2.0 1.5 collective-permute-start
  3.5 0.0 copy-done.6
  3.5 1.5 collective-permute-done
  5.0 0.4 maximum_select_fusion.4.keys.values
  5.5 0.0 copy-start.2
  5.5 1.2 pad_maximum_fusion
  6.8 0.1 copy-done.2
  6.9 11.2 %all-to-all-start = ((bf16[64,9,8,128]{3,2,1,0:T(8,128)(2,1)}), bf16[64,9,8,128]{3,2,1,0:T(8,128)(2,1)S(1)}, u32[]{:S(2)}, u32[]{:S(2)}) async-start(bf16[64,9,8,128]{3,2,1,0:T(8,128)(2,1)} %pad_maximum_fusion), calls=%async_computation | async-start | bytes 2359296 | tf_op jit(solution)/shard_map/all_to_all | solution.py:364
  18.1 19.4 %all-to-all-done.shares = bf16[64,9,8,128]{3,2,1,0:T(8,128)(2,1)S(1)} async-done(((bf16[64,9,8,128]{3,2,1,0:T(8,128)(2,1)}), bf16[64,9,8,128]{3,2,1,0:T(8,128)(2,1)S(1)}, u32[]{:S(2)}, u32[]{:S(2)}) %all-to-all-start) | async-done | bytes 1179680 | tf_op jit(solution)/shard_map/all_to_all | solution.py:364
  37.6 0.1 slice_select_fusion
  37.6 0.1 reshape.26.table
  37.7 2.5 %pick.1 = bf16[64,4,2,16,128]{4,3,2,1,0:T(8,128)(2,1)} custom-call(s32[512]{0:T(512)S(1)} %reshape.26.table, bf16[64,9,8,128]{3,2,1,0:T(8,128)(2,1)S(1)} %all-to-all-done.shares), custom_call_target="tpu_custom_call" | custom-call | tf_op jit(solution)/shard_map/pick/pallas_call | solution.py:52
  40.2 5.6 %all-to-all-start.1 = ((bf16[64,4,2,16,128]{4,3,2,1,0:T(8,128)(2,1)}), bf16[64,4,2,16,128]{4,3,2,1,0:T(8,128)(2,1)}, u32[]{:S(2)}, u32[]{:S(2)}) async-start(bf16[64,4,2,16,128]{4,3,2,1,0:T(8,128)(2,1)} %pick.1), calls=%async_computation.1 | async-start | bytes 4194304 | tf_op jit(solution)/shard_map/all_to_all | solution.py:364
  45.8 0.0 copy-start.3
  45.8 2.9 %constant_dynamic-slice_fusion.6 = (bf16[256,2048]{1,0:T(8,128)(2,1)S(1)}, bf16[256,2048]{1,0:T(8,128)(2,1)}) fusion(bf16[256,4096]{1,0:T(8,128)(2,1)} %param.8, s32[]{:T(128)S(6)} %select_n.100, s32[]{:T(128)S(6)} %select_n.101), kind=kLoop, calls=%fused_computation.18 | loop fusion | bytes 4194312 | tf_op jit(solution)/shard_map/dynamic_slice | solution.py:369
  48.6 1.8 collective-permute-start.2
  50.5 0.0 copy-done.3
  50.5 1.2 constant_dynamic-slice_fusion.8
  51.6 0.0 collective-permute-start.1
  51.6 0.6 fusion.chosen
  52.2 0.8 collective-permute-done.2
  53.0 2.3 %maximum_select_fusion.1.cot = bf16[512,2048]{1,0:T(8,128)(2,1)} fusion(bf16[256,2048]{1,0:T(8,128)(2,1)S(1)} %collective-permute-done.2, bf16[256,2048]{1,0:T(8,128)(2,1)S(1)} %get-tuple-element.66, pred[]{:T(512)S(6)} %eq.4), kind=kLoop, calls=%fused_computation.1 | loop fusion | flops 9437184 | bytes 4194305 | tf_op jit(solution)/shard_map/jit(_where)/select_n | solution.py:378
  55.3 0.0 collective-permute-done.1
  55.3 3.9 %maximum_select_fusion.queries = bf16[512,2048]{1,0:T(8,128)(2,1)} fusion(bf16[256,2048]{1,0:T(8,128)(2,1)} %collective-permute-done.1, bf16[256,2048]{1,0:T(8,128)(2,1)S(1)} %get-tuple-element.68, pred[]{:T(512)S(6)} %eq.4), kind=kLoop, calls=%fused_computation | loop fusion | flops 9437184 | bytes 4194305 | tf_op jit(solution)/shard_map/jit(_where)/select_n | solution.py:378
  59.2 12.0 %near_forward.1 = (f32[2048,512]{1,0:T(8,128)}, f32[32,512]{1,0:T(8,128)}, bf16[2048,512]{1,0:T(8,128)(2,1)}) custom-call(bf16[512,2048]{1,0:T(8,128)(2,1)} %maximum_select_fusion.queries, bf16[512,2048]{1,0:T(8,128)(2,1)} %maximum_select_fusion.1.cot, bf16[512,1024]{1,0:T(8,128)(2,1)} %copy-done.2, bf16[512,1024]{1,0:T(8,128)(2,1)} %copy-done.2), custom_call_target="tpu_custom_call" | custom-call | flops 3221225472 | bytes 20971520 | tf_op jit(solution)/shard_map/near_forward/pallas_call | solution.py:208
  71.2 2.3 %all-to-all-done.1.far = bf16[64,4,2,16,128]{4,3,2,1,0:T(8,128)(2,1)} async-done(((bf16[64,4,2,16,128]{4,3,2,1,0:T(8,128)(2,1)}), bf16[64,4,2,16,128]{4,3,2,1,0:T(8,128)(2,1)}, u32[]{:S(2)}, u32[]{:S(2)}) %all-to-all-start.1) | async-done | bytes 2097184 | tf_op jit(solution)/shard_map/all_to_all | solution.py:364
  73.5 31.1 %far_attention.1 = (bf16[2048,512]{1,0:T(8,128)(2,1)}, f32[2048,512]{1,0:T(8,128)}, f32[32,512]{1,0:T(8,128)}, bf16[64,4,2,16,128]{4,3,2,1,0:T(8,128)(2,1)}) custom-call(s32[8]{0:T(128)} %fusion.chosen, bf16[512,2048]{1,0:T(8,128)(2,1)} %maximum_select_fusion.queries, bf16[2048,512]{1,0:T(8,128)(2,1)} %get-tuple-element.41.cot_t, ...), custom_call_target="tpu_custom_call" | custom-call | flops 25769803776 | bytes 20971520 | tf_op jit(solution)/shard_map/far_attention/pallas_call | solution.py:295
  104.6 38.6 %all-to-all-start.2 = ((bf16[64,4,2,16,128]{4,3,2,1,0:T(8,128)(2,1)}), bf16[64,4,2,16,128]{4,3,2,1,0:T(8,128)(2,1)S(1)}, u32[]{:S(2)}, u32[]{:S(2)}) async-start(bf16[64,4,2,16,128]{4,3,2,1,0:T(8,128)(2,1)} %get-tuple-element.45), calls=%async_computation.2 | async-start | bytes 4194304 | tf_op jit(solution)/shard_map/all_to_all | solution.py:364
  143.2 13.9 %near_backward.1 = (bf16[512,2048]{1,0:T(8,128)(2,1)}, bf16[512,2048]{1,0:T(8,128)(2,1)}, f32[512,512]{1,0:T(8,128)}, f32[512,512]{1,0:T(8,128)}) custom-call(bf16[512,2048]{1,0:T(8,128)(2,1)} %maximum_select_fusion.queries, bf16[512,2048]{1,0:T(8,128)(2,1)} %maximum_select_fusion.1.cot, bf16[512,1024]{1,0:T(8,128)(2,1)} %copy-done.2, ...), custom_call_target="tpu_custom_call" | custom-call | flops 8053063680 | bytes 20971520 | tf_op jit(solution)/shard_map/near_backward/pallas_call | solution.py:349
  157.1 0.0 copy-start.5
  157.1 0.0 copy-start
  157.1 2.5 %constant_dynamic-slice_fusion.4 = bf16[256,2048]{1,0:T(8,128)(2,1)} fusion(bf16[512,2048]{1,0:T(8,128)(2,1)} %get-tuple-element.54, s32[]{:T(128)S(6)} %select_n.104), kind=kLoop, calls=%fused_computation.16 | loop fusion | bytes 2097156 | tf_op jit(solution)/shard_map/dynamic_slice | solution.py:392
  159.6 0.7 collective-permute-start.4
  160.2 0.0 copy-done.5
  160.2 1.0 constant_dynamic-slice_fusion.3
  161.3 0.0 collective-permute-start.5
  161.3 0.0 copy-done
  161.3 1.1 dynamic-slice_convert_fusion
  162.4 0.9 pad_maximum_fusion.2
  163.3 0.5 collective-permute-start.3
  163.8 1.9 collective-permute-done.3.near_other
  165.6 0.0 collective-permute-done.4
  165.7 0.0 collective-permute-done.5
  165.7 6.5 %all-to-all-done.2.terms = bf16[64,4,2,16,128]{4,3,2,1,0:T(8,128)(2,1)S(1)} async-done(((bf16[64,4,2,16,128]{4,3,2,1,0:T(8,128)(2,1)}), bf16[64,4,2,16,128]{4,3,2,1,0:T(8,128)(2,1)S(1)}, u32[]{:S(2)}, u32[]{:S(2)}) %all-to-all-start.2) | async-done | bytes 2097184 | tf_op jit(solution)/shard_map/all_to_all | solution.py:364
  172.1 2.9 %add_terms.1 = bf16[64,8,8,128]{3,2,1,0:T(8,128)(2,1)} custom-call(s32[512]{0:T(512)S(1)} %reshape.26.table, bf16[64,4,2,16,128]{4,3,2,1,0:T(8,128)(2,1)S(1)} %all-to-all-done.2.terms), custom_call_target="tpu_custom_call" | custom-call | tf_op jit(solution)/shard_map/add_terms/pallas_call | solution.py:102
  175.0 6.7 %all-to-all-start.3 = ((bf16[64,8,8,128]{3,2,1,0:T(8,128)(2,1)}), bf16[64,8,8,128]{3,2,1,0:T(8,128)(2,1)S(1)}, u32[]{:S(2)}, u32[]{:S(2)}) async-start(bf16[64,8,8,128]{3,2,1,0:T(8,128)(2,1)} %add_terms.1), calls=%async_computation.3 | async-start | bytes 2097152 | tf_op jit(solution)/shard_map/all_to_all | solution.py:364
  181.7 0.0 copy-start.4
  181.7 1.5 constant_dynamic-slice_fusion.1
  183.2 0.4 copy-done.4
  183.6 0.1 constant_dynamic-slice_fusion.2
  183.7 3.7 %maximum_select_fusion.3 = bf16[256,4096]{1,0:T(8,128)(2,1)} fusion(bf16[256,2048]{1,0:T(8,128)(2,1)} %collective-permute-done.5, bf16[256,2048]{1,0:T(8,128)(2,1)S(1)} %constant_dynamic-slice_fusion.1, pred[]{:T(512)S(6)} %eq.4), kind=kLoop, calls=%fused_computation.3 | loop fusion | flops 9437184 | bytes 4194305 | tf_op jit(solution)/shard_map/jit(_where)/select_n | solution.py:378
  187.4 0.0 copy-start.1
  187.4 3.8 %maximum_select_fusion.2 = bf16[256,4096]{1,0:T(8,128)(2,1)} fusion(bf16[256,2048]{1,0:T(8,128)(2,1)} %collective-permute-done.4, bf16[256,2048]{1,0:T(8,128)(2,1)S(1)} %constant_dynamic-slice_fusion.2, pred[]{:T(512)S(6)} %eq.4), kind=kLoop, calls=%fused_computation.2 | loop fusion | flops 9437184 | bytes 4194305 | tf_op jit(solution)/shard_map/jit(_where)/select_n | solution.py:378
  191.1 8.0 %all-to-all-done.3.mine = bf16[64,8,8,128]{3,2,1,0:T(8,128)(2,1)S(1)} async-done(((bf16[64,8,8,128]{3,2,1,0:T(8,128)(2,1)}), bf16[64,8,8,128]{3,2,1,0:T(8,128)(2,1)S(1)}, u32[]{:S(2)}, u32[]{:S(2)}) %all-to-all-start.3) | async-done | bytes 1048608 | tf_op jit(solution)/shard_map/all_to_all | solution.py:364
  199.2 2.5 %collective-permute-start.6 = (bf16[32,8,8,128]{3,2,1,0:T(8,128)(2,1)S(1)}, bf16[32,8,8,128]{3,2,1,0:T(8,128)(2,1)S(1)}, u32[]{:S(2)}, u32[]{:S(2)}) collective-permute-start(bf16[32,8,8,128]{3,2,1,0:T(8,128)(2,1)S(1)} %constant_dynamic-slice_fusion), channel_id=1, source_target_pairs={{0,1},{1,0},{2,3},{3,2},{4,5},{5,4},{6,7},{7,6},{8,9},{9,8},{10,11... | collective-permute-start | bytes 1572872 | tf_op jit(solution)/shard_map/ppermute | solution.py:374
  201.7 1.5 collective-permute-done.6.other
  203.2 0.0 copy-done.1
  203.2 3.4 %finish.1 = (bf16[256,1024]{1,0:T(8,128)(2,1)}, bf16[256,1024]{1,0:T(8,128)(2,1)}) custom-call(s32[1]{0:T(128)} %bitcast.4.core, bf16[64,8,8,128]{3,2,1,0:T(8,128)(2,1)S(1)} %all-to-all-done.3.mine, bf16[32,8,8,128]{3,2,1,0:T(8,128)(2,1)S(1)} %collective-permute-done.6.other, f32[512,512]{1,0:T(8,128)S(1)} %copy-done, f32[512,512]{1,0:T(8,128)S(1)} %copy-done.1, ...), custom_call_target="tpu_custom_call" | custom-call | tf_op jit(solution)/shard_map/finish/pallas_call | solution.py:140
  (6 shorter events, 0.1 us)
Async XLA Ops:
  0.6 2.9 %copy-start.6 = (s32[1,16]{1,0:T(1,128)S(1)}, s32[1,16]{1,0:T(1,128)}, u32[]{:S(2)}) copy-start(s32[1,16]{1,0:T(1,128)} %param.9) | copy-start | bytes 196
  2.0 3.0 %collective-permute-start = (bf16[256,1024]{1,0:T(8,128)(2,1)S(1)}, bf16[256,1024]{1,0:T(8,128)(2,1)S(1)}, u32[]{:S(2)}, u32[]{:S(2)}) collective-permute-start(bf16[256,1024]{1,0:T(8,128)(2,1)S(1)} %pad_maximum_fusion.1), channel_id=1, source_target_pairs={{0,1},{1,0},{2,3},{3,2},{4,5},{5,4},{6,7},{7,6},{8,9},{9,8},{10,11... | collective-permute-start | bytes 1572872 | tf_op jit(solution)/shard_map/ppermute | solution.py:374
  5.5 1.4 copy-start.2
  6.9 30.6 %all-to-all-start = ((bf16[64,9,8,128]{3,2,1,0:T(8,128)(2,1)}), bf16[64,9,8,128]{3,2,1,0:T(8,128)(2,1)S(1)}, u32[]{:S(2)}, u32[]{:S(2)}) async-start(bf16[64,9,8,128]{3,2,1,0:T(8,128)(2,1)} %pad_maximum_fusion), calls=%async_computation | async-start | bytes 2359296 | tf_op jit(solution)/shard_map/all_to_all | solution.py:364
  40.2 33.3 %all-to-all-start.1 = ((bf16[64,4,2,16,128]{4,3,2,1,0:T(8,128)(2,1)}), bf16[64,4,2,16,128]{4,3,2,1,0:T(8,128)(2,1)}, u32[]{:S(2)}, u32[]{:S(2)}) async-start(bf16[64,4,2,16,128]{4,3,2,1,0:T(8,128)(2,1)} %pick.1), calls=%async_computation.1 | async-start | bytes 4194304 | tf_op jit(solution)/shard_map/all_to_all | solution.py:364
  45.8 4.7 %copy-start.3 = (bf16[256,4096]{1,0:T(8,128)(2,1)S(1)}, bf16[256,4096]{1,0:T(8,128)(2,1)}, u32[]{:S(2)}) copy-start(bf16[256,4096]{1,0:T(8,128)(2,1)} %param.5) | copy-start | bytes 6291460
  48.6 4.3 %collective-permute-start.2 = (bf16[256,2048]{1,0:T(8,128)(2,1)}, bf16[256,2048]{1,0:T(8,128)(2,1)S(1)}, u32[]{:S(2)}, u32[]{:S(2)}) collective-permute-start(bf16[256,2048]{1,0:T(8,128)(2,1)} %get-tuple-element.67), channel_id=1, source_target_pairs={{0,1},{1,0},{2,3},{3,2},{4,5},{5,4},{6,7},{7,6},{8,9},{9,8},{10,11... | collective-permute-start | bytes 3145736 | tf_op jit(solution)/shard_map/ppermute | solution.py:374
  51.6 3.7 %collective-permute-start.1 = (bf16[256,2048]{1,0:T(8,128)(2,1)}, bf16[256,2048]{1,0:T(8,128)(2,1)}, u32[]{:S(2)}, u32[]{:S(2)}) collective-permute-start(bf16[256,2048]{1,0:T(8,128)(2,1)} %get-tuple-element.69), channel_id=1, source_target_pairs={{0,1},{1,0},{2,3},{3,2},{4,5},{5,4},{6,7},{7,6},{8,9},{9,8},{10,11... | collective-permute-start | bytes 3145736 | tf_op jit(solution)/shard_map/ppermute | solution.py:374
  104.6 67.5 %all-to-all-start.2 = ((bf16[64,4,2,16,128]{4,3,2,1,0:T(8,128)(2,1)}), bf16[64,4,2,16,128]{4,3,2,1,0:T(8,128)(2,1)S(1)}, u32[]{:S(2)}, u32[]{:S(2)}) async-start(bf16[64,4,2,16,128]{4,3,2,1,0:T(8,128)(2,1)} %get-tuple-element.45), calls=%async_computation.2 | async-start | bytes 4194304 | tf_op jit(solution)/shard_map/all_to_all | solution.py:364
  157.1 3.1 %copy-start.5 = (bf16[512,2048]{1,0:T(8,128)(2,1)S(1)}, bf16[512,2048]{1,0:T(8,128)(2,1)}, u32[]{:S(2)}) copy-start(bf16[512,2048]{1,0:T(8,128)(2,1)} %get-tuple-element.56) | copy-start | bytes 6291460
  157.1 4.2 %copy-start = (f32[512,512]{1,0:T(8,128)S(1)}, f32[512,512]{1,0:T(8,128)}, u32[]{:S(2)}) copy-start(f32[512,512]{1,0:T(8,128)} %get-tuple-element.61.near_k) | copy-start | bytes 3145732
  159.6 6.1 %collective-permute-start.4 = (bf16[256,2048]{1,0:T(8,128)(2,1)}, bf16[256,2048]{1,0:T(8,128)(2,1)}, u32[]{:S(2)}, u32[]{:S(2)}) collective-permute-start(bf16[256,2048]{1,0:T(8,128)(2,1)} %constant_dynamic-slice_fusion.4), channel_id=1, source_target_pairs={{0,1},{1,0},{2,3},{3,2},{4,5},{5,4},{6,7},{7,6},{8,9},{9,8},{10,11... | collective-permute-start | bytes 3145736 | tf_op jit(solution)/shard_map/ppermute | solution.py:374
  161.3 4.4 %collective-permute-start.5 = (bf16[256,2048]{1,0:T(8,128)(2,1)}, bf16[256,2048]{1,0:T(8,128)(2,1)}, u32[]{:S(2)}, u32[]{:S(2)}) collective-permute-start(bf16[256,2048]{1,0:T(8,128)(2,1)} %constant_dynamic-slice_fusion.3), channel_id=1, source_target_pairs={{0,1},{1,0},{2,3},{3,2},{4,5},{5,4},{6,7},{7,6},{8,9},{9,8},{10,11... | collective-permute-start | bytes 3145736 | tf_op jit(solution)/shard_map/ppermute | solution.py:374
  163.3 2.4 %collective-permute-start.3 = (bf16[256,1024]{1,0:T(8,128)(2,1)}, bf16[256,1024]{1,0:T(8,128)(2,1)}, u32[]{:S(2)}, u32[]{:S(2)}) collective-permute-start(bf16[256,1024]{1,0:T(8,128)(2,1)} %pad_maximum_fusion.2), channel_id=1, source_target_pairs={{0,1},{1,0},{2,3},{3,2},{4,5},{5,4},{6,7},{7,6},{8,9},{9,8},{10,11... | collective-permute-start | bytes 1572872 | tf_op jit(solution)/shard_map/ppermute | solution.py:374
  175.0 24.2 %all-to-all-start.3 = ((bf16[64,8,8,128]{3,2,1,0:T(8,128)(2,1)}), bf16[64,8,8,128]{3,2,1,0:T(8,128)(2,1)S(1)}, u32[]{:S(2)}, u32[]{:S(2)}) async-start(bf16[64,8,8,128]{3,2,1,0:T(8,128)(2,1)} %add_terms.1), calls=%async_computation.3 | async-start | bytes 2097152 | tf_op jit(solution)/shard_map/all_to_all | solution.py:364
  181.7 1.9 copy-start.4
  187.4 15.9 %copy-start.1 = (f32[512,512]{1,0:T(8,128)S(1)}, f32[512,512]{1,0:T(8,128)}, u32[]{:S(2)}) copy-start(f32[512,512]{1,0:T(8,128)} %get-tuple-element.62.near_v) | copy-start | bytes 3145732
  199.2 4.0 %collective-permute-start.6 = (bf16[32,8,8,128]{3,2,1,0:T(8,128)(2,1)S(1)}, bf16[32,8,8,128]{3,2,1,0:T(8,128)(2,1)S(1)}, u32[]{:S(2)}, u32[]{:S(2)}) collective-permute-start(bf16[32,8,8,128]{3,2,1,0:T(8,128)(2,1)S(1)} %constant_dynamic-slice_fusion), channel_id=1, source_target_pairs={{0,1},{1,0},{2,3},{3,2},{4,5},{5,4},{6,7},{7,6},{8,9},{9,8},{10,11... | collective-permute-start | bytes 1572872 | tf_op jit(solution)/shard_map/ppermute | solution.py:374

commit v4 on v3

--- a/solution.py
+++ b/solution.py
@@ -130,7 +130,7 @@
 
 
 def finish(core, mine, other, near_k, near_v, near_other):
-    steps = 4
+    steps = 2
     tiles = mine.shape[1]
     chunk = ROWS // 8 // steps
     far = pl.BlockSpec((chunk, tiles, 8, HD), lambda i, c: (i, 0, 0, 0))
@@ -179,7 +179,20 @@
     return jnp.concatenate([score[:, :ROWS], diagonal], axis=1) if piece else diagonal
 
 
-def near_forward_kernel(queries, cot, keys, values, out_t, lse_t, cot_t, keys_t):
+def near_forward_kernel(
+    core, my_q, got_q, my_cot, got_cot, keys, values, out_t, lse_t, queries, cot_t, cot, keys_t
+):
+    for side in (0, 1):
+        mine = slice(ROWS * side, ROWS * side + ROWS)
+        other = slice(ROWS - ROWS * side, 2 * ROWS - ROWS * side)
+
+        @pl.when(core[0] == side)
+        def _():
+            queries[mine] = my_q[...]
+            queries[other] = got_q[...]
+            cot[mine] = my_cot[...]
+            cot[other] = got_cot[...]
+
     keys_t[...] = keys[...].T
     cot_t[...] = cot[...].T
     for piece in (0, 1):
@@ -193,33 +206,40 @@
             raised = jnp.exp2(score - top)
             total = jnp.sum(raised, axis=1, keepdims=True)
             out = dot(raised.astype(bf16), values[:width], NN) * (1.0 / total)
-            out_t[cols, rows] = out.T
+            out_t[cols, rows] = out.T.astype(out_t.dtype)
             found.append(top + jnp.log2(total))
         lse = lanes(found).T
         for g in range(GROUP):
             lse_t[g : g + 1, rows] = lse[HD // GROUP * g : HD // GROUP * g + 1]
 
 
-def near_forward(queries, cot, near):
-    wide = pl.BlockSpec((BLOCK, GROUP * HD), lambda h: (0, h))
-    key = pl.BlockSpec((BLOCK, HD), lambda h: (0, h))
-    value = pl.BlockSpec((BLOCK, HD), lambda h: (0, HALF + h))
-    tall = pl.BlockSpec((GROUP * HD, BLOCK), lambda h: (h, 0))
+def near_forward(core, my_q, got_q, my_cot, got_cot, near):
+    mine = pl.BlockSpec((ROWS, GROUP * HD), lambda h, c: (0, HALF * c[0] + h))
+    got = pl.BlockSpec((ROWS, GROUP * HD), lambda h, c: (0, h))
+    wide = pl.BlockSpec((BLOCK, GROUP * HD), lambda h, c: (0, h))
+    key = pl.BlockSpec((BLOCK, HD), lambda h, c: (0, h))
+    value = pl.BlockSpec((BLOCK, HD), lambda h, c: (0, HALF + h))
+    tall = pl.BlockSpec((GROUP * HD, BLOCK), lambda h, c: (h, 0))
+    width = HALF * GROUP * HD
     return pl.pallas_call(
         near_forward_kernel,
-        grid=(HALF,),
-        in_specs=[wide, wide, key, value],
-        out_specs=[tall, pl.BlockSpec((8, BLOCK), lambda h: (h, 0)), tall],
+        grid_spec=pltpu.PrefetchScalarGridSpec(
+            num_scalar_prefetch=1,
+            grid=(HALF,),
+            in_specs=[mine, got, mine, got, key, value],
+            out_specs=[tall, pl.BlockSpec((8, BLOCK), lambda h, c: (h, 0)), wide, tall],
+            scratch_shapes=[pltpu.VMEM((BLOCK, GROUP * HD), bf16), pltpu.VMEM((HD, BLOCK), bf16)],
+        ),
         out_shape=[
-            jax.ShapeDtypeStruct(queries.shape[::-1], f32),
+            jax.ShapeDtypeStruct((width, BLOCK), f32),
             jax.ShapeDtypeStruct((HALF * 8, BLOCK), f32),
-            jax.ShapeDtypeStruct(queries.shape[::-1], bf16),
+            jax.ShapeDtypeStruct((BLOCK, width), bf16),
+            jax.ShapeDtypeStruct((width, BLOCK), bf16),
         ],
-        scratch_shapes=[pltpu.VMEM((HD, BLOCK), bf16)],
-        compiler_params=pltpu.CompilerParams(vmem_limit_bytes=60 * 2**20),
+        compiler_params=pltpu.CompilerParams(vmem_limit_bytes=62 * 2**20),
         cost_estimate=cost(HALF, BLOCK * 3 // 4, 2),
         name="near_forward",
-    )(queries, cot, near, near)
+    )(core.reshape(1), my_q, got_q, my_cot, got_cot, near, near)
 
 
 def far_kernel(
@@ -248,12 +268,12 @@
         total = jnp.sum(raised, axis=0, keepdims=True) + near
         over = 1.0 / total
         raised_b = raised.astype(bf16)
-        out = (dot(values_t[...], raised_b, NN) + near * near_t[cols, :]) * over
+        out = (dot(values_t[...], raised_b, NN) + near * near_t[cols, :].astype(f32)) * over
         att_t[cols, :] = out.astype(bf16)
         cot_over = (cot_t[cols, :].astype(f32) * over).astype(bf16)
         delta = jnp.sum(cot_over.astype(f32) * out, axis=0, keepdims=True)
         dscore = (raised * (dot(v, cot_over, NN) - delta)).astype(bf16)
-        grad_t[cols, :] = dot(keys_t[...], dscore, NN)
+        grad_t[cols, :] = dot(keys_t[...], dscore, NN).astype(grad_t.dtype)
         sum_v[...] += dot(raised_b, cot_over, NT)
         sum_k[...] += dot(dscore, q, NN)
         stats[pl.ds(g, 1), :] = top + jnp.log2(total)
@@ -314,7 +334,7 @@
 
 
 def near_backward_kernel(
-    queries, cot, keys, values, stats, att_t, far_t, att, grad_q, grad_k, grad_v, keys_t, values_t, sum_k, sum_v
+    queries, cot_t, keys, values, stats, att_t, far_t, att, grad_q, grad_k, grad_v, keys_t, values_t, sum_k, sum_v
 ):
     keys_t[...] = keys[...].T
     values_t[...] = values[...].T
@@ -328,20 +348,20 @@
         for g in range(GROUP):
             cols = slice(HD * g, HD * g + HD)
             q = queries[rows, cols]
-            c = cot[rows, cols]
+            c = cot_t[cols, rows]
             score = near_scores(q, keys_t[:, :width], piece)
             weight = jnp.exp2(score - columns[rows, g : g + 1])
-            dweight = dot(c, values_t[:, :width], NN)
+            dweight = dot(c, values_t[:, :width], TN)
             dscore = (weight * (dweight - columns[rows, GROUP + g : GROUP + g + 1])).astype(bf16)
-            grad = far_t[cols, rows].T + dot(dscore, keys[:width], NN)
+            grad = far_t[cols, rows].astype(f32).T + dot(dscore, keys[:width], NN)
             grad_q[rows, cols] = (grad * SCALE).astype(bf16)
-            sum_v[:, :width] += dot(c, weight.astype(bf16), TN)
+            sum_v[:, :width] += dot(c, weight.astype(bf16), NN)
             sum_k[:, :width] += dot(q, dscore, TN)
     grad_k[...] = sum_k[...].T * SCALE
     grad_v[...] = sum_v[...].T
 
 
-def near_backward(queries, cot, near, stats, att_t, far_t):
+def near_backward(queries, cot_t, near, stats, att_t, far_t):
     wide = pl.BlockSpec((BLOCK, GROUP * HD), lambda h: (0, h))
     tall = pl.BlockSpec((GROUP * HD, BLOCK), lambda h: (h, 0))
     key = pl.BlockSpec((BLOCK, HD), lambda h: (0, h))
@@ -349,7 +369,7 @@
     return pl.pallas_call(
         near_backward_kernel,
         grid=(HALF,),
-        in_specs=[wide, wide, key, value, pl.BlockSpec((8, BLOCK), lambda h: (h, 0)), tall, tall],
+        in_specs=[wide, tall, key, value, pl.BlockSpec((8, BLOCK), lambda h: (h, 0)), tall, tall],
         out_specs=[wide, wide, key, key],
         out_shape=[jax.ShapeDtypeStruct(queries.shape, bf16)] * 2
         + [jax.ShapeDtypeStruct((BLOCK, HALF * HD), f32)] * 2,
@@ -357,7 +377,7 @@
         compiler_params=pltpu.CompilerParams(vmem_limit_bytes=58 * 2**20),
         cost_estimate=cost(HALF, BLOCK * 3 // 4, 5),
         name="near_backward",
-    )(queries, cot, near, near, stats, att_t, far_t)
+    )(queries, cot_t, near, near, stats, att_t, far_t)
 
 
 def spread(x):
@@ -380,11 +400,6 @@
         jnp.concatenate([mine, other], axis=axis),
         jnp.concatenate([other, mine], axis=axis),
     )
-
-
-def to_block(x, core):
-    mine, other = halves(x, core)
-    return in_order(mine, swap(other), core, 0)
 
 
 def others_rows(x, core):
@@ -418,17 +433,15 @@
     picked = pick(table, shares)
     picked, queries, cotangent = lax.optimization_barrier((picked, queries, cotangent))
     far = spread(picked)
-    block_queries = to_block(queries, core)
-    block_cot = to_block(cotangent, core)
-    near_t, lse_t, cot_t = near_forward(block_queries, block_cot, near)
+    got_q = swap(halves(queries, core)[1])
+    got_cot = swap(halves(cotangent, core)[1])
+    near_t, lse_t, block_q, cot_t = near_forward(core, queries, got_q, cotangent, got_cot, near)
     far, near_t, lse_t, cot_t = lax.optimization_barrier((far, near_t, lse_t, cot_t))
     att_t, far_t, stats, grad_far = far_attention(
-        chosen, block_queries, cot_t, near_t, lse_t, far
+        chosen, block_q, cot_t, near_t, lse_t, far
     )
     back = spread(grad_far)
-    attended, grad_q, grad_k, grad_v = near_backward(
-        block_queries, block_cot, near, stats, att_t, far_t
-    )
+    attended, grad_q, grad_k, grad_v = near_backward(block_q, cot_t, near, stats, att_t, far_t)
     near_other = swap(
         jnp.concatenate([others_rows(x, core).astype(bf16) for x in (grad_k, grad_v)], axis=1)
     )

time: 207 us -> 202 us (0.976)
  blocking collectives: 0 us -> 30.4 us
  waiting for transfers between devices: 41.9 us -> 26.8 us
  starting transfers between devices: 69.1 us -> 59 us
  other arithmetic: 16.9 us -> 9.59 us
  local copies, waits for them, and re-layouts: 12.1 us -> 9.43 us
    all_to_all x0 -> x1, blocking collectives: none -> 30.4 us  [spread(): lax.all_to_all(x, 'ctx', 0, 0, axis_index_groups=SAME_HALF, tiled=True)]
    all_to_all x4 -> x3, waiting for transfers between devices: 36.2 us -> 19.7 us  [spread(): lax.all_to_all(x, 'ctx', 0, 0, axis_index_groups=SAME_HALF, tiled=True)]
    all_to_all x4 -> x3, starting transfers between devices: 62.1 us -> 49.2 us  [spread(): lax.all_to_all(x, 'ctx', 0, 0, axis_index_groups=SAME_HALF, tiled=True)]
    select_n x5 -> x3, other arithmetic: 14.1 us -> 7.85 us  [in_order(): jnp.where(core == 0, jnp.concatenate([mine, other], axis=axis), jnp.conca...]
    dynamic_slice x3 -> x1, local copies, waits for them, and re-layouts: 5.28 us -> 1.27 us  [halves(): mine = lax.dynamic_slice_in_dim(x, core * width, width, 1)]
    ppermute x7, starting transfers between devices: 7.01 us -> 9.74 us  [swap(): return lax.ppermute(x, 'ctx', PAIR)]
  transfers between devices with their start and end apart: 11 -> 10, of which waited for: 8 -> 8; matrix products, arithmetic and copies ran while one was open for 12% -> 8% of each run, Pallas kernels for 13% -> 13%
where the time goes in v4:
time: 202 us; the launch traced here: 201 us
  Pallas kernels  64.8 us (32%)
  starting transfers between devices  59 us (29%)
  blocking collectives  30.4 us (15%)
  waiting for transfers between devices  26.8 us (13%)
  other arithmetic  9.59 us (5%)
  local copies, waits for them, and re-layouts  9.43 us (5%)
    all_to_all x3, starting transfers between devices, spread(): lax.all_to_all(x, 'ctx', 0, 0, axis_index_groups=SAME_HALF, tiled=True)  49.2 us
    pallas_call x1, Pallas kernels, far_attention(): pl.pallas_call(far_kernel, grid_spec=pltpu.PrefetchScalarGridSpec(num_sca...  31.1 us
    all_to_all x1, blocking collectives, spread(): lax.all_to_all(x, 'ctx', 0, 0, axis_index_groups=SAME_HALF, tiled=True)  30.4 us
    all_to_all x3, waiting for transfers between devices, spread(): lax.all_to_all(x, 'ctx', 0, 0, axis_index_groups=SAME_HALF, tiled=True)  19.7 us
    pallas_call x1, Pallas kernels, near_backward(): pl.pallas_call(near_backward_kernel, grid=(HALF,), in_specs=[wide, tall,...  13.9 us
    pallas_call x1, Pallas kernels, near_forward(): pl.pallas_call(near_forward_kernel, grid_spec=pltpu.PrefetchScalarGridSpe...  12.4 us
    ppermute x7, starting transfers between devices, swap(): return lax.ppermute(x, 'ctx', PAIR)  9.74 us
    select_n x3, other arithmetic, in_order(): jnp.where(core == 0, jnp.concatenate([mine, other], axis=axis), jnp.conca...  7.85 us
  transfers between devices with their start and end apart: 10, of which 8 were waited for; matrix products, arithmetic and copies ran while one was open for 8% of the time, Pallas kernels for 13%

profile of v4, /device:TPU:1, one launch (start us, length us, event | category | flops | bytes accessed | tf_op | source)
XLA Modules:
  0.0 200.8 jit_solution(12423375370332195666)
XLA Ops:
  0.6 0.0 copy-start.6
  0.7 1.3 constant_dynamic-slice_fusion.9
  1.9 0.1 pad_maximum_fusion.1
  2.0 1.5 collective-permute-start
  3.5 0.0 copy-done.6
  3.5 1.5 collective-permute-done
  5.0 0.4 maximum_select_fusion.2.keys.values
  5.5 0.0 copy-start.2
  5.5 0.1 pad_maximum_fusion
  5.6 30.4 %all_to_all.20.shares = bf16[64,9,8,128]{3,2,1,0:T(8,128)(2,1)S(1)} all-to-all(bf16[64,9,8,128]{3,2,1,0:T(8,128)(2,1)S(1)} %pad_maximum_fusion), channel_id=1, replica_groups={{0,2,4,6,8,10,12,14,16,18,20,22,24,26,28,30,32,34,36,38,40,42,44,46,48,..., dimensions={0} | all-to-all | bytes 2359296 | tf_op jit(solution)/shard_map/all_to_all | solution.py:384
  36.1 0.0 copy-done.2
  36.1 0.1 slice_select_fusion
  36.2 0.1 reshape.27.table
  36.3 2.5 %pick.1 = bf16[64,4,2,16,128]{4,3,2,1,0:T(8,128)(2,1)} custom-call(s32[512]{0:T(512)S(1)} %reshape.27.table, bf16[64,9,8,128]{3,2,1,0:T(8,128)(2,1)S(1)} %all_to_all.20.shares), custom_call_target="tpu_custom_call" | custom-call | tf_op jit(solution)/shard_map/pick/pallas_call | solution.py:52
  38.8 0.0 copy-start.5
  38.8 5.7 %all-to-all-start.1 = ((bf16[64,4,2,16,128]{4,3,2,1,0:T(8,128)(2,1)}), bf16[64,4,2,16,128]{4,3,2,1,0:T(8,128)(2,1)}, u32[]{:S(2)}, u32[]{:S(2)}) async-start(bf16[64,4,2,16,128]{4,3,2,1,0:T(8,128)(2,1)} %pick.1), calls=%async_computation.1 | async-start | bytes 4194304 | tf_op jit(solution)/shard_map/all_to_all | solution.py:384
  44.5 0.0 copy-done.5
  44.5 0.1 constant_dynamic-slice_fusion.5
  44.6 1.9 collective-permute-start.2
  46.5 1.3 constant_dynamic-slice_fusion.6
  47.8 0.1 collective-permute-start.1
  47.9 0.6 fusion.chosen
  48.5 0.3 collective-permute-done.2.got_cot
  48.8 0.0 copy-start.7
  48.8 1.9 collective-permute-done.1.got_q
  50.7 0.0 copy-done.7
  50.7 12.4 %near_forward.1 = (f32[2048,512]{1,0:T(8,128)}, f32[32,512]{1,0:T(8,128)}, bf16[512,2048]{1,0:T(8,128)(2,1)}, bf16[2048,512]{1,0:T(8,128)(2,1)}) custom-call(s32[1]{0:T(128)} %bitcast.4.core, bf16[256,4096]{1,0:T(8,128)(2,1)} %my_q, bf16[256,2048]{1,0:T(8,128)(2,1)} %collective-permute-done.1.got_q, bf16[256,4096]{1,0:T(8,128)(2,1)} %my_cot, ...), custom_call_target="tpu_custom_call" | custom-call | flops 3221225472 | bytes 20971520 | tf_op jit(solution)/shard_map/near_forward/pallas_call | solution.py:224
  63.1 9.1 %all-to-all-done.1.far = bf16[64,4,2,16,128]{4,3,2,1,0:T(8,128)(2,1)} async-done(((bf16[64,4,2,16,128]{4,3,2,1,0:T(8,128)(2,1)}), bf16[64,4,2,16,128]{4,3,2,1,0:T(8,128)(2,1)}, u32[]{:S(2)}, u32[]{:S(2)}) %all-to-all-start.1) | async-done | bytes 2097184 | tf_op jit(solution)/shard_map/all_to_all | solution.py:384
  72.2 31.1 %far_attention.1 = (bf16[2048,512]{1,0:T(8,128)(2,1)}, f32[2048,512]{1,0:T(8,128)}, f32[32,512]{1,0:T(8,128)}, bf16[64,4,2,16,128]{4,3,2,1,0:T(8,128)(2,1)}) custom-call(s32[8]{0:T(128)} %fusion.chosen, bf16[512,2048]{1,0:T(8,128)(2,1)} %get-tuple-element.38.queries, bf16[2048,512]{1,0:T(8,128)(2,1)} %get-tuple-element.43.cot_t, ...), custom_call_target="tpu_custom_call" | custom-call | flops 25769803776 | bytes 20971520 | tf_op jit(solution)/shard_map/far_attention/pallas_call | solution.py:315
  103.3 37.1 %all-to-all-start.2 = ((bf16[64,4,2,16,128]{4,3,2,1,0:T(8,128)(2,1)}), bf16[64,4,2,16,128]{4,3,2,1,0:T(8,128)(2,1)S(1)}, u32[]{:S(2)}, u32[]{:S(2)}) async-start(bf16[64,4,2,16,128]{4,3,2,1,0:T(8,128)(2,1)} %get-tuple-element.47), calls=%async_computation.2 | async-start | bytes 4194304 | tf_op jit(solution)/shard_map/all_to_all | solution.py:384
  140.4 13.9 %near_backward.1 = (bf16[512,2048]{1,0:T(8,128)(2,1)}, bf16[512,2048]{1,0:T(8,128)(2,1)}, f32[512,512]{1,0:T(8,128)}, f32[512,512]{1,0:T(8,128)}) custom-call(bf16[512,2048]{1,0:T(8,128)(2,1)} %get-tuple-element.38.queries, bf16[2048,512]{1,0:T(8,128)(2,1)} %get-tuple-element.43.cot_t, bf16[512,1024]{1,0:T(8,128)(2,1)} %copy-done.2, ...), custom_call_target="tpu_custom_call" | custom-call | flops 8053063680 | bytes 20971520 | tf_op jit(solution)/shard_map/near_backward/pallas_call | solution.py:369
  154.3 0.0 copy-start.4
  154.3 0.0 copy-start
  154.3 2.5 %constant_dynamic-slice_fusion.4 = bf16[256,2048]{1,0:T(8,128)(2,1)} fusion(bf16[512,2048]{1,0:T(8,128)(2,1)} %get-tuple-element.56, s32[]{:T(128)S(6)} %select_n.84), kind=kLoop, calls=%fused_computation.14 | loop fusion | bytes 2097156 | tf_op jit(solution)/shard_map/dynamic_slice | solution.py:407
  156.8 2.0 %collective-permute-start.4 = (bf16[256,2048]{1,0:T(8,128)(2,1)}, bf16[256,2048]{1,0:T(8,128)(2,1)}, u32[]{:S(2)}, u32[]{:S(2)}) collective-permute-start(bf16[256,2048]{1,0:T(8,128)(2,1)} %constant_dynamic-slice_fusion.4), channel_id=1, source_target_pairs={{0,1},{1,0},{2,3},{3,2},{4,5},{5,4},{6,7},{7,6},{8,9},{9,8},{10,11... | collective-permute-start | bytes 3145736 | tf_op jit(solution)/shard_map/ppermute | solution.py:394
  158.8 0.0 copy-done.4
  158.8 1.0 constant_dynamic-slice_fusion.3
  159.8 0.0 collective-permute-start.5
  159.8 0.0 copy-done
  159.9 1.1 dynamic-slice_convert_fusion
  160.9 0.9 pad_maximum_fusion.2
  161.8 0.5 collective-permute-start.3
  162.3 1.9 collective-permute-done.3.near_other
  164.2 0.0 collective-permute-done.4
  164.2 0.0 collective-permute-done.5
  164.2 3.8 %all-to-all-done.2.terms = bf16[64,4,2,16,128]{4,3,2,1,0:T(8,128)(2,1)S(1)} async-done(((bf16[64,4,2,16,128]{4,3,2,1,0:T(8,128)(2,1)}), bf16[64,4,2,16,128]{4,3,2,1,0:T(8,128)(2,1)S(1)}, u32[]{:S(2)}, u32[]{:S(2)}) %all-to-all-start.2) | async-done | bytes 2097184 | tf_op jit(solution)/shard_map/all_to_all | solution.py:384
  168.0 2.8 %add_terms.1 = bf16[64,8,8,128]{3,2,1,0:T(8,128)(2,1)} custom-call(s32[512]{0:T(512)S(1)} %reshape.27.table, bf16[64,4,2,16,128]{4,3,2,1,0:T(8,128)(2,1)S(1)} %all-to-all-done.2.terms), custom_call_target="tpu_custom_call" | custom-call | tf_op jit(solution)/shard_map/add_terms/pallas_call | solution.py:102
  170.8 6.5 %all-to-all-start.3 = ((bf16[64,8,8,128]{3,2,1,0:T(8,128)(2,1)}), bf16[64,8,8,128]{3,2,1,0:T(8,128)(2,1)S(1)}, u32[]{:S(2)}, u32[]{:S(2)}) async-start(bf16[64,8,8,128]{3,2,1,0:T(8,128)(2,1)} %add_terms.1), calls=%async_computation.3 | async-start | bytes 2097152 | tf_op jit(solution)/shard_map/all_to_all | solution.py:384
  177.2 0.0 copy-start.3
  177.3 1.4 constant_dynamic-slice_fusion.1
  178.7 0.4 copy-done.3
  179.2 0.1 constant_dynamic-slice_fusion.2
  179.2 3.7 %maximum_select_fusion.1 = bf16[256,4096]{1,0:T(8,128)(2,1)} fusion(bf16[256,2048]{1,0:T(8,128)(2,1)} %collective-permute-done.5, bf16[256,2048]{1,0:T(8,128)(2,1)S(1)} %constant_dynamic-slice_fusion.1, pred[]{:T(512)S(6)} %eq.4), kind=kLoop, calls=%fused_computation.1 | loop fusion | flops 9437184 | bytes 4194305 | tf_op jit(solution)/shard_map/jit(_where)/select_n | solution.py:398
  182.9 0.0 copy-start.1
  182.9 3.8 %maximum_select_fusion = bf16[256,4096]{1,0:T(8,128)(2,1)} fusion(bf16[256,2048]{1,0:T(8,128)(2,1)} %collective-permute-done.4, bf16[256,2048]{1,0:T(8,128)(2,1)S(1)} %constant_dynamic-slice_fusion.2, pred[]{:T(512)S(6)} %eq.4), kind=kLoop, calls=%fused_computation | loop fusion | flops 9437184 | bytes 4194305 | tf_op jit(solution)/shard_map/jit(_where)/select_n | solution.py:398
  186.6 6.8 %all-to-all-done.3.mine = bf16[64,8,8,128]{3,2,1,0:T(8,128)(2,1)S(1)} async-done(((bf16[64,8,8,128]{3,2,1,0:T(8,128)(2,1)}), bf16[64,8,8,128]{3,2,1,0:T(8,128)(2,1)S(1)}, u32[]{:S(2)}, u32[]{:S(2)}) %all-to-all-start.3) | async-done | bytes 1048608 | tf_op jit(solution)/shard_map/all_to_all | solution.py:384
  193.5 3.7 %collective-permute-start.6 = (bf16[32,8,8,128]{3,2,1,0:T(8,128)(2,1)S(1)}, bf16[32,8,8,128]{3,2,1,0:T(8,128)(2,1)S(1)}, u32[]{:S(2)}, u32[]{:S(2)}) collective-permute-start(bf16[32,8,8,128]{3,2,1,0:T(8,128)(2,1)S(1)} %constant_dynamic-slice_fusion), channel_id=1, source_target_pairs={{0,1},{1,0},{2,3},{3,2},{4,5},{5,4},{6,7},{7,6},{8,9},{9,8},{10,11... | collective-permute-start | bytes 1572872 | tf_op jit(solution)/shard_map/ppermute | solution.py:394
  197.2 1.5 collective-permute-done.6.other
  198.7 0.0 copy-done.1
  198.7 2.1 %finish.1 = (bf16[256,1024]{1,0:T(8,128)(2,1)}, bf16[256,1024]{1,0:T(8,128)(2,1)}) custom-call(s32[1]{0:T(128)} %bitcast.4.core, bf16[64,8,8,128]{3,2,1,0:T(8,128)(2,1)S(1)} %all-to-all-done.3.mine, bf16[32,8,8,128]{3,2,1,0:T(8,128)(2,1)S(1)} %collective-permute-done.6.other, f32[512,512]{1,0:T(8,128)S(1)} %copy-done, f32[512,512]{1,0:T(8,128)S(1)} %copy-done.1, ...), custom_call_target="tpu_custom_call" | custom-call | tf_op jit(solution)/shard_map/finish/pallas_call | solution.py:140
  (6 shorter events, 0.1 us)
Async XLA Ops:
  0.6 2.9 %copy-start.6 = (s32[1,16]{1,0:T(1,128)S(1)}, s32[1,16]{1,0:T(1,128)}, u32[]{:S(2)}) copy-start(s32[1,16]{1,0:T(1,128)} %param.9) | copy-start | bytes 196
  2.0 3.0 %collective-permute-start = (bf16[256,1024]{1,0:T(8,128)(2,1)S(1)}, bf16[256,1024]{1,0:T(8,128)(2,1)S(1)}, u32[]{:S(2)}, u32[]{:S(2)}) collective-permute-start(bf16[256,1024]{1,0:T(8,128)(2,1)S(1)} %pad_maximum_fusion.1), channel_id=1, source_target_pairs={{0,1},{1,0},{2,3},{3,2},{4,5},{5,4},{6,7},{7,6},{8,9},{9,8},{10,11... | collective-permute-start | bytes 1572872 | tf_op jit(solution)/shard_map/ppermute | solution.py:394
  5.5 30.6 %copy-start.2 = (bf16[512,1024]{1,0:T(8,128)(2,1)}, bf16[512,1024]{1,0:T(8,128)(2,1)S(1)}, u32[]{:S(2)}) copy-start(bf16[512,1024]{1,0:T(8,128)(2,1)S(1)} %maximum_select_fusion.2.keys.values) | copy-start | bytes 3145732
  38.8 5.7 %copy-start.5 = (bf16[256,4096]{1,0:T(8,128)(2,1)S(1)}, bf16[256,4096]{1,0:T(8,128)(2,1)}, u32[]{:S(2)}) copy-start(bf16[256,4096]{1,0:T(8,128)(2,1)} %my_cot) | copy-start | bytes 6291460
  38.8 33.5 %all-to-all-start.1 = ((bf16[64,4,2,16,128]{4,3,2,1,0:T(8,128)(2,1)}), bf16[64,4,2,16,128]{4,3,2,1,0:T(8,128)(2,1)}, u32[]{:S(2)}, u32[]{:S(2)}) async-start(bf16[64,4,2,16,128]{4,3,2,1,0:T(8,128)(2,1)} %pick.1), calls=%async_computation.1 | async-start | bytes 4194304 | tf_op jit(solution)/shard_map/all_to_all | solution.py:384
  44.6 4.2 %collective-permute-start.2 = (bf16[256,2048]{1,0:T(8,128)(2,1)S(1)}, bf16[256,2048]{1,0:T(8,128)(2,1)S(1)}, u32[]{:S(2)}, u32[]{:S(2)}) collective-permute-start(bf16[256,2048]{1,0:T(8,128)(2,1)S(1)} %constant_dynamic-slice_fusion.5), channel_id=1, source_target_pairs={{0,1},{1,0},{2,3},{3,2},{4,5},{5,4},{6,7},{7,6},{8,9},{9,8},{10,11... | collective-permute-start | bytes 3145736 | tf_op jit(solution)/shard_map/ppermute | solution.py:394
  47.8 2.9 %collective-permute-start.1 = (bf16[256,2048]{1,0:T(8,128)(2,1)S(1)}, bf16[256,2048]{1,0:T(8,128)(2,1)}, u32[]{:S(2)}, u32[]{:S(2)}) collective-permute-start(bf16[256,2048]{1,0:T(8,128)(2,1)S(1)} %constant_dynamic-slice_fusion.6), channel_id=1, source_target_pairs={{0,1},{1,0},{2,3},{3,2},{4,5},{5,4},{6,7},{7,6},{8,9},{9,8},{10,11... | collective-permute-start | bytes 3145736 | tf_op jit(solution)/shard_map/ppermute | solution.py:394
  48.8 1.9 copy-start.7
  103.3 64.6 %all-to-all-start.2 = ((bf16[64,4,2,16,128]{4,3,2,1,0:T(8,128)(2,1)}), bf16[64,4,2,16,128]{4,3,2,1,0:T(8,128)(2,1)S(1)}, u32[]{:S(2)}, u32[]{:S(2)}) async-start(bf16[64,4,2,16,128]{4,3,2,1,0:T(8,128)(2,1)} %get-tuple-element.47), calls=%async_computation.2 | async-start | bytes 4194304 | tf_op jit(solution)/shard_map/all_to_all | solution.py:384
  154.3 4.5 %copy-start.4 = (bf16[512,2048]{1,0:T(8,128)(2,1)S(1)}, bf16[512,2048]{1,0:T(8,128)(2,1)}, u32[]{:S(2)}) copy-start(bf16[512,2048]{1,0:T(8,128)(2,1)} %get-tuple-element.58) | copy-start | bytes 6291460
  154.3 5.5 %copy-start = (f32[512,512]{1,0:T(8,128)S(1)}, f32[512,512]{1,0:T(8,128)}, u32[]{:S(2)}) copy-start(f32[512,512]{1,0:T(8,128)} %get-tuple-element.63.near_k) | copy-start | bytes 3145732
  156.8 7.4 %collective-permute-start.4 = (bf16[256,2048]{1,0:T(8,128)(2,1)}, bf16[256,2048]{1,0:T(8,128)(2,1)}, u32[]{:S(2)}, u32[]{:S(2)}) collective-permute-start(bf16[256,2048]{1,0:T(8,128)(2,1)} %constant_dynamic-slice_fusion.4), channel_id=1, source_target_pairs={{0,1},{1,0},{2,3},{3,2},{4,5},{5,4},{6,7},{7,6},{8,9},{9,8},{10,11... | collective-permute-start | bytes 3145736 | tf_op jit(solution)/shard_map/ppermute | solution.py:394
  159.8 4.4 %collective-permute-start.5 = (bf16[256,2048]{1,0:T(8,128)(2,1)}, bf16[256,2048]{1,0:T(8,128)(2,1)}, u32[]{:S(2)}, u32[]{:S(2)}) collective-permute-start(bf16[256,2048]{1,0:T(8,128)(2,1)} %constant_dynamic-slice_fusion.3), channel_id=1, source_target_pairs={{0,1},{1,0},{2,3},{3,2},{4,5},{5,4},{6,7},{7,6},{8,9},{9,8},{10,11... | collective-permute-start | bytes 3145736 | tf_op jit(solution)/shard_map/ppermute | solution.py:394
  161.8 2.4 %collective-permute-start.3 = (bf16[256,1024]{1,0:T(8,128)(2,1)}, bf16[256,1024]{1,0:T(8,128)(2,1)}, u32[]{:S(2)}, u32[]{:S(2)}) collective-permute-start(bf16[256,1024]{1,0:T(8,128)(2,1)} %pad_maximum_fusion.2), channel_id=1, source_target_pairs={{0,1},{1,0},{2,3},{3,2},{4,5},{5,4},{6,7},{7,6},{8,9},{9,8},{10,11... | collective-permute-start | bytes 1572872 | tf_op jit(solution)/shard_map/ppermute | solution.py:394
  170.8 22.7 %all-to-all-start.3 = ((bf16[64,8,8,128]{3,2,1,0:T(8,128)(2,1)}), bf16[64,8,8,128]{3,2,1,0:T(8,128)(2,1)S(1)}, u32[]{:S(2)}, u32[]{:S(2)}) async-start(bf16[64,8,8,128]{3,2,1,0:T(8,128)(2,1)} %add_terms.1), calls=%async_computation.3 | async-start | bytes 2097152 | tf_op jit(solution)/shard_map/all_to_all | solution.py:384
  177.2 1.9 copy-start.3
  182.9 15.9 %copy-start.1 = (f32[512,512]{1,0:T(8,128)S(1)}, f32[512,512]{1,0:T(8,128)}, u32[]{:S(2)}) copy-start(f32[512,512]{1,0:T(8,128)} %get-tuple-element.64.near_v) | copy-start | bytes 3145732
  193.5 5.2 %collective-permute-start.6 = (bf16[32,8,8,128]{3,2,1,0:T(8,128)(2,1)S(1)}, bf16[32,8,8,128]{3,2,1,0:T(8,128)(2,1)S(1)}, u32[]{:S(2)}, u32[]{:S(2)}) collective-permute-start(bf16[32,8,8,128]{3,2,1,0:T(8,128)(2,1)S(1)} %constant_dynamic-slice_fusion), channel_id=1, source_target_pairs={{0,1},{1,0},{2,3},{3,2},{4,5},{5,4},{6,7},{7,6},{8,9},{9,8},{10,11... | collective-permute-start | bytes 1572872 | tf_op jit(solution)/shard_map/ppermute | solution.py:394

commit v5 on v4

--- a/solution.py
+++ b/solution.py
@@ -40,8 +40,7 @@
             second = jnp.maximum(table[row + 2 * h + 1], 0)
             for kv in range(2):
                 tile = kv * HALF + h
-                out[i, h, kv, :8] = shares[first, tile]
-                out[i, h, kv, 8:] = shares[second, tile]
+                out[i, h, kv] = jnp.concatenate([shares[first, tile], shares[second, tile]], axis=0)
         return carry
 
     lax.fori_loop(0, count, one, 0, unroll=8)
@@ -120,11 +119,11 @@
         for kv, (out, near) in enumerate(((grad_k, near_k), (grad_v, near_v))):
             for h in range(HALF):
                 tile = kv * HALF + h
-                term = far[:, tile].reshape(rows, HD).astype(f32)
+                term = far[:, tile].astype(f32).reshape(rows, HD)
                 if far is mine:
                     term += near[:, HD * h : HD * h + HD]
                 else:
-                    term += near_other[:, HD * tile : HD * tile + HD].astype(f32)
+                    term += near_other[kv, :, HD * h : HD * h + HD].astype(f32)
                 place = pl.ds(pl.multiple_of((side * HALF + h) * HD, HD), HD)
                 out[:, place] = term.astype(bf16)
 
@@ -142,7 +141,13 @@
         grid_spec=pltpu.PrefetchScalarGridSpec(
             num_scalar_prefetch=1,
             grid=(steps,),
-            in_specs=[far_mine, far, rows_mine, rows_mine, rows],
+            in_specs=[
+                far_mine,
+                far,
+                rows_mine,
+                rows_mine,
+                pl.BlockSpec((2, ROWS // steps, HALF * HD), lambda i, c: (0, i, 0)),
+            ],
             out_specs=[rows, rows],
         ),
         out_shape=[jax.ShapeDtypeStruct((ROWS, KVH * HD), bf16)] * 2,
@@ -333,12 +338,11 @@
     )(chosen, queries, cot_t, near_t, lse_t, far)
 
 
-def near_backward_kernel(
-    queries, cot_t, keys, values, stats, att_t, far_t, att, grad_q, grad_k, grad_v, keys_t, values_t, sum_k, sum_v
-):
+def near_backward_kernel(core, queries, cot_t, keys, values, stats, att_t, far_t, *refs):
+    att, att_other, q_mine, q_other, grad_k, grad_v, kv_other = refs[:7]
+    grad_q, keys_t, values_t, sum_k, sum_v = refs[7:]
     keys_t[...] = keys[...].T
     values_t[...] = values[...].T
-    att[...] = att_t[...].T
     sum_k[...] = jnp.zeros_like(sum_k)
     sum_v[...] = jnp.zeros_like(sum_v)
     columns = stats[...].T
@@ -359,25 +363,46 @@
             sum_k[:, :width] += dot(q, dscore, TN)
     grad_k[...] = sum_k[...].T * SCALE
     grad_v[...] = sum_v[...].T
-
-
-def near_backward(queries, cot_t, near, stats, att_t, far_t):
-    wide = pl.BlockSpec((BLOCK, GROUP * HD), lambda h: (0, h))
-    tall = pl.BlockSpec((GROUP * HD, BLOCK), lambda h: (h, 0))
-    key = pl.BlockSpec((BLOCK, HD), lambda h: (0, h))
-    value = pl.BlockSpec((BLOCK, HD), lambda h: (0, HALF + h))
+    for side in (0, 1):
+        mine = slice(ROWS * side, ROWS * side + ROWS)
+        other = slice(ROWS - ROWS * side, 2 * ROWS - ROWS * side)
+
+        @pl.when(core[0] == side)
+        def _():
+            att[...] = att_t[:, mine].T
+            att_other[...] = att_t[:, other].T
+            q_mine[...] = grad_q[mine]
+            q_other[...] = grad_q[other]
+            kv_other[0] = grad_k[other].astype(bf16)
+            kv_other[1] = grad_v[other].astype(bf16)
+
+
+def near_backward(core, queries, cot_t, near, stats, att_t, far_t):
+    wide = pl.BlockSpec((BLOCK, GROUP * HD), lambda h, c: (0, h))
+    part = pl.BlockSpec((ROWS, GROUP * HD), lambda h, c: (0, h))
+    tall = pl.BlockSpec((GROUP * HD, BLOCK), lambda h, c: (h, 0))
+    key = pl.BlockSpec((BLOCK, HD), lambda h, c: (0, h))
+    value = pl.BlockSpec((BLOCK, HD), lambda h, c: (0, HALF + h))
+    rows = pl.BlockSpec((8, BLOCK), lambda h, c: (h, 0))
+    both = pl.BlockSpec((2, ROWS, HD), lambda h, c: (0, 0, h))
     return pl.pallas_call(
         near_backward_kernel,
-        grid=(HALF,),
-        in_specs=[wide, tall, key, value, pl.BlockSpec((8, BLOCK), lambda h: (h, 0)), tall, tall],
-        out_specs=[wide, wide, key, key],
-        out_shape=[jax.ShapeDtypeStruct(queries.shape, bf16)] * 2
-        + [jax.ShapeDtypeStruct((BLOCK, HALF * HD), f32)] * 2,
-        scratch_shapes=[pltpu.VMEM((HD, BLOCK), bf16)] * 2 + [pltpu.VMEM((HD, BLOCK), f32)] * 2,
+        grid_spec=pltpu.PrefetchScalarGridSpec(
+            num_scalar_prefetch=1,
+            grid=(HALF,),
+            in_specs=[wide, tall, key, value, rows, tall, tall],
+            out_specs=[part] * 4 + [key, key, both],
+            scratch_shapes=[pltpu.VMEM((BLOCK, GROUP * HD), bf16)]
+            + [pltpu.VMEM((HD, BLOCK), bf16)] * 2
+            + [pltpu.VMEM((HD, BLOCK), f32)] * 2,
+        ),
+        out_shape=[jax.ShapeDtypeStruct((ROWS, queries.shape[1]), bf16)] * 4
+        + [jax.ShapeDtypeStruct((BLOCK, HALF * HD), f32)] * 2
+        + [jax.ShapeDtypeStruct((2, ROWS, HALF * HD), bf16)],
         compiler_params=pltpu.CompilerParams(vmem_limit_bytes=58 * 2**20),
         cost_estimate=cost(HALF, BLOCK * 3 // 4, 5),
         name="near_backward",
-    )(queries, cot_t, near, near, stats, att_t, far_t)
+    )(core.reshape(1), queries, cot_t, near, near, stats, att_t, far_t)
 
 
 def spread(x):
@@ -405,11 +430,6 @@
 def others_rows(x, core):
     half = x.shape[0] // 2
     return lax.dynamic_slice_in_dim(x, (1 - core) * half, half, 0)
-
-
-def my_rows(x, core):
-    half = x.shape[0] // 2
-    return lax.dynamic_slice_in_dim(x, core * half, half, 0)
 
 
 def per_device(queries, keys, values, cotangent, selected):
@@ -441,20 +461,17 @@
         chosen, block_q, cot_t, near_t, lse_t, far
     )
     back = spread(grad_far)
-    attended, grad_q, grad_k, grad_v = near_backward(block_q, cot_t, near, stats, att_t, far_t)
-    near_other = swap(
-        jnp.concatenate([others_rows(x, core).astype(bf16) for x in (grad_k, grad_v)], axis=1)
-    )
-    other_attended = swap(others_rows(attended, core))
-    other_q = swap(others_rows(grad_q, core))
-    back, grad_k, grad_v, near_other, attended, grad_q, other_attended, other_q = (
+    attended, other_attended, grad_q, other_q, grad_k, grad_v, near_other = near_backward(
+        core, block_q, cot_t, near, stats, att_t, far_t
+    )
+    back, attended, grad_q, grad_k, grad_v, other_attended, other_q, near_other = (
         lax.optimization_barrier(
-            (back, grad_k, grad_v, near_other, attended, grad_q, other_attended, other_q)
+            (back, attended, grad_q, grad_k, grad_v, swap(other_attended), swap(other_q), swap(near_other))
         )
     )
     summed = spread(add_terms(table, back))
-    attended = in_order(my_rows(attended, core), other_attended, core, 1)
-    grad_q = in_order(my_rows(grad_q, core), other_q, core, 1)
+    attended = in_order(attended, other_attended, core, 1)
+    grad_q = in_order(grad_q, other_q, core, 1)
     summed, attended, grad_q = lax.optimization_barrier((summed, attended, grad_q))
     other = swap(others_rows(summed, core))
     grad_k, grad_v = finish(core, summed, other, grad_k, grad_v, near_other)

time: 202 us -> 202 us (level)
  waiting for transfers between devices: 26.8 us -> 31.3 us
  local copies, waits for them, and re-layouts: 9.43 us -> 6.93 us
  other arithmetic: 9.59 us -> 7.22 us
    unnamed x16 -> x28, local copies, waits for them, and re-layouts: 0.48 us -> 5.3 us
    dynamic_slice x3 -> x1, local copies, waits for them, and re-layouts: 3.53 us -> 0.03 us  [others_rows(): return lax.dynamic_slice_in_dim(x, (1 - core) * half, half, 0)]
    ppermute x7, waiting for transfers between devices: 7.11 us -> 10.2 us  [swap(): return lax.ppermute(x, 'ctx', PAIR)]
  transfers between devices with their start and end apart: 10 -> 10, of which waited for: 8 -> 8; matrix products, arithmetic and copies ran while one was open for 8% -> 3% of each run, Pallas kernels for 13% -> 14%
where the time goes in v5:
time: 202 us; the launch traced here: 201 us
  Pallas kernels  65.3 us (32%)
  starting transfers between devices  59.2 us (29%)
  waiting for transfers between devices  31.3 us (15%)
  blocking collectives  30.4 us (15%)
  other arithmetic  7.22 us (4%)
  local copies, waits for them, and re-layouts  6.93 us (3%)
    all_to_all x3, starting transfers between devices, spread(): lax.all_to_all(x, 'ctx', 0, 0, axis_index_groups=SAME_HALF, tiled=True)  49.4 us
    pallas_call x1, Pallas kernels, far_attention(): pl.pallas_call(far_kernel, grid_spec=pltpu.PrefetchScalarGridSpec(num_sca...  31.1 us
    all_to_all x1, blocking collectives, spread(): lax.all_to_all(x, 'ctx', 0, 0, axis_index_groups=SAME_HALF, tiled=True)  30.4 us
    all_to_all x3, waiting for transfers between devices, spread(): lax.all_to_all(x, 'ctx', 0, 0, axis_index_groups=SAME_HALF, tiled=True)  21 us
    pallas_call x1, Pallas kernels, near_backward(): pl.pallas_call(near_backward_kernel, grid_spec=pltpu.PrefetchScalarGridSp...  15.3 us
    pallas_call x1, Pallas kernels, near_forward(): pl.pallas_call(near_forward_kernel, grid_spec=pltpu.PrefetchScalarGridSpe...  12.4 us
    ppermute x7, waiting for transfers between devices, swap(): return lax.ppermute(x, 'ctx', PAIR)  10.2 us
    ppermute x7, starting transfers between devices, swap(): return lax.ppermute(x, 'ctx', PAIR)  9.81 us
  transfers between devices with their start and end apart: 10, of which 8 were waited for; matrix products, arithmetic and copies ran while one was open for 3% of the time, Pallas kernels for 14%

profile of v5, /device:TPU:1, one launch (start us, length us, event | category | flops | bytes accessed | tf_op | source)
XLA Modules:
  0.0 201.2 jit_solution(7538316705658419741)
XLA Ops:
  0.6 0.0 copy-start.11
  0.7 1.3 constant_dynamic-slice_fusion.5
  1.9 0.1 pad_maximum_fusion.1
  2.0 1.5 collective-permute-start
  3.5 0.0 copy-done.11
  3.5 1.5 collective-permute-done
  5.0 0.4 maximum_select_fusion.2.keys.values
  5.5 0.0 copy-start.4
  5.5 0.1 pad_maximum_fusion
  5.7 30.4 %all_to_all.20.shares = bf16[64,9,8,128]{3,2,1,0:T(8,128)(2,1)S(1)} all-to-all(bf16[64,9,8,128]{3,2,1,0:T(8,128)(2,1)S(1)} %pad_maximum_fusion), channel_id=1, replica_groups={{0,2,4,6,8,10,12,14,16,18,20,22,24,26,28,30,32,34,36,38,40,42,44,46,48,..., dimensions={0} | all-to-all | bytes 2359296 | tf_op jit(solution)/shard_map/all_to_all | solution.py:409
  36.1 0.0 copy-done.4
  36.1 0.1 slice_select_fusion
  36.2 0.1 reshape.28.table
  36.3 2.5 %pick.1 = bf16[64,4,2,16,128]{4,3,2,1,0:T(8,128)(2,1)} custom-call(s32[512]{0:T(512)S(1)} %reshape.28.table, bf16[64,9,8,128]{3,2,1,0:T(8,128)(2,1)S(1)} %all_to_all.20.shares), custom_call_target="tpu_custom_call" | custom-call | tf_op jit(solution)/shard_map/pick/pallas_call | solution.py:51
  38.8 0.0 copy-start.9
  38.8 5.7 %all-to-all-start.1 = ((bf16[64,4,2,16,128]{4,3,2,1,0:T(8,128)(2,1)}), bf16[64,4,2,16,128]{4,3,2,1,0:T(8,128)(2,1)}, u32[]{:S(2)}, u32[]{:S(2)}) async-start(bf16[64,4,2,16,128]{4,3,2,1,0:T(8,128)(2,1)} %pick.1), calls=%async_computation.1 | async-start | bytes 4194304 | tf_op jit(solution)/shard_map/all_to_all | solution.py:409
  44.5 0.0 copy-done.9
  44.5 0.0 copy-start.10
  44.5 0.1 constant_dynamic-slice_fusion.2
  44.6 1.5 copy-done.10
  46.1 0.1 constant_dynamic-slice_fusion.1
  46.2 1.9 collective-permute-start.2
  48.1 0.1 collective-permute-start.1
  48.2 0.6 fusion.chosen
  48.8 1.6 collective-permute-done.2.got_cot
  50.4 0.0 copy-start.12
  50.4 1.5 collective-permute-done.1.got_q
  51.9 0.0 copy-start.13
  51.9 1.0 copy-done.13
  52.9 0.0 copy-done.12
  52.9 12.4 %near_forward.1 = (f32[2048,512]{1,0:T(8,128)}, f32[32,512]{1,0:T(8,128)}, bf16[512,2048]{1,0:T(8,128)(2,1)}, bf16[2048,512]{1,0:T(8,128)(2,1)}) custom-call(s32[1]{0:T(128)} %bitcast.4.core, bf16[256,4096]{1,0:T(8,128)(2,1)} %my_q, bf16[256,2048]{1,0:T(8,128)(2,1)} %copy-done.13, bf16[256,4096]{1,0:T(8,128)(2,1)} %my_cot, bf16[256,2048]{1,0:T(8,128)(2,1)} %copy-done.12, ...), custom_call_target="tpu_custom_call" | custom-call | flops 3221225472 | bytes 20971520 | tf_op jit(solution)/shard_map/near_forward/pallas_call | solution.py:229
  65.3 6.9 %all-to-all-done.1.far = bf16[64,4,2,16,128]{4,3,2,1,0:T(8,128)(2,1)} async-done(((bf16[64,4,2,16,128]{4,3,2,1,0:T(8,128)(2,1)}), bf16[64,4,2,16,128]{4,3,2,1,0:T(8,128)(2,1)}, u32[]{:S(2)}, u32[]{:S(2)}) %all-to-all-start.1) | async-done | bytes 2097184 | tf_op jit(solution)/shard_map/all_to_all | solution.py:409
  72.2 31.1 %far_attention.1 = (bf16[2048,512]{1,0:T(8,128)(2,1)}, f32[2048,512]{1,0:T(8,128)}, f32[32,512]{1,0:T(8,128)}, bf16[64,4,2,16,128]{4,3,2,1,0:T(8,128)(2,1)}) custom-call(s32[8]{0:T(128)} %fusion.chosen, bf16[512,2048]{1,0:T(8,128)(2,1)} %get-tuple-element.41.queries, bf16[2048,512]{1,0:T(8,128)(2,1)} %get-tuple-element.46.cot_t, ...), custom_call_target="tpu_custom_call" | custom-call | flops 25769803776 | bytes 20971520 | tf_op jit(solution)/shard_map/far_attention/pallas_call | solution.py:320
  103.3 37.2 %all-to-all-start.2 = ((bf16[64,4,2,16,128]{4,3,2,1,0:T(8,128)(2,1)}), bf16[64,4,2,16,128]{4,3,2,1,0:T(8,128)(2,1)S(1)}, u32[]{:S(2)}, u32[]{:S(2)}) async-start(bf16[64,4,2,16,128]{4,3,2,1,0:T(8,128)(2,1)} %get-tuple-element.50), calls=%async_computation.2 | async-start | bytes 4194304 | tf_op jit(solution)/shard_map/all_to_all | solution.py:409
  140.6 15.3 %near_backward.1 = (bf16[256,2048]{1,0:T(8,128)(2,1)}, bf16[256,2048]{1,0:T(8,128)(2,1)}, bf16[256,2048]{1,0:T(8,128)(2,1)}, bf16[256,2048]{1,0:T(8,128)(2,1)}, ...) custom-call(s32[1]{0:T(128)} %bitcast.4.core, bf16[512,2048]{1,0:T(8,128)(2,1)} %get-tuple-element.41.queries, ...), custom_call_target="tpu_custom_call" | custom-call | flops 8053063680 | bytes 20971520 | tf_op jit(solution)/shard_map/near_backward/pallas_call | solution.py:388
  155.9 2.0 %collective-permute-start.3 = (bf16[256,2048]{1,0:T(8,128)(2,1)}, bf16[256,2048]{1,0:T(8,128)(2,1)S(1)}, u32[]{:S(2)}, u32[]{:S(2)}) collective-permute-start(bf16[256,2048]{1,0:T(8,128)(2,1)} %get-tuple-element.58), channel_id=1, source_target_pairs={{0,1},{1,0},{2,3},{3,2},{4,5},{5,4},{6,7},{7,6},{8,9},{9,8},{10,11... | collective-permute-start | bytes 3145736 | tf_op jit(solution)/shard_map/ppermute | solution.py:419
  157.9 0.1 collective-permute-start.4
  158.0 0.4 collective-permute-start.5
  158.4 4.1 %collective-permute-done.5.near_other = bf16[2,256,512]{2,1,0:T(8,128)(2,1)S(1)} collective-permute-done((bf16[2,256,512]{2,1,0:T(8,128)(2,1)}, bf16[2,256,512]{2,1,0:T(8,128)(2,1)S(1)}, u32[]{:S(2)}, u32[]{:S(2)}) %collective-permute-start.5) | collective-permute-done | bytes 524320 | tf_op jit(solution)/shard_map/ppermute | solution.py:419
  162.5 0.0 copy-start.2
  162.5 0.8 copy-done.2
  163.3 0.0 collective-permute-done.3
  163.3 0.0 copy-start.7
  163.3 1.0 copy-done.7
  164.3 0.0 collective-permute-done.4
  164.3 3.9 %all-to-all-done.2.terms = bf16[64,4,2,16,128]{4,3,2,1,0:T(8,128)(2,1)S(1)} async-done(((bf16[64,4,2,16,128]{4,3,2,1,0:T(8,128)(2,1)}), bf16[64,4,2,16,128]{4,3,2,1,0:T(8,128)(2,1)S(1)}, u32[]{:S(2)}, u32[]{:S(2)}) %all-to-all-start.2) | async-done | bytes 2097184 | tf_op jit(solution)/shard_map/all_to_all | solution.py:409
  168.2 0.0 copy-start.6
  168.2 2.8 %add_terms.1 = bf16[64,8,8,128]{3,2,1,0:T(8,128)(2,1)} custom-call(s32[512]{0:T(512)S(1)} %reshape.28.table, bf16[64,4,2,16,128]{4,3,2,1,0:T(8,128)(2,1)S(1)} %all-to-all-done.2.terms), custom_call_target="tpu_custom_call" | custom-call | tf_op jit(solution)/shard_map/add_terms/pallas_call | solution.py:101
  171.0 0.0 copy-start.8
  171.0 6.4 %all-to-all-start.3 = ((bf16[64,8,8,128]{3,2,1,0:T(8,128)(2,1)}), bf16[64,8,8,128]{3,2,1,0:T(8,128)(2,1)S(1)}, u32[]{:S(2)}, u32[]{:S(2)}) async-start(bf16[64,8,8,128]{3,2,1,0:T(8,128)(2,1)} %add_terms.1), calls=%async_computation.3 | async-start | bytes 2097152 | tf_op jit(solution)/shard_map/all_to_all | solution.py:409
  177.4 0.0 copy-done.6
  177.4 0.0 copy-done.8
  177.5 0.0 copy-start.5
  177.5 2.1 %maximum_select_fusion = bf16[256,4096]{1,0:T(8,128)(2,1)} fusion(bf16[256,2048]{1,0:T(8,128)(2,1)S(1)} %copy-done.8, bf16[256,2048]{1,0:T(8,128)(2,1)S(1)} %copy-done.6, pred[]{:T(512)S(6)} %eq.4), kind=kLoop, calls=%fused_computation | loop fusion | flops 9437184 | bytes 4194305 | tf_op jit(solution)/shard_map/jit(_where)/select_n | solution.py:423
  179.6 0.0 copy-done.5
  179.6 0.0 copy-start
  179.6 3.8 %maximum_select_fusion.1 = bf16[256,4096]{1,0:T(8,128)(2,1)} fusion(bf16[256,2048]{1,0:T(8,128)(2,1)} %collective-permute-done.4, bf16[256,2048]{1,0:T(8,128)(2,1)S(1)} %copy-done.5, pred[]{:T(512)S(6)} %eq.4), kind=kLoop, calls=%fused_computation.1 | loop fusion | flops 9437184 | bytes 4194305 | tf_op jit(solution)/shard_map/jit(_where)/select_n | solution.py:423
  183.4 10.2 %all-to-all-done.3.mine = bf16[64,8,8,128]{3,2,1,0:T(8,128)(2,1)S(1)} async-done(((bf16[64,8,8,128]{3,2,1,0:T(8,128)(2,1)}), bf16[64,8,8,128]{3,2,1,0:T(8,128)(2,1)S(1)}, u32[]{:S(2)}, u32[]{:S(2)}) %all-to-all-start.3) | async-done | bytes 1048608 | tf_op jit(solution)/shard_map/all_to_all | solution.py:409
  193.6 3.8 %collective-permute-start.6 = (bf16[32,8,8,128]{3,2,1,0:T(8,128)(2,1)S(1)}, bf16[32,8,8,128]{3,2,1,0:T(8,128)(2,1)S(1)}, u32[]{:S(2)}, u32[]{:S(2)}) collective-permute-start(bf16[32,8,8,128]{3,2,1,0:T(8,128)(2,1)S(1)} %constant_dynamic-slice_fusion), channel_id=1, source_target_pairs={{0,1},{1,0},{2,3},{3,2},{4,5},{5,4},{6,7},{7,6},{8,9},{9,8},{10,11... | collective-permute-start | bytes 1572872 | tf_op jit(solution)/shard_map/ppermute | solution.py:419
  197.4 1.5 collective-permute-done.6.other
  198.9 0.0 copy-done
  198.9 0.0 copy-done.1
  198.9 1.0 copy-done.3
  200.0 1.2 finish.1
  (7 shorter events, 0.1 us)
Async XLA Ops:
  0.6 2.9 %copy-start.11 = (s32[1,16]{1,0:T(1,128)S(1)}, s32[1,16]{1,0:T(1,128)}, u32[]{:S(2)}) copy-start(s32[1,16]{1,0:T(1,128)} %param.9) | copy-start | bytes 196
  2.0 3.0 %collective-permute-start = (bf16[256,1024]{1,0:T(8,128)(2,1)S(1)}, bf16[256,1024]{1,0:T(8,128)(2,1)S(1)}, u32[]{:S(2)}, u32[]{:S(2)}) collective-permute-start(bf16[256,1024]{1,0:T(8,128)(2,1)S(1)} %pad_maximum_fusion.1), channel_id=1, source_target_pairs={{0,1},{1,0},{2,3},{3,2},{4,5},{5,4},{6,7},{7,6},{8,9},{9,8},{10,11... | collective-permute-start | bytes 1572872 | tf_op jit(solution)/shard_map/ppermute | solution.py:419
  5.5 30.6 %copy-start.4 = (bf16[512,1024]{1,0:T(8,128)(2,1)}, bf16[512,1024]{1,0:T(8,128)(2,1)S(1)}, u32[]{:S(2)}) copy-start(bf16[512,1024]{1,0:T(8,128)(2,1)S(1)} %maximum_select_fusion.2.keys.values) | copy-start | bytes 3145732
  38.8 5.7 %copy-start.9 = (bf16[256,4096]{1,0:T(8,128)(2,1)S(1)}, bf16[256,4096]{1,0:T(8,128)(2,1)}, u32[]{:S(2)}) copy-start(bf16[256,4096]{1,0:T(8,128)(2,1)} %my_q) | copy-start | bytes 6291460
  38.8 33.4 %all-to-all-start.1 = ((bf16[64,4,2,16,128]{4,3,2,1,0:T(8,128)(2,1)}), bf16[64,4,2,16,128]{4,3,2,1,0:T(8,128)(2,1)}, u32[]{:S(2)}, u32[]{:S(2)}) async-start(bf16[64,4,2,16,128]{4,3,2,1,0:T(8,128)(2,1)} %pick.1), calls=%async_computation.1 | async-start | bytes 4194304 | tf_op jit(solution)/shard_map/all_to_all | solution.py:409
  44.5 1.6 copy-start.10
  46.2 4.2 %collective-permute-start.2 = (bf16[256,2048]{1,0:T(8,128)(2,1)S(1)}, bf16[256,2048]{1,0:T(8,128)(2,1)S(1)}, u32[]{:S(2)}, u32[]{:S(2)}) collective-permute-start(bf16[256,2048]{1,0:T(8,128)(2,1)S(1)} %constant_dynamic-slice_fusion.1), channel_id=1, source_target_pairs={{0,1},{1,0},{2,3},{3,2},{4,5},{5,4},{6,7},{7,6},{8,9},{9,8},{10,11... | collective-permute-start | bytes 3145736 | tf_op jit(solution)/shard_map/ppermute | solution.py:419
  48.1 3.8 %collective-permute-start.1 = (bf16[256,2048]{1,0:T(8,128)(2,1)S(1)}, bf16[256,2048]{1,0:T(8,128)(2,1)S(1)}, u32[]{:S(2)}, u32[]{:S(2)}) collective-permute-start(bf16[256,2048]{1,0:T(8,128)(2,1)S(1)} %constant_dynamic-slice_fusion.2), channel_id=1, source_target_pairs={{0,1},{1,0},{2,3},{3,2},{4,5},{5,4},{6,7},{7,6},{8,9},{9,8},{10,11... | collective-permute-start | bytes 3145736 | tf_op jit(solution)/shard_map/ppermute | solution.py:419
  50.4 2.5 %copy-start.12 = (bf16[256,2048]{1,0:T(8,128)(2,1)}, bf16[256,2048]{1,0:T(8,128)(2,1)S(1)}, u32[]{:S(2)}) copy-start(bf16[256,2048]{1,0:T(8,128)(2,1)S(1)} %collective-permute-done.2.got_cot) | copy-start | bytes 3145732
  51.9 1.0 copy-start.13
  103.3 64.8 %all-to-all-start.2 = ((bf16[64,4,2,16,128]{4,3,2,1,0:T(8,128)(2,1)}), bf16[64,4,2,16,128]{4,3,2,1,0:T(8,128)(2,1)S(1)}, u32[]{:S(2)}, u32[]{:S(2)}) async-start(bf16[64,4,2,16,128]{4,3,2,1,0:T(8,128)(2,1)} %get-tuple-element.50), calls=%async_computation.2 | async-start | bytes 4194304 | tf_op jit(solution)/shard_map/all_to_all | solution.py:409
  155.9 7.4 %collective-permute-start.3 = (bf16[256,2048]{1,0:T(8,128)(2,1)}, bf16[256,2048]{1,0:T(8,128)(2,1)S(1)}, u32[]{:S(2)}, u32[]{:S(2)}) collective-permute-start(bf16[256,2048]{1,0:T(8,128)(2,1)} %get-tuple-element.58), channel_id=1, source_target_pairs={{0,1},{1,0},{2,3},{3,2},{4,5},{5,4},{6,7},{7,6},{8,9},{9,8},{10,11... | collective-permute-start | bytes 3145736 | tf_op jit(solution)/shard_map/ppermute | solution.py:419
  157.9 6.3 %collective-permute-start.4 = (bf16[256,2048]{1,0:T(8,128)(2,1)}, bf16[256,2048]{1,0:T(8,128)(2,1)}, u32[]{:S(2)}, u32[]{:S(2)}) collective-permute-start(bf16[256,2048]{1,0:T(8,128)(2,1)} %get-tuple-element.59), channel_id=1, source_target_pairs={{0,1},{1,0},{2,3},{3,2},{4,5},{5,4},{6,7},{7,6},{8,9},{9,8},{10,11... | collective-permute-start | bytes 3145736 | tf_op jit(solution)/shard_map/ppermute | solution.py:419
  158.0 4.5 %collective-permute-start.5 = (bf16[2,256,512]{2,1,0:T(8,128)(2,1)}, bf16[2,256,512]{2,1,0:T(8,128)(2,1)S(1)}, u32[]{:S(2)}, u32[]{:S(2)}) collective-permute-start(bf16[2,256,512]{2,1,0:T(8,128)(2,1)} %get-tuple-element.60), channel_id=1, source_target_pairs={{0,1},{1,0},{2,3},{3,2},{4,5},{5,4},{6,7},{7,6},{8,9},{9,8},{10,11... | collective-permute-start | bytes 1572872 | tf_op jit(solution)/shard_map/ppermute | solution.py:419
  162.5 0.8 copy-start.2
  163.3 1.0 copy-start.7
  168.2 9.2 %copy-start.6 = (bf16[256,2048]{1,0:T(8,128)(2,1)S(1)}, bf16[256,2048]{1,0:T(8,128)(2,1)}, u32[]{:S(2)}) copy-start(bf16[256,2048]{1,0:T(8,128)(2,1)} %get-tuple-element.62) | copy-start | bytes 3145732
  171.0 6.5 %copy-start.8 = (bf16[256,2048]{1,0:T(8,128)(2,1)S(1)}, bf16[256,2048]{1,0:T(8,128)(2,1)}, u32[]{:S(2)}) copy-start(bf16[256,2048]{1,0:T(8,128)(2,1)} %copy-done.7) | copy-start | bytes 3145732
  171.0 22.6 %all-to-all-start.3 = ((bf16[64,8,8,128]{3,2,1,0:T(8,128)(2,1)}), bf16[64,8,8,128]{3,2,1,0:T(8,128)(2,1)S(1)}, u32[]{:S(2)}, u32[]{:S(2)}) async-start(bf16[64,8,8,128]{3,2,1,0:T(8,128)(2,1)} %add_terms.1), calls=%async_computation.3 | async-start | bytes 2097152 | tf_op jit(solution)/shard_map/all_to_all | solution.py:409
  177.5 2.1 %copy-start.5 = (bf16[256,2048]{1,0:T(8,128)(2,1)S(1)}, bf16[256,2048]{1,0:T(8,128)(2,1)}, u32[]{:S(2)}) copy-start(bf16[256,2048]{1,0:T(8,128)(2,1)} %get-tuple-element.64) | copy-start | bytes 3145732
  179.6 19.4 %copy-start = (f32[512,512]{1,0:T(8,128)S(1)}, f32[512,512]{1,0:T(8,128)}, u32[]{:S(2)}) copy-start(f32[512,512]{1,0:T(8,128)} %get-tuple-element.69.near_k) | copy-start | bytes 3145732
  179.6 19.4 %copy-start.1 = (f32[512,512]{1,0:T(8,128)S(1)}, f32[512,512]{1,0:T(8,128)}, u32[]{:S(2)}) copy-start(f32[512,512]{1,0:T(8,128)} %get-tuple-element.70.near_v) | copy-start | bytes 3145732
  193.6 5.3 %collective-permute-start.6 = (bf16[32,8,8,128]{3,2,1,0:T(8,128)(2,1)S(1)}, bf16[32,8,8,128]{3,2,1,0:T(8,128)(2,1)S(1)}, u32[]{:S(2)}, u32[]{:S(2)}) collective-permute-start(bf16[32,8,8,128]{3,2,1,0:T(8,128)(2,1)S(1)} %constant_dynamic-slice_fusion), channel_id=1, source_target_pairs={{0,1},{1,0},{2,3},{3,2},{4,5},{5,4},{6,7},{7,6},{8,9},{9,8},{10,11... | collective-permute-start | bytes 1572872 | tf_op jit(solution)/shard_map/ppermute | solution.py:419
  198.9 1.0 copy-start.3

commit v6 on v5

--- a/solution.py
+++ b/solution.py
@@ -95,7 +95,7 @@
 
 
 def add_terms(table, terms):
-    count = 16
+    count = 64
     tiles = 2 * terms.shape[1]
     whole = lambda i, t: (0, 0, 0, 0)
     return pl.pallas_call(

time: 202 us -> 202 us (level)
  no operation moved by 1% of the time
where the time goes in v6:
time: 202 us; the launch traced here: 201 us
  Pallas kernels  65.2 us (32%)
  starting transfers between devices  59 us (29%)
  waiting for transfers between devices  31.4 us (16%)
  blocking collectives  30.4 us (15%)
  other arithmetic  7.22 us (4%)
  local copies, waits for them, and re-layouts  6.93 us (3%)
    all_to_all x3, starting transfers between devices, spread(): lax.all_to_all(x, 'ctx', 0, 0, axis_index_groups=SAME_HALF, tiled=True)  49.3 us
    pallas_call x1, Pallas kernels, far_attention(): pl.pallas_call(far_kernel, grid_spec=pltpu.PrefetchScalarGridSpec(num_sca...  31.1 us
    all_to_all x1, blocking collectives, spread(): lax.all_to_all(x, 'ctx', 0, 0, axis_index_groups=SAME_HALF, tiled=True)  30.4 us
    all_to_all x3, waiting for transfers between devices, spread(): lax.all_to_all(x, 'ctx', 0, 0, axis_index_groups=SAME_HALF, tiled=True)  21.2 us
    pallas_call x1, Pallas kernels, near_backward(): pl.pallas_call(near_backward_kernel, grid_spec=pltpu.PrefetchScalarGridSp...  15.3 us
    pallas_call x1, Pallas kernels, near_forward(): pl.pallas_call(near_forward_kernel, grid_spec=pltpu.PrefetchScalarGridSpe...  12.4 us
    ppermute x7, waiting for transfers between devices, swap(): return lax.ppermute(x, 'ctx', PAIR)  10.2 us
    ppermute x7, starting transfers between devices, swap(): return lax.ppermute(x, 'ctx', PAIR)  9.67 us
  transfers between devices with their start and end apart: 10, of which 8 were waited for; matrix products, arithmetic and copies ran while one was open for 3% of the time, Pallas kernels for 14%

profile of v6, /device:TPU:1, one launch (start us, length us, event | category | flops | bytes accessed | tf_op | source)
XLA Modules:
  0.0 201.1 jit_solution(4119509671861886109)
XLA Ops:
  0.6 0.0 copy-start.11
  0.7 1.3 constant_dynamic-slice_fusion.5
  1.9 0.1 pad_maximum_fusion.1
  2.0 1.5 collective-permute-start
  3.5 0.0 copy-done.11
  3.5 1.5 collective-permute-done
  5.0 0.4 maximum_select_fusion.2.keys.values
  5.5 0.0 copy-start.4
  5.5 0.1 pad_maximum_fusion
  5.7 30.4 %all_to_all.20.shares = bf16[64,9,8,128]{3,2,1,0:T(8,128)(2,1)S(1)} all-to-all(bf16[64,9,8,128]{3,2,1,0:T(8,128)(2,1)S(1)} %pad_maximum_fusion), channel_id=1, replica_groups={{0,2,4,6,8,10,12,14,16,18,20,22,24,26,28,30,32,34,36,38,40,42,44,46,48,..., dimensions={0} | all-to-all | bytes 2359296 | tf_op jit(solution)/shard_map/all_to_all | solution.py:409
  36.1 0.0 copy-done.4
  36.1 0.1 slice_select_fusion
  36.2 0.1 reshape.28.table
  36.3 2.5 %pick.1 = bf16[64,4,2,16,128]{4,3,2,1,0:T(8,128)(2,1)} custom-call(s32[512]{0:T(512)S(1)} %reshape.28.table, bf16[64,9,8,128]{3,2,1,0:T(8,128)(2,1)S(1)} %all_to_all.20.shares), custom_call_target="tpu_custom_call" | custom-call | tf_op jit(solution)/shard_map/pick/pallas_call | solution.py:51
  38.8 0.0 copy-start.9
  38.8 5.7 %all-to-all-start.1 = ((bf16[64,4,2,16,128]{4,3,2,1,0:T(8,128)(2,1)}), bf16[64,4,2,16,128]{4,3,2,1,0:T(8,128)(2,1)}, u32[]{:S(2)}, u32[]{:S(2)}) async-start(bf16[64,4,2,16,128]{4,3,2,1,0:T(8,128)(2,1)} %pick.1), calls=%async_computation.1 | async-start | bytes 4194304 | tf_op jit(solution)/shard_map/all_to_all | solution.py:409
  44.5 0.0 copy-done.9
  44.5 0.0 copy-start.10
  44.5 0.1 constant_dynamic-slice_fusion.2
  44.6 1.5 copy-done.10
  46.1 0.1 constant_dynamic-slice_fusion.1
  46.2 1.9 collective-permute-start.2
  48.1 0.1 collective-permute-start.1
  48.2 0.6 fusion.chosen
  48.8 1.6 collective-permute-done.2.got_cot
  50.4 0.0 copy-start.12
  50.4 1.5 collective-permute-done.1.got_q
  51.9 0.0 copy-start.13
  51.9 1.0 copy-done.13
  52.9 0.0 copy-done.12
  52.9 12.4 %near_forward.1 = (f32[2048,512]{1,0:T(8,128)}, f32[32,512]{1,0:T(8,128)}, bf16[512,2048]{1,0:T(8,128)(2,1)}, bf16[2048,512]{1,0:T(8,128)(2,1)}) custom-call(s32[1]{0:T(128)} %bitcast.4.core, bf16[256,4096]{1,0:T(8,128)(2,1)} %my_q, bf16[256,2048]{1,0:T(8,128)(2,1)} %copy-done.13, bf16[256,4096]{1,0:T(8,128)(2,1)} %my_cot, bf16[256,2048]{1,0:T(8,128)(2,1)} %copy-done.12, ...), custom_call_target="tpu_custom_call" | custom-call | flops 3221225472 | bytes 20971520 | tf_op jit(solution)/shard_map/near_forward/pallas_call | solution.py:229
  65.3 6.9 %all-to-all-done.1.far = bf16[64,4,2,16,128]{4,3,2,1,0:T(8,128)(2,1)} async-done(((bf16[64,4,2,16,128]{4,3,2,1,0:T(8,128)(2,1)}), bf16[64,4,2,16,128]{4,3,2,1,0:T(8,128)(2,1)}, u32[]{:S(2)}, u32[]{:S(2)}) %all-to-all-start.1) | async-done | bytes 2097184 | tf_op jit(solution)/shard_map/all_to_all | solution.py:409
  72.2 31.1 %far_attention.1 = (bf16[2048,512]{1,0:T(8,128)(2,1)}, f32[2048,512]{1,0:T(8,128)}, f32[32,512]{1,0:T(8,128)}, bf16[64,4,2,16,128]{4,3,2,1,0:T(8,128)(2,1)}) custom-call(s32[8]{0:T(128)} %fusion.chosen, bf16[512,2048]{1,0:T(8,128)(2,1)} %get-tuple-element.41.queries, bf16[2048,512]{1,0:T(8,128)(2,1)} %get-tuple-element.46.cot_t, ...), custom_call_target="tpu_custom_call" | custom-call | flops 25769803776 | bytes 20971520 | tf_op jit(solution)/shard_map/far_attention/pallas_call | solution.py:320
  103.3 37.1 %all-to-all-start.2 = ((bf16[64,4,2,16,128]{4,3,2,1,0:T(8,128)(2,1)}), bf16[64,4,2,16,128]{4,3,2,1,0:T(8,128)(2,1)S(1)}, u32[]{:S(2)}, u32[]{:S(2)}) async-start(bf16[64,4,2,16,128]{4,3,2,1,0:T(8,128)(2,1)} %get-tuple-element.50), calls=%async_computation.2 | async-start | bytes 4194304 | tf_op jit(solution)/shard_map/all_to_all | solution.py:409
  140.4 15.3 %near_backward.1 = (bf16[256,2048]{1,0:T(8,128)(2,1)}, bf16[256,2048]{1,0:T(8,128)(2,1)}, bf16[256,2048]{1,0:T(8,128)(2,1)}, bf16[256,2048]{1,0:T(8,128)(2,1)}, ...) custom-call(s32[1]{0:T(128)} %bitcast.4.core, bf16[512,2048]{1,0:T(8,128)(2,1)} %get-tuple-element.41.queries, ...), custom_call_target="tpu_custom_call" | custom-call | flops 8053063680 | bytes 20971520 | tf_op jit(solution)/shard_map/near_backward/pallas_call | solution.py:388
  155.7 1.9 collective-permute-start.3
  157.6 0.1 collective-permute-start.4
  157.7 0.4 collective-permute-start.5
  158.1 4.1 %collective-permute-done.5.near_other = bf16[2,256,512]{2,1,0:T(8,128)(2,1)S(1)} collective-permute-done((bf16[2,256,512]{2,1,0:T(8,128)(2,1)}, bf16[2,256,512]{2,1,0:T(8,128)(2,1)S(1)}, u32[]{:S(2)}, u32[]{:S(2)}) %collective-permute-start.5) | collective-permute-done | bytes 524320 | tf_op jit(solution)/shard_map/ppermute | solution.py:419
  162.2 0.0 copy-start.2
  162.2 0.8 copy-done.2
  163.0 0.0 collective-permute-done.3
  163.0 0.0 copy-start.7
  163.0 1.0 copy-done.7
  164.0 0.0 collective-permute-done.4
  164.0 4.1 %all-to-all-done.2.terms = bf16[64,4,2,16,128]{4,3,2,1,0:T(8,128)(2,1)S(1)} async-done(((bf16[64,4,2,16,128]{4,3,2,1,0:T(8,128)(2,1)}), bf16[64,4,2,16,128]{4,3,2,1,0:T(8,128)(2,1)S(1)}, u32[]{:S(2)}, u32[]{:S(2)}) %all-to-all-start.2) | async-done | bytes 2097184 | tf_op jit(solution)/shard_map/all_to_all | solution.py:409
  168.0 0.0 copy-start.6
  168.0 2.7 %add_terms.1 = bf16[64,8,8,128]{3,2,1,0:T(8,128)(2,1)} custom-call(s32[512]{0:T(512)S(1)} %reshape.28.table, bf16[64,4,2,16,128]{4,3,2,1,0:T(8,128)(2,1)S(1)} %all-to-all-done.2.terms), custom_call_target="tpu_custom_call" | custom-call | tf_op jit(solution)/shard_map/add_terms/pallas_call | solution.py:101
  170.7 0.0 copy-start.8
  170.7 6.6 %all-to-all-start.3 = ((bf16[64,8,8,128]{3,2,1,0:T(8,128)(2,1)}), bf16[64,8,8,128]{3,2,1,0:T(8,128)(2,1)S(1)}, u32[]{:S(2)}, u32[]{:S(2)}) async-start(bf16[64,8,8,128]{3,2,1,0:T(8,128)(2,1)} %add_terms.1), calls=%async_computation.3 | async-start | bytes 2097152 | tf_op jit(solution)/shard_map/all_to_all | solution.py:409
  177.3 0.0 copy-done.6
  177.3 0.0 copy-done.8
  177.3 0.0 copy-start.5
  177.3 2.1 %maximum_select_fusion = bf16[256,4096]{1,0:T(8,128)(2,1)} fusion(bf16[256,2048]{1,0:T(8,128)(2,1)S(1)} %copy-done.8, bf16[256,2048]{1,0:T(8,128)(2,1)S(1)} %copy-done.6, pred[]{:T(512)S(6)} %eq.4), kind=kLoop, calls=%fused_computation | loop fusion | flops 9437184 | bytes 4194305 | tf_op jit(solution)/shard_map/jit(_where)/select_n | solution.py:423
  179.4 0.0 copy-done.5
  179.4 0.0 copy-start
  179.4 3.8 %maximum_select_fusion.1 = bf16[256,4096]{1,0:T(8,128)(2,1)} fusion(bf16[256,2048]{1,0:T(8,128)(2,1)} %collective-permute-done.4, bf16[256,2048]{1,0:T(8,128)(2,1)S(1)} %copy-done.5, pred[]{:T(512)S(6)} %eq.4), kind=kLoop, calls=%fused_computation.1 | loop fusion | flops 9437184 | bytes 4194305 | tf_op jit(solution)/shard_map/jit(_where)/select_n | solution.py:423
  183.3 10.2 %all-to-all-done.3.mine = bf16[64,8,8,128]{3,2,1,0:T(8,128)(2,1)S(1)} async-done(((bf16[64,8,8,128]{3,2,1,0:T(8,128)(2,1)}), bf16[64,8,8,128]{3,2,1,0:T(8,128)(2,1)S(1)}, u32[]{:S(2)}, u32[]{:S(2)}) %all-to-all-start.3) | async-done | bytes 1048608 | tf_op jit(solution)/shard_map/all_to_all | solution.py:409
  193.5 3.8 %collective-permute-start.6 = (bf16[32,8,8,128]{3,2,1,0:T(8,128)(2,1)S(1)}, bf16[32,8,8,128]{3,2,1,0:T(8,128)(2,1)S(1)}, u32[]{:S(2)}, u32[]{:S(2)}) collective-permute-start(bf16[32,8,8,128]{3,2,1,0:T(8,128)(2,1)S(1)} %constant_dynamic-slice_fusion), channel_id=1, source_target_pairs={{0,1},{1,0},{2,3},{3,2},{4,5},{5,4},{6,7},{7,6},{8,9},{9,8},{10,11... | collective-permute-start | bytes 1572872 | tf_op jit(solution)/shard_map/ppermute | solution.py:419
  197.3 1.5 collective-permute-done.6.other
  198.8 0.0 copy-done
  198.8 0.0 copy-done.1
  198.8 1.0 copy-done.3
  199.8 1.2 finish.1
  (7 shorter events, 0.1 us)
Async XLA Ops:
  0.6 2.9 %copy-start.11 = (s32[1,16]{1,0:T(1,128)S(1)}, s32[1,16]{1,0:T(1,128)}, u32[]{:S(2)}) copy-start(s32[1,16]{1,0:T(1,128)} %param.9) | copy-start | bytes 196
  2.0 3.0 %collective-permute-start = (bf16[256,1024]{1,0:T(8,128)(2,1)S(1)}, bf16[256,1024]{1,0:T(8,128)(2,1)S(1)}, u32[]{:S(2)}, u32[]{:S(2)}) collective-permute-start(bf16[256,1024]{1,0:T(8,128)(2,1)S(1)} %pad_maximum_fusion.1), channel_id=1, source_target_pairs={{0,1},{1,0},{2,3},{3,2},{4,5},{5,4},{6,7},{7,6},{8,9},{9,8},{10,11... | collective-permute-start | bytes 1572872 | tf_op jit(solution)/shard_map/ppermute | solution.py:419
  5.5 30.6 %copy-start.4 = (bf16[512,1024]{1,0:T(8,128)(2,1)}, bf16[512,1024]{1,0:T(8,128)(2,1)S(1)}, u32[]{:S(2)}) copy-start(bf16[512,1024]{1,0:T(8,128)(2,1)S(1)} %maximum_select_fusion.2.keys.values) | copy-start | bytes 3145732
  38.8 5.7 %copy-start.9 = (bf16[256,4096]{1,0:T(8,128)(2,1)S(1)}, bf16[256,4096]{1,0:T(8,128)(2,1)}, u32[]{:S(2)}) copy-start(bf16[256,4096]{1,0:T(8,128)(2,1)} %my_q) | copy-start | bytes 6291460
  38.8 33.4 %all-to-all-start.1 = ((bf16[64,4,2,16,128]{4,3,2,1,0:T(8,128)(2,1)}), bf16[64,4,2,16,128]{4,3,2,1,0:T(8,128)(2,1)}, u32[]{:S(2)}, u32[]{:S(2)}) async-start(bf16[64,4,2,16,128]{4,3,2,1,0:T(8,128)(2,1)} %pick.1), calls=%async_computation.1 | async-start | bytes 4194304 | tf_op jit(solution)/shard_map/all_to_all | solution.py:409
  44.5 1.6 copy-start.10
  46.2 4.2 %collective-permute-start.2 = (bf16[256,2048]{1,0:T(8,128)(2,1)S(1)}, bf16[256,2048]{1,0:T(8,128)(2,1)S(1)}, u32[]{:S(2)}, u32[]{:S(2)}) collective-permute-start(bf16[256,2048]{1,0:T(8,128)(2,1)S(1)} %constant_dynamic-slice_fusion.1), channel_id=1, source_target_pairs={{0,1},{1,0},{2,3},{3,2},{4,5},{5,4},{6,7},{7,6},{8,9},{9,8},{10,11... | collective-permute-start | bytes 3145736 | tf_op jit(solution)/shard_map/ppermute | solution.py:419
  48.1 3.8 %collective-permute-start.1 = (bf16[256,2048]{1,0:T(8,128)(2,1)S(1)}, bf16[256,2048]{1,0:T(8,128)(2,1)S(1)}, u32[]{:S(2)}, u32[]{:S(2)}) collective-permute-start(bf16[256,2048]{1,0:T(8,128)(2,1)S(1)} %constant_dynamic-slice_fusion.2), channel_id=1, source_target_pairs={{0,1},{1,0},{2,3},{3,2},{4,5},{5,4},{6,7},{7,6},{8,9},{9,8},{10,11... | collective-permute-start | bytes 3145736 | tf_op jit(solution)/shard_map/ppermute | solution.py:419
  50.4 2.5 %copy-start.12 = (bf16[256,2048]{1,0:T(8,128)(2,1)}, bf16[256,2048]{1,0:T(8,128)(2,1)S(1)}, u32[]{:S(2)}) copy-start(bf16[256,2048]{1,0:T(8,128)(2,1)S(1)} %collective-permute-done.2.got_cot) | copy-start | bytes 3145732
  51.9 1.0 copy-start.13
  103.3 64.7 %all-to-all-start.2 = ((bf16[64,4,2,16,128]{4,3,2,1,0:T(8,128)(2,1)}), bf16[64,4,2,16,128]{4,3,2,1,0:T(8,128)(2,1)S(1)}, u32[]{:S(2)}, u32[]{:S(2)}) async-start(bf16[64,4,2,16,128]{4,3,2,1,0:T(8,128)(2,1)} %get-tuple-element.50), calls=%async_computation.2 | async-start | bytes 4194304 | tf_op jit(solution)/shard_map/all_to_all | solution.py:409
  155.7 7.3 %collective-permute-start.3 = (bf16[256,2048]{1,0:T(8,128)(2,1)}, bf16[256,2048]{1,0:T(8,128)(2,1)S(1)}, u32[]{:S(2)}, u32[]{:S(2)}) collective-permute-start(bf16[256,2048]{1,0:T(8,128)(2,1)} %get-tuple-element.58), channel_id=1, source_target_pairs={{0,1},{1,0},{2,3},{3,2},{4,5},{5,4},{6,7},{7,6},{8,9},{9,8},{10,11... | collective-permute-start | bytes 3145736 | tf_op jit(solution)/shard_map/ppermute | solution.py:419
  157.6 6.3 %collective-permute-start.4 = (bf16[256,2048]{1,0:T(8,128)(2,1)}, bf16[256,2048]{1,0:T(8,128)(2,1)}, u32[]{:S(2)}, u32[]{:S(2)}) collective-permute-start(bf16[256,2048]{1,0:T(8,128)(2,1)} %get-tuple-element.59), channel_id=1, source_target_pairs={{0,1},{1,0},{2,3},{3,2},{4,5},{5,4},{6,7},{7,6},{8,9},{9,8},{10,11... | collective-permute-start | bytes 3145736 | tf_op jit(solution)/shard_map/ppermute | solution.py:419
  157.7 4.5 %collective-permute-start.5 = (bf16[2,256,512]{2,1,0:T(8,128)(2,1)}, bf16[2,256,512]{2,1,0:T(8,128)(2,1)S(1)}, u32[]{:S(2)}, u32[]{:S(2)}) collective-permute-start(bf16[2,256,512]{2,1,0:T(8,128)(2,1)} %get-tuple-element.60), channel_id=1, source_target_pairs={{0,1},{1,0},{2,3},{3,2},{4,5},{5,4},{6,7},{7,6},{8,9},{9,8},{10,11... | collective-permute-start | bytes 1572872 | tf_op jit(solution)/shard_map/ppermute | solution.py:419
  162.2 0.8 copy-start.2
  163.0 1.0 copy-start.7
  168.0 9.3 %copy-start.6 = (bf16[256,2048]{1,0:T(8,128)(2,1)S(1)}, bf16[256,2048]{1,0:T(8,128)(2,1)}, u32[]{:S(2)}) copy-start(bf16[256,2048]{1,0:T(8,128)(2,1)} %get-tuple-element.62) | copy-start | bytes 3145732
  170.7 6.6 %copy-start.8 = (bf16[256,2048]{1,0:T(8,128)(2,1)S(1)}, bf16[256,2048]{1,0:T(8,128)(2,1)}, u32[]{:S(2)}) copy-start(bf16[256,2048]{1,0:T(8,128)(2,1)} %copy-done.7) | copy-start | bytes 3145732
  170.7 22.7 %all-to-all-start.3 = ((bf16[64,8,8,128]{3,2,1,0:T(8,128)(2,1)}), bf16[64,8,8,128]{3,2,1,0:T(8,128)(2,1)S(1)}, u32[]{:S(2)}, u32[]{:S(2)}) async-start(bf16[64,8,8,128]{3,2,1,0:T(8,128)(2,1)} %add_terms.1), calls=%async_computation.3 | async-start | bytes 2097152 | tf_op jit(solution)/shard_map/all_to_all | solution.py:409
  177.3 2.1 %copy-start.5 = (bf16[256,2048]{1,0:T(8,128)(2,1)S(1)}, bf16[256,2048]{1,0:T(8,128)(2,1)}, u32[]{:S(2)}) copy-start(bf16[256,2048]{1,0:T(8,128)(2,1)} %get-tuple-element.64) | copy-start | bytes 3145732
  179.4 19.4 %copy-start = (f32[512,512]{1,0:T(8,128)S(1)}, f32[512,512]{1,0:T(8,128)}, u32[]{:S(2)}) copy-start(f32[512,512]{1,0:T(8,128)} %get-tuple-element.69.near_k) | copy-start | bytes 3145732
  179.4 19.4 %copy-start.1 = (f32[512,512]{1,0:T(8,128)S(1)}, f32[512,512]{1,0:T(8,128)}, u32[]{:S(2)}) copy-start(f32[512,512]{1,0:T(8,128)} %get-tuple-element.70.near_v) | copy-start | bytes 3145732
  193.5 5.3 %collective-permute-start.6 = (bf16[32,8,8,128]{3,2,1,0:T(8,128)(2,1)S(1)}, bf16[32,8,8,128]{3,2,1,0:T(8,128)(2,1)S(1)}, u32[]{:S(2)}, u32[]{:S(2)}) collective-permute-start(bf16[32,8,8,128]{3,2,1,0:T(8,128)(2,1)S(1)} %constant_dynamic-slice_fusion), channel_id=1, source_target_pairs={{0,1},{1,0},{2,3},{3,2},{4,5},{5,4},{6,7},{7,6},{8,9},{9,8},{10,11... | collective-permute-start | bytes 1572872 | tf_op jit(solution)/shard_map/ppermute | solution.py:419
  198.8 1.0 copy-start.3
